TPU v7x, 32 devices: a whole 2x2x4 slice. The times are simulated.
32 devices in a mesh: ctx: 16 (over z, y, x), head: 2 (over core).
Axes of the slice: x: 2, y: 2, z: 4, core: 2. Of those that a mesh axis runs over, the one named last changes fastest.
Arguments:
- tokens: bfloat16 [4096, 2048], P('ctx'), may hold values from -6 to 6
- queries: float32 [4096, 256], P('ctx', 'head'), may hold values from -6 to 6
- values: float32 [4096, 256], P('ctx', 'head'), may hold values from -6 to 6
- dout: float32 [4096, 256], P('ctx', 'head'), may hold values from -6 to 6
- key_weight: bfloat16 [2048, 4, 256], P('ctx', None, 'head'), may hold values from -0.125 to 0.125
- routing: int32 [4096, 2], P('ctx'), may hold values from 0 to 3, all different within a row
- gates: float32 [4096, 2], P('ctx'), may hold values from 0.25 to 1
Outputs:
- key_grad: float32 [2048, 4, 256], P('ctx', None, 'head')
- query_grad: float32 [4096, 256], P('ctx', 'head')
- value_grad: float32 [4096, 256], P('ctx', 'head')
- gate_grad: float32 [4096, 2], P('ctx')
Inputs may be any that keep to these rules, and one draw needn't show every extreme that they name: `routing`: each row names 2 different memories.
All inputs are finite; a program needn't handle non-finite values.
Results may differ from a plain program's by a relative error of at most 0.0029.
Values may be sent and summed in bfloat16 or wider, within the bound.
No kernel may reach another device: no remote copies, remote signals or barrier semaphores. Data moves between devices by JAX's collectives and lax.ppermute only.
A program may use at most 128 MiB of HBM per device.

v0:
```python
import math

import jax
import jax.numpy as jnp
from jax import lax
from jax.sharding import PartitionSpec as P


def prefix(x, axis, combine, identity, reverse):
    count, here = (lax.axis_size(axis), lax.axis_index(axis))
    everything = lax.all_gather(x, axis)
    start = jnp.broadcast_to(jnp.asarray(identity, x.dtype), x.shape)

    def step(k, before):
        at = count - 1 - k if reverse else k
        reached = at > here if reverse else at < here
        new = combine(before, everything[at])
        return jnp.where(reached, new, before)

    return lax.fori_loop(0, count, step, start)


def routing_tables(routing, gates, memories):
    onehot = (routing[:, :, None] == jnp.arange(memories, dtype=jnp.int32)[None, None, :]).astype(
        jnp.float32
    )
    routed = jnp.sum(onehot, axis=1)
    weighted = jnp.sum(gates[:, :, None] * onehot, axis=1)
    return (routed, weighted, onehot)


def block_states(queries, values, dout, keys, routed, weighted, scale):
    highest = lax.Precision.HIGHEST
    masked_keys = keys * routed[:, :, None]
    key_local = jnp.einsum("tmk,tv->mkv", masked_keys, values, precision=highest)
    lifted = weighted[:, :, None] * queries[:, None, :]
    grad_local = scale * jnp.einsum("tmk,tv->mkv", lifted, dout, precision=highest)
    return (key_local, grad_local)


def block_grads(queries, values, dout, keys, routed, weighted, key_in, grad_in, scale):
    highest = lax.Precision.HIGHEST
    count = queries.shape[0]
    memories = keys.shape[1]
    head_dim = keys.shape[2]
    places = jnp.arange(count, dtype=jnp.int32)
    causal = (places[:, None] >= places[None, :]).astype(jnp.float32)
    masked_keys = keys * routed[:, :, None]
    scores = jnp.dot(dout, values.T, precision=highest) * causal
    carried_q = jnp.einsum("tv,mkv->tmk", dout, key_in, precision=highest)
    inner_q = jnp.dot(
        scores, masked_keys.reshape(count, memories * head_dim), precision=highest
    ).reshape(count, memories, head_dim)
    state_dout = carried_q + inner_q
    query_grad = scale * jnp.einsum("tm,tmk->tk", weighted, state_dout, precision=highest)
    gate_part = scale * jnp.einsum("tk,tmk->tm", queries, state_dout, precision=highest)
    lifted = (weighted[:, :, None] * queries[:, None, :]).reshape(count, memories * head_dim)
    carried_k = jnp.einsum("tv,mkv->tmk", values, grad_in, precision=highest)
    inner_k = scale * jnp.dot(scores.T, lifted, precision=highest).reshape(
        count, memories, head_dim
    )
    key_part = routed[:, :, None] * (carried_k + inner_k)
    carried_v = jnp.einsum("tmk,mkv->tv", masked_keys, grad_in, precision=highest)
    products = jnp.einsum("sk,tmk->mst", queries, masked_keys, precision=highest)
    mixed = jnp.einsum("mst,sm->st", products, weighted, precision=highest) * causal
    value_grad = carried_v + scale * jnp.dot(mixed.T, dout, precision=highest)
    return (query_grad, key_part, value_grad, gate_part)


def add_pair(earlier, later):
    return jax.tree.map(lambda first, second: first + second, earlier, later)


def on_device(tokens, queries, values, dout, key_weight, routing, gates):
    count = tokens.shape[0]
    width = tokens.shape[1]
    memories = key_weight.shape[1]
    head_dim = key_weight.shape[2]
    parts = lax.axis_size("ctx")
    scale = 1.0 / math.sqrt(head_dim * count * parts)
    piece = lax.all_gather(key_weight, "ctx", axis=0, tiled=True)
    columns = tokens
    keys_flat = jnp.dot(
        columns,
        piece.reshape(piece.shape[0], memories * head_dim),
        preferred_element_type=jnp.float32,
    )
    keys = keys_flat.reshape(count, memories, head_dim)
    routed, weighted, onehot = routing_tables(routing, gates, memories)
    key_local, grad_local = block_states(queries, values, dout, keys, routed, weighted, scale)
    zeros_state = jnp.zeros_like(key_local)
    key_in = prefix(key_local, "ctx", add_pair, zeros_state, False)
    grad_in = prefix(grad_local, "ctx", add_pair, zeros_state, True)
    query_grad, key_part, value_grad, gate_part = block_grads(
        queries, values, dout, keys, routed, weighted, key_in, grad_in, scale
    )
    gate_sum = lax.psum(gate_part, "head")
    gate_grad = jnp.einsum("tjm,tm->tj", onehot, gate_sum, precision=lax.Precision.HIGHEST)
    key_low = key_part.reshape(count, memories * head_dim).astype(jnp.bfloat16)
    columns = tokens
    product = lax.dot_general(
        columns, key_low, (((0,), (0,)), ((), ())), preferred_element_type=jnp.float32
    )
    key_grad = lax.psum_scatter(
        product.reshape(width // parts * lax.axis_size("ctx"), memories, head_dim),
        "ctx",
        scatter_dimension=0,
        tiled=True,
    )
    return (key_grad, query_grad, value_grad, gate_grad)


def solution(mesh):
    return jax.shard_map(
        on_device,
        mesh=mesh,
        in_specs=(
            P("ctx", None),
            P("ctx", "head"),
            P("ctx", "head"),
            P("ctx", "head"),
            P("ctx", None, "head"),
            P("ctx", None),
            P("ctx", None),
        ),
        out_specs=(P("ctx", None, "head"), P("ctx", "head"), P("ctx", "head"), P("ctx", None)),
        check_vma=False,
    )
```

profile of v0, /device:TPU:0, one launch (start us, length us, event | category | flops | bytes accessed | tf_op | source)
XLA Modules:
  0.0 410.3 jit_solution(14847489965872079192)
XLA Ops:
  9.7 2.2 convolution_multiply_fusion.1
  12.0 62.3 %all-gather.6.cloned.1.call-done = bf16[2048,4,128]{2,1,0:T(4,128)(2,1)} async-done(((bf16[128,4,128]{2,1,0:T(4,128)(2,1)}), bf16[2048,4,128]{2,1,0:T(4,128)(2,1)}) %all-gather.6.cloned.1.call-update) | async-done | bytes 2097168 | tf_op jit(solution)/shard_map/all_gather | solution.py:81
  74.2 4.4 %copy.54 = bf16[2048,4,128]{0,2,1:T(8,128)(2,1)} copy(bf16[2048,4,128]{2,1,0:T(4,128)(2,1)} %all-gather.6.cloned.1.call-done) | data formatting | bytes 4194304 | tf_op jit(solution)/shard_map/reshape | solution.py:85
  78.6 2.4 fusion.4
  81.0 1.3 fusion.23
  87.2 65.2 %all-gather.8.cloned.1.call-done = f32[64,128,128]{2,1,0:T(8,128)} async-done(((f32[4,128,128]{2,1,0:T(8,128)}), f32[64,128,128]{2,1,0:T(8,128)}) %all-gather.8.cloned.1.call-update) | async-done | bytes 4194320 | tf_op jit(solution)/shard_map/all_gather | solution.py:11
  152.3 17.1 %while.30 = (s32[]{:T(128)}, f32[4,128,128]{2,1,0:T(8,128)S(1)}, s32[]{:T(128)}, f32[16,4,128,128]{3,2,1,0:T(8,128)}, s32[]{:T(128)}, /*index=5*/s32[]{:T(128)}, s32[]{:T(128)}, s32[]{:T(128)}) while((s32[]{:T(128)}, f32[4,128,128]{2,1,0:T(8,128)S(1)}, s32[]{:T(128)}, f32[16,4,128,128]{3,2,1,0:T(8,128)}, s32[]{:T(128)}, ...), condition=%wide.region_3.4_spmd.clone, body=%wide.region_2.3_spmd.clone.sunk | while | flops 196616 | bytes 786587 | solution.py:20
  160.9 1.1 add_select_fusion.4
  162.0 1.0 add_select_fusion.4
  167.3 1.0 add_select_fusion.4
  169.5 1.5 fusion.10
  171.0 2.7 fusion.31
  173.6 5.3 %copy.26 = f32[2048,4,128]{2,1,0:T(4,128)} copy(f32[2048,4,128]{0,2,1:T(8,128)} %bitcast.103) | data formatting | bytes 8388608 | tf_op jit(solution)/shard_map/reshape | solution.py:105
  179.9 1.2 fusion.12
  181.1 48.7 %all-gather.10.cloned.1.call-done = f32[64,128,128]{2,1,0:T(8,128)} async-done(((f32[4,128,128]{2,1,0:T(8,128)}), f32[64,128,128]{2,1,0:T(8,128)}) %all-gather.10.cloned.1.call-update) | async-done | bytes 4194320 | tf_op jit(solution)/shard_map/all_gather | solution.py:11
  229.8 17.1 %while.31 = (s32[]{:T(128)}, f32[4,128,128]{2,1,0:T(8,128)S(1)}, s32[]{:T(128)}, f32[16,4,128,128]{3,2,1,0:T(8,128)}, s32[]{:T(128)}, /*index=5*/s32[]{:T(128)}) while((s32[]{:T(128)}, f32[4,128,128]{2,1,0:T(8,128)S(1)}, s32[]{:T(128)}, f32[16,4,128,128]{3,2,1,0:T(8,128)}, s32[]{:T(128)}, /*index=5*/s32[]{:T(128)}) %tuple.87), condition=%wide.region_6.7_spmd.clone, body=%wide.region_5.6_spmd.clone.sunk | while | flops 196612 | bytes 786525 | solution.py:20
  229.8 1.0 add_select_fusion.5
  238.4 1.1 add_select_fusion.5
  239.4 1.1 add_select_fusion.5
  240.5 1.0 add_select_fusion.5
  247.7 1.8 fusion.32
  249.5 3.7 psum.7
  254.7 147.4 %all-reduce.3.cloned.1.call-done = f32[2048,4,128]{2,1,0:T(4,128)} async-done(((f32[2048,4,128]{2,1,0:T(4,128)}), f32[2048,4,128]{2,1,0:T(4,128)}) %all-reduce.3.cloned.1.call-update) | async-done | bytes 4194320
  402.1 1.7 constant_dynamic-slice_fusion
  (67 shorter events, 36.0 us)
Async XLA Ops:
  7.2 71.4 %copy-start = (bf16[256,2048]{1,0:T(8,128)(2,1)S(1)}, bf16[256,2048]{1,0:T(8,128)(2,1)}, u32[]{:S(2)}) copy-start(bf16[256,2048]{1,0:T(8,128)(2,1)} %param.11) | copy-start | bytes 3145732
  7.2 67.0 %all-gather.6.cloned.1.call-start = ((), (), s32[]{:S(2)}) async-start(), calls=%async_computation | async-start | bytes 2228224 | tf_op jit(solution)/shard_map/all_gather | solution.py:81
  7.9 144.4 %all-gather.8.cloned.1.call-start = ((), (), s32[]{:S(2)}) async-start(), calls=%async_computation.1 | async-start | bytes 4456448 | tf_op jit(solution)/shard_map/all_gather | solution.py:11
  11.9 69.1 %copy-start.2 = (f32[256,128]{1,0:T(8,128)S(1)}, f32[256,128]{1,0:T(8,128)}, u32[]{:S(2)}) copy-start(f32[256,128]{1,0:T(8,128)} %param.13) | copy-start | bytes 393220
  11.9 217.9 %all-gather.10.cloned.1.call-start = ((), (), s32[]{:S(2)}) async-start(), calls=%async_computation.2 | async-start | bytes 4456448 | tf_op jit(solution)/shard_map/all_gather | solution.py:11
  78.6 3.8 copy-start.7
  78.6 5.1 %copy-start.1 = (f32[256,128]{1,0:T(8,128)S(1)}, f32[256,128]{1,0:T(8,128)}, u32[]{:S(2)}) copy-start(f32[256,128]{1,0:T(8,128)} %param.14) | copy-start | bytes 393220
  78.6 6.1 %copy-start.4 = (f32[256,128]{1,0:T(8,128)S(1)}, f32[256,128]{1,0:T(8,128)}, u32[]{:S(2)}) copy-start(f32[256,128]{1,0:T(8,128)} %param.12) | copy-start | bytes 393220
  82.3 319.8 %all-reduce.3.cloned.1.call-start = ((), (), s32[]{:S(2)}) async-start(), calls=%async_computation.3 | async-start | bytes 8388608
  173.6 6.3 %copy-start.3 = (f32[256,256]{1,0:T(8,128)S(1)}, f32[256,256]{1,0:T(8,128)}, u32[]{:S(2)}) copy-start(f32[256,256]{1,0:T(8,128)} %copy.44) | copy-start | bytes 786436
  181.1 66.6 %copy-start.5 = (f32[256,128]{1,0:T(8,128)S(1)}, f32[256,128]{1,0:T(8,128)}, u32[]{:S(2)}) copy-start(f32[256,128]{1,0:T(8,128)} %param.12) | copy-start | bytes 393220
  229.8 23.6 %copy-start.6 = (s32[256,2]{0,1:T(2,128)S(1)}, s32[256,2]{0,1:T(2,128)}, u32[]{:S(2)}) copy-start(s32[256,2]{0,1:T(2,128)} %param.16) | copy-start | bytes 6148
Sparse Core Ops, SparseCore 0:
  10.8 63.3 all-gather.5
  77.6 74.7 all-gather.7
  155.1 74.6 all-gather.9
  235.3 166.7 all-reduce.2
where the time goes:
time: 412 us; the launch traced here: 410 us
  waiting for transfers between devices  324 us (79%)
  other arithmetic  35.4 us (9%)
  matrix products  17.1 us (4%)
  between operations  14.7 us (4%)
  local copies, waits for them, and re-layouts  14.2 us (3%)
    unnamed x5, waiting for transfers between devices  148 us
    all_gather x2, waiting for transfers between devices, prefix(): everything = lax.all_gather(x, axis)  114 us
    all_gather x1, waiting for transfers between devices, on_device(): piece = lax.all_gather(key_weight, 'ctx', axis=0, tiled=True)  62.3 us
    select_n x32, other arithmetic, step(): return jnp.where(reached, new, before)  33.4 us
  transfers between devices with their start and end apart: 4, of which 4 were waited for; matrix products, arithmetic and copies ran while one was open for 16% of the time, Pallas kernels for 0%

commit v1 on v0

v1 whole, which is shorter than its diff:
```python
import functools
import math

import jax
import jax.numpy as jnp
from jax import lax
from jax.experimental import pallas as pl
from jax.experimental.pallas import tpu as pltpu
from jax.sharding import PartitionSpec as P

F32 = jnp.float32
BF16 = jnp.bfloat16


def split(x):
    high = x.astype(BF16)
    return high, (x - high.astype(F32)).astype(BF16)


def dot3(a, b, b_last=False):
    dims = (((1,), (1 if b_last else 0,)), ((), ()))

    def one(x, y):
        return lax.dot_general(x, y, dims, preferred_element_type=F32)

    return one(a[0], b[0]) + (one(a[0], b[1]) + one(a[1], b[0]))


def routed_columns(routing, memories):
    columns = []
    for m in range(memories):
        hit = (routing == m).astype(F32)
        columns.append(jnp.sum(hit, axis=1, keepdims=True))
    return columns


def weighted_columns(routing, gates, memories):
    return [
        jnp.sum(jnp.where(routing == m, gates, 0.0), axis=1, keepdims=True) for m in range(memories)
    ]


def lift(queries, routing, gates, memories):
    return jnp.concatenate(
        [w * queries for w in weighted_columns(routing, gates, memories)], axis=1
    )


def mask(x, routing, memories):
    width = x.shape[1] // memories
    return jnp.concatenate(
        [r * x[:, m * width : (m + 1) * width] for m, r in enumerate(routed_columns(routing, memories))],
        axis=1,
    )


def call(body, outs, *args, scratch=(), spaces=None, flops=0):
    vmem = pl.BlockSpec(memory_space=pltpu.VMEM)
    size = sum(a.size * a.dtype.itemsize for a in args)
    return pl.pallas_call(
        body,
        out_shape=outs,
        in_specs=[vmem] * len(args) if spaces is None else spaces,
        out_specs=jax.tree.map(lambda _: vmem, outs),
        scratch_shapes=list(scratch),
        cost_estimate=pl.CostEstimate(flops=flops, bytes_accessed=size, transcendentals=0),
        compiler_params=pltpu.CompilerParams(vmem_limit_bytes=40 * 1024 * 1024),
    )(*args)


def grad_states(memories, scale, q_ref, dout_ref, routing_ref, gates_ref, a_ref, b_ref):
    lifted = lift(q_ref[...], routing_ref[...], gates_ref[...], memories)
    states = scale * dot3(split(dout_ref[...].T), split(lifted))
    half = a_ref.shape[1]
    a_ref[...] = states[:, :half]
    b_ref[...] = states[:, half:]


def inner_key(memories, scale, q_ref, v_ref, dout_ref, routing_ref, gates_ref, out_ref):
    count = q_ref.shape[0]
    routing = routing_ref[...]
    lifted = lift(q_ref[...], routing, gates_ref[...], memories)
    places = lax.broadcasted_iota(jnp.int32, (count, count), 0)
    later = lax.broadcasted_iota(jnp.int32, (count, count), 1)
    scores = dot3(split(v_ref[...]), split(dout_ref[...]), True)
    scores = jnp.where(later >= places, scores, 0.0)
    out_ref[...] = scale * dot3(split(scores), split(lifted))


def turned_tokens(parts, here_ref, tokens_ref, out_ref, turned):
    width = tokens_ref.shape[1]
    step = 256
    for at in range(0, width, step):
        turned[at : at + step, :] = tokens_ref[:, at : at + step].T
    rows = width // parts
    here = here_ref[0]
    for off in range(parts):
        start = pl.multiple_of((here ^ off) * rows, rows)
        out_ref[off * rows : (off + 1) * rows, :] = turned[pl.ds(start, rows), :]


def key_states(memories, layout, parts, here_ref, *refs):
    chunks = len(layout)
    chunk_refs = refs[:chunks]
    tokens_ref, v_ref, routing_ref, keys_ref, a_ref, b_ref, weights, sem = refs[chunks:]
    rows = weights.shape[0] // parts
    here = here_ref[0]
    copies = []
    for ref, (column, source, blocks) in zip(chunk_refs, layout, strict=True):
        half = a_ref.shape[1]
        for k, off in enumerate(blocks):
            start = pl.multiple_of((here ^ off) * rows, rows)
            copy = pltpu.make_async_copy(
                ref.at[pl.ds(k * rows, rows), pl.ds(source * half, half)],
                weights.at[pl.ds(start, rows), pl.ds(column * half, half)],
                sem.at[len(copies)],
            )
            copy.start()
            copies.append(copy)
    for copy in copies:
        copy.wait()
    keys = jnp.dot(tokens_ref[...], weights[...], preferred_element_type=F32)
    keys = mask(keys, routing_ref[...], memories)
    keys_ref[...] = keys
    states = dot3(split(v_ref[...].T), split(keys))
    half = a_ref.shape[1]
    a_ref[...] = states[:, :half]
    b_ref[...] = states[:, half:]


def inner_rest(memories, scale, q_ref, v_ref, dout_ref, routing_ref, gates_ref, keys_ref, value_ref, state_ref):
    count = q_ref.shape[0]
    places = lax.broadcasted_iota(jnp.int32, (count, count), 0)
    others = lax.broadcasted_iota(jnp.int32, (count, count), 1)
    keys = split(keys_ref[...])
    dout = split(dout_ref[...])
    lifted = lift(q_ref[...], routing_ref[...], gates_ref[...], memories)
    mixed = jnp.where(others >= places, dot3(keys, split(lifted), True), 0.0)
    value_ref[...] = scale * dot3(split(mixed), dout)
    scores = jnp.where(places >= others, dot3(dout, split(v_ref[...]), True), 0.0)
    state_ref[...] = dot3(split(scores), keys)


def key_grad_low(memories, v_ref, routing_ref, inner_ref, grad_a, grad_b):
    values = split(v_ref[...])
    carried = jnp.concatenate([dot3(values, split(grad_a)), dot3(values, split(grad_b))], axis=1)
    return mask(carried + inner_ref[...], routing_ref[...], memories).astype(BF16)


def blocks_of(order, chosen, parts):
    found = []
    for place in range(parts):
        off = 0
        for k, bit in enumerate(order):
            if place >> (len(order) - 1 - k) & 1:
                off |= 1 << bit
        if (off >> order[0]) & 1 == chosen:
            found.append(off)
    return found


def products(turned_ref, low, parts, orders, chosen, out_refs):
    rows = turned_ref.shape[0] // parts
    half = low.shape[1] // 2
    for h, (order, out_ref) in enumerate(zip(orders, out_refs, strict=True)):
        side = low[:, h * half : (h + 1) * half]
        for k, off in enumerate(blocks_of(order, chosen, parts)):
            block = turned_ref[off * rows : (off + 1) * rows, :]
            out_ref[k * rows : (k + 1) * rows, :] = jnp.dot(
                block, side, preferred_element_type=F32
            ).astype(out_ref.dtype)


def key_sent(memories, parts, orders, v_ref, routing_ref, inner_ref, ga_ref, gb_ref, turned_ref, low_ref, a_ref, b_ref):
    low = key_grad_low(memories, v_ref, routing_ref, inner_ref, ga_ref[...], gb_ref[...])
    low_ref[...] = low
    products(turned_ref, low, parts, orders, 1, (a_ref, b_ref))


def key_kept(parts, orders, low_ref, turned_ref, a_ref, b_ref):
    products(turned_ref, low_ref[...], parts, orders, 0, (a_ref, b_ref))


def value_out(inner_ref, keys_ref, ga_ref, gb_ref, out_ref):
    half = ga_ref.shape[1]
    keys = split(keys_ref[...])
    first = dot3((keys[0][:, :half], keys[1][:, :half]), split(ga_ref[...]), True)
    second = dot3((keys[0][:, half:], keys[1][:, half:]), split(gb_ref[...]), True)
    out_ref[...] = inner_ref[...] + (first + second)


def query_out(memories, scale, q_ref, dout_ref, routing_ref, gates_ref, state_ref, sa_ref, sb_ref, query_ref, gate_ref):
    dout = split(dout_ref[...])
    state = state_ref[...] + jnp.concatenate(
        [dot3(dout, split(sa_ref[...])), dot3(dout, split(sb_ref[...]))], axis=1
    )
    queries = q_ref[...]
    routing = routing_ref[...]
    width = queries.shape[1]
    query = jnp.zeros_like(queries)
    gate = jnp.zeros(gate_ref.shape, F32)
    for m, w in enumerate(weighted_columns(routing, gates_ref[...], memories)):
        part = state[:, m * width : (m + 1) * width]
        query = query + w * part
        mine = jnp.sum(queries * part, axis=1, keepdims=True)
        gate = gate + jnp.where(routing == m, mine, 0.0)
    query_ref[...] = scale * query
    gate_ref[...] = scale * gate


def swap(x, bit, parts):
    return lax.ppermute(x, "ctx", [(i, i ^ (1 << bit)) for i in range(parts)])


def one_way(x, bit, parts, reverse):
    sources = [i for i in range(parts) if (i >> bit & 1) == (1 if reverse else 0)]
    return lax.ppermute(x, "ctx", [(i, i ^ (1 << bit)) for i in sources])


def prefix(state, bits, parts, here, reverse, wire):
    total = state
    before = jnp.zeros_like(state)
    for bit in bits:
        if bit == bits[-1]:
            return before + one_way(total.astype(wire), bit, parts, reverse).astype(F32)
        got = swap(total.astype(wire), bit, parts).astype(F32)
        after = (here >> bit & 1) == (0 if reverse else 1)
        before = before + jnp.where(after, got, 0.0)
        total = total + got
    return before


def prefix_x_last(state, bits, parts, here, reverse, wire):
    low, second, high = bits[0], bits[1], bits[2:]
    own = state
    got = swap(own.astype(wire), second, parts).astype(F32)
    after = (here >> second & 1) == (0 if reverse else 1)
    before = prefix(own + got, high, parts, here, reverse, wire) + jnp.where(after, got, 0.0)
    first = (here >> low & 1) == (1 if reverse else 0)
    sent = before + jnp.where(first, own, 0.0)
    return before + swap(sent.astype(wire), low, parts).astype(F32)


def reduce_scatter(kept, got, order, parts):
    for bit in order[1:]:
        rows = kept.shape[0] // 2
        sent = (kept[rows:] + got[rows:].astype(F32)).astype(BF16)
        kept = kept[:rows] + got[:rows].astype(F32)
        got = swap(sent, bit, parts)
    return kept + got.astype(F32)


def on_device(tokens, queries, values, dout, key_weight, routing, gates):
    count, width = tokens.shape
    rows, memories, head_dim = key_weight.shape
    parts = lax.axis_size("ctx")
    bits = list(range(parts.bit_length() - 1))
    here = lax.axis_index("ctx")
    at = here.astype(jnp.int32).reshape(1)
    scale = 1.0 / math.sqrt(head_dim * count * parts)
    full = memories * head_dim
    half = full // 2
    smem = pl.BlockSpec(memory_space=pltpu.SMEM)
    vmem = pl.BlockSpec(memory_space=pltpu.VMEM)
    anywhere = pl.BlockSpec(memory_space=pl.ANY)

    def shape(r, c, dtype=F32):
        return jax.ShapeDtypeStruct((r, c), dtype)

    gathered = key_weight.reshape(rows, full)
    blocks = [0]
    for bit in bits[2:]:
        gathered = jnp.concatenate([gathered, swap(gathered, bit, parts)], axis=0)
        blocks = blocks + [off | (1 << bit) for off in blocks]

    grad_a, grad_b = call(
        functools.partial(grad_states, memories, scale),
        (shape(head_dim, half), shape(head_dim, half)),
        queries, dout, routing, gates,
        flops=6 * count * head_dim * full,
    )
    grad_in_a = prefix(grad_a, bits, parts, here, True, F32)
    grad_in_b = prefix_x_last(grad_b, bits, parts, here, True, F32)

    chunks = [gathered, gathered]
    layout = [(0, 0, blocks), (1, 1, blocks)]
    for side in range(2):
        first, second = (bits[1], bits[0]) if side == 0 else (bits[0], bits[1])
        mine = gathered[:, side * half : (side + 1) * half]
        near = swap(mine, first, parts)
        far = swap(mine, second, parts)
        both = swap(near, second, parts)
        chunks += [near, far, both]
        one, two = 1 << first, 1 << second
        layout += [
            (side, 0, [off | one for off in blocks]),
            (side, 0, [off | two for off in blocks]),
            (side, 0, [off | one | two for off in blocks]),
        ]

    inner_k = call(
        functools.partial(inner_key, memories, scale),
        shape(count, full),
        queries, values, dout, routing, gates,
        flops=6 * count * count * (head_dim + full),
    )
    turned = call(
        functools.partial(turned_tokens, parts),
        shape(width, count, BF16),
        at, tokens,
        spaces=[smem, vmem],
        scratch=[pltpu.VMEM((width, count), BF16)],
        flops=2 * width * count,
    )

    orders = (bits, [bits[1], bits[0]] + bits[2:])
    low, sent_a, sent_b = call(
        functools.partial(key_sent, memories, parts, orders),
        (shape(count, full, BF16), shape(width // 2, half, BF16), shape(width // 2, half, BF16)),
        values, routing, inner_k, grad_in_a, grad_in_b, turned,
        flops=count * width * full + 6 * count * head_dim * full,
    )
    got_a = swap(sent_a, orders[0][0], parts)
    got_b = swap(sent_b, orders[1][0], parts)
    kept_a, kept_b = call(
        functools.partial(key_kept, parts, orders),
        (shape(width // 2, half), shape(width // 2, half)),
        low, turned,
        flops=count * width * full,
    )
    key_grad_a = reduce_scatter(kept_a, got_a, orders[0], parts)
    key_grad_b = reduce_scatter(kept_b, got_b, orders[1], parts)
    key_grad = jnp.concatenate([key_grad_a, key_grad_b], axis=1).reshape(rows, memories, head_dim)

    keys, state_a, state_b = call(
        functools.partial(key_states, memories, layout, parts),
        (shape(count, full), shape(head_dim, half), shape(head_dim, half)),
        at, *chunks, tokens, values, routing,
        spaces=[smem] + [anywhere] * len(chunks) + [vmem] * 3,
        scratch=[
            pltpu.VMEM((width, full), BF16),
            pltpu.SemaphoreType.DMA((sum(len(entry[2]) for entry in layout),)),
        ],
        flops=2 * count * width * full + 6 * count * head_dim * full,
    )
    state_in_a = prefix(state_a, bits, parts, here, False, BF16)
    state_in_b = prefix_x_last(state_b, bits, parts, here, False, BF16)
    inner_v, inner_state = call(
        functools.partial(inner_rest, memories, scale),
        (shape(count, head_dim), shape(count, full)),
        queries, values, dout, routing, gates, keys,
        flops=12 * count * count * (head_dim + full),
    )
    value_grad = call(
        value_out,
        shape(count, head_dim),
        inner_v, keys, grad_in_a, grad_in_b,
        flops=6 * count * head_dim * full,
    )
    query_grad, gate_part = call(
        functools.partial(query_out, memories, scale),
        (shape(count, head_dim), shape(count, routing.shape[1])),
        queries, dout, routing, gates, inner_state, state_in_a, state_in_b,
        flops=6 * count * head_dim * full,
    )
    gate_grad = lax.psum(gate_part, "head")
    return (key_grad, query_grad, value_grad, gate_grad)


def solution(mesh):
    return jax.shard_map(
        on_device,
        mesh=mesh,
        in_specs=(
            P("ctx", None),
            P("ctx", "head"),
            P("ctx", "head"),
            P("ctx", "head"),
            P("ctx", None, "head"),
            P("ctx", None),
            P("ctx", None),
        ),
        out_specs=(P("ctx", None, "head"), P("ctx", "head"), P("ctx", "head"), P("ctx", None)),
        check_vma=False,
    )
```

time: 412 us -> 106 us (0.26)
  waiting for transfers between devices: 324 us -> 36.1 us
  starting transfers between devices: 0.16 us -> 50.6 us
  other arithmetic: 35.4 us -> 2.55 us
  matrix products: 17.1 us -> 0 us
  between operations: 14.7 us -> 1.03 us
  local copies, waits for them, and re-layouts: 14.2 us -> 3.85 us
  Pallas kernels: 0 us -> 7.9 us
    all_gather x3 -> x0, waiting for transfers between devices: 176 us -> none  [the longest x2 114 us: prefix(): everything = lax.all_gather(x, axis)]
    unnamed x5 -> x0, waiting for transfers between devices: 148 us -> none
    ppermute x0 -> x32, starting transfers between devices: none -> 50.6 us  [the longest x28 39.8 us: swap(): return lax.ppermute(x, 'ctx', [(i, i ^ 1 << bit) for i in range(parts)])]
    ppermute x0 -> x32, waiting for transfers between devices: none -> 36.1 us  [the longest x28 33.2 us: swap(): return lax.ppermute(x, 'ctx', [(i, i ^ 1 << bit) for i in range(parts)])]
    select_n x32 -> x0, other arithmetic: 33.4 us -> none  [step(): return jnp.where(reached, new, before)]
    dot_general x13 -> x0, matrix products: 17.1 us -> none  [the longest x1 2.66 us: on_device(): lax.dot_general(columns, key_low, (((0,), (0,)), ((), ())), preferred_ele...]
    reshape x2 -> x1, local copies, waits for them, and re-layouts: 9.67 us -> 0.79 us  [on_device(): jnp.concatenate([key_grad_a, key_grad_b], axis=1)]
    pallas_call x0 -> x9, Pallas kernels: none -> 7.9 us  [call(): pl.pallas_call(body, out_shape=outs, in_specs=[vmem] * len(args) if space...]
  transfers between devices with their start and end apart: 4 -> 32, of which waited for: 4 -> 16; matrix products, arithmetic and copies ran while one was open for 16% -> 4% of each run, Pallas kernels for 0% -> 7%
where the time goes in v1:
time: 106 us
  starting transfers between devices  50.6 us (48%)
  waiting for transfers between devices  36.1 us (34%)
  Pallas kernels  7.9 us (7%)
  local copies, waits for them, and re-layouts  3.85 us (4%)
  blocking collectives  3.73 us (4%)
  other arithmetic  2.55 us (2%)
    ppermute x28, starting transfers between devices, swap(): return lax.ppermute(x, 'ctx', [(i, i ^ 1 << bit) for i in range(parts)])  39.8 us
    ppermute x28, waiting for transfers between devices, swap(): return lax.ppermute(x, 'ctx', [(i, i ^ 1 << bit) for i in range(parts)])  33.2 us
    ppermute x4, starting transfers between devices, one_way(): return lax.ppermute(x, 'ctx', [(i, i ^ 1 << bit) for i in sources])  10.7 us
    pallas_call x9, Pallas kernels, call(): pl.pallas_call(body, out_shape=outs, in_specs=[vmem] * len(args) if space...  7.9 us
    psum x1, blocking collectives, on_device(): gate_grad = lax.psum(gate_part, 'head')  3.73 us
    ppermute x4, waiting for transfers between devices, one_way(): return lax.ppermute(x, 'ctx', [(i, i ^ 1 << bit) for i in sources])  2.89 us
    unnamed x18, local copies, waits for them, and re-layouts  2.21 us
  transfers between devices with their start and end apart: 32, of which 16 were waited for; matrix products, arithmetic and copies ran while one was open for 4% of the time, Pallas kernels for 7%

profile of v1, /device:TPU:0, one launch (start us, length us, event | category | flops | bytes accessed | tf_op | source)
XLA Modules:
  0.0 105.7 jit_solution(11891215567987599184)
XLA Ops:
  2.2 3.0 %collective-permute-start = (f32[128,256]{1,0:T(8,128)S(1)}, f32[128,256]{1,0:T(8,128)S(1)}, u32[]{:S(2)}, u32[]{:S(2)}) collective-permute-start(f32[128,256]{1,0:T(8,128)S(1)} %get-tuple-element.18), channel_id=1, source_target_pairs={{0,2},{2,0},{4,6},{6,4},{8,10},{10,8},{12,14},{14,12},{16,18},{18,... | collective-permute-start | bytes 393224 | tf_op jit(solution)/shard_map/ppermute | solution.py:212
  5.2 1.5 %collective-permute-start.4 = (f32[128,256]{1,0:T(8,128)S(1)}, f32[128,256]{1,0:T(8,128)S(1)}, u32[]{:S(2)}, u32[]{:S(2)}) collective-permute-start(f32[128,256]{1,0:T(8,128)S(1)} %get-tuple-element.19), channel_id=1, source_target_pairs={{0,4},{2,6},{4,0},{6,2},{8,12},{10,14},{12,8},{14,10},{16,20},{18,... | collective-permute-start | bytes 393224 | tf_op jit(solution)/shard_map/ppermute | solution.py:212
  6.7 1.6 %collective-permute-start.16 = (bf16[128,512]{1,0:T(8,128)(2,1)S(1)}, bf16[128,512]{1,0:T(8,128)(2,1)S(1)}, u32[]{:S(2)}, u32[]{:S(2)}) collective-permute-start(bf16[128,512]{1,0:T(8,128)(2,1)S(1)} %bitcast.9), channel_id=1, source_target_pairs={{0,8},{2,10},{4,12},{6,14},{8,0},{10,2},{12,4},{14,6},{16,24},{18,... | collective-permute-start | bytes 393224 | tf_op jit(solution)/shard_map/ppermute | solution.py:212
  8.7 1.8 %collective-permute-start.1 = (f32[128,256]{1,0:T(8,128)S(1)}, f32[128,256]{1,0:T(8,128)S(1)}, u32[]{:S(2)}, u32[]{:S(2)}) collective-permute-start(f32[128,256]{1,0:T(8,128)S(1)} %add.116), channel_id=1, source_target_pairs={{0,4},{2,6},{4,0},{6,2},{8,12},{10,14},{12,8},{14,10},{16,20},{18,... | collective-permute-start | bytes 393224 | tf_op jit(solution)/shard_map/ppermute | solution.py:212
  10.6 1.6 %collective-permute-start.5 = (f32[128,256]{1,0:T(8,128)S(1)}, f32[128,256]{1,0:T(8,128)S(1)}, u32[]{:S(2)}, u32[]{:S(2)}) collective-permute-start(f32[128,256]{1,0:T(8,128)S(1)} %add.122), channel_id=1, source_target_pairs={{0,8},{2,10},{4,12},{6,14},{8,0},{10,2},{12,4},{14,6},{16,24},{18,... | collective-permute-start | bytes 393224 | tf_op jit(solution)/shard_map/ppermute | solution.py:212
  12.2 2.7 %collective-permute-start.17 = (bf16[256,512]{1,0:T(8,128)(2,1)S(1)}, bf16[256,512]{1,0:T(8,128)(2,1)S(1)}, u32[]{:S(2)}, u32[]{:S(2)}) collective-permute-start(bf16[256,512]{1,0:T(8,128)(2,1)S(1)} %pad_maximum_fusion.1), channel_id=1, source_target_pairs={{0,16},{2,18},{4,20},{6,22},{8,24},{10,26},{12,28},{14,30},{16,0},... | collective-permute-start | bytes 786440 | tf_op jit(solution)/shard_map/ppermute | solution.py:212
  16.2 3.1 %collective-permute-done.5 = f32[128,256]{1,0:T(8,128)S(1)} collective-permute-done((f32[128,256]{1,0:T(8,128)S(1)}, f32[128,256]{1,0:T(8,128)S(1)}, u32[]{:S(2)}, u32[]{:S(2)}) %collective-permute-start.5) | collective-permute-done | bytes 131104 | tf_op jit(solution)/shard_map/ppermute | solution.py:212
  20.6 9.1 %collective-permute-done.17 = bf16[256,512]{1,0:T(8,128)(2,1)S(1)} collective-permute-done((bf16[256,512]{1,0:T(8,128)(2,1)S(1)}, bf16[256,512]{1,0:T(8,128)(2,1)S(1)}, u32[]{:S(2)}, u32[]{:S(2)}) %collective-permute-start.17) | collective-permute-done | bytes 262176 | tf_op jit(solution)/shard_map/ppermute | solution.py:212
  39.7 1.5 %collective-permute-start.19 = (bf16[512,256]{1,0:T(8,128)(2,1)}, bf16[512,256]{1,0:T(8,128)(2,1)S(1)}, u32[]{:S(2)}, u32[]{:S(2)}) collective-permute-start(bf16[512,256]{1,0:T(8,128)(2,1)} %get-tuple-element.47), channel_id=1, source_target_pairs={{0,2},{2,0},{4,6},{6,4},{8,10},{10,8},{12,14},{14,12},{16,18},{18,... | collective-permute-start | bytes 786440 | tf_op jit(solution)/shard_map/ppermute | solution.py:212
  44.8 2.2 %collective-permute-done.22.refs_6_ = bf16[512,256]{1,0:T(8,128)(2,1)S(1)} collective-permute-done((bf16[512,256]{1,0:T(8,128)(2,1)}, bf16[512,256]{1,0:T(8,128)(2,1)S(1)}, u32[]{:S(2)}, u32[]{:S(2)}) %collective-permute-start.22) | collective-permute-done | bytes 262176 | tf_op jit(solution)/shard_map/ppermute | solution.py:212
  49.2 3.4 %collective-permute-done.23.refs_7_ = bf16[512,256]{1,0:T(8,128)(2,1)S(1)} collective-permute-done((bf16[512,256]{1,0:T(8,128)(2,1)S(1)}, bf16[512,256]{1,0:T(8,128)(2,1)S(1)}, u32[]{:S(2)}, u32[]{:S(2)}) %collective-permute-start.23) | collective-permute-done | bytes 262176 | tf_op jit(solution)/shard_map/ppermute | solution.py:212
  52.6 2.2 %collective-permute-done.20.refs_4_ = bf16[512,256]{1,0:T(8,128)(2,1)S(1)} collective-permute-done((bf16[512,256]{1,0:T(8,128)(2,1)S(1)}, bf16[512,256]{1,0:T(8,128)(2,1)S(1)}, u32[]{:S(2)}, u32[]{:S(2)}) %collective-permute-start.20) | collective-permute-done | bytes 262176 | tf_op jit(solution)/shard_map/ppermute | solution.py:212
  54.8 1.5 %shard_map.107 = (f32[256,512]{1,0:T(8,128)S(1)}, f32[128,256]{1,0:T(8,128)S(1)}, f32[128,256]{1,0:T(8,128)S(1)}) custom-call(s32[1]{0:T(128)} %bitcast.here_ref, bf16[512,512]{1,0:T(8,128)(2,1)S(1)} %constant_dynamic-update-slice_fusion.refs_0_.refs_1_, bf16[512,512]{1,0:T(8,128)(2,1)S(1)} %constant_dynamic-update-slice_fusion.refs_0_.refs_1_, ...), custom_call_target="tpu_custom_call" | custom-call | flops 637534208 | bytes 3803140 | tf_op jit(solution)/shard_map/pallas_call | solution.py:60
  65.1 2.0 %collective-permute-start.9 = (bf16[512,256]{1,0:T(8,128)(2,1)S(1)}, bf16[512,256]{1,0:T(8,128)(2,1)S(1)}, u32[]{:S(2)}, u32[]{:S(2)}) collective-permute-start(bf16[512,256]{1,0:T(8,128)(2,1)S(1)} %get-tuple-element.38), channel_id=1, source_target_pairs={{0,4},{2,6},{4,0},{6,2},{8,12},{10,14},{12,8},{14,10},{16,20},{18,... | collective-permute-start | bytes 786440 | tf_op jit(solution)/shard_map/ppermute | solution.py:212
  67.2 4.8 %collective-permute-start.30 = (bf16[128,256]{1,0:T(8,128)(2,1)S(1)}, bf16[128,256]{1,0:T(8,128)(2,1)S(1)}, u32[]{:S(2)}, u32[]{:S(2)}) collective-permute-start(bf16[128,256]{1,0:T(8,128)(2,1)S(1)} %fusion.8), channel_id=1, source_target_pairs={{0,16},{2,18},{4,20},{6,22},{8,24},{10,26},{12,28},{14,30},{1,17},... | collective-permute-start | bytes 196616 | tf_op jit(solution)/shard_map/ppermute | solution.py:217
  74.5 1.9 %collective-permute-done.26 = bf16[128,256]{1,0:T(8,128)(2,1)S(1)} collective-permute-done((bf16[128,256]{1,0:T(8,128)(2,1)S(1)}, bf16[128,256]{1,0:T(8,128)(2,1)S(1)}, u32[]{:S(2)}, u32[]{:S(2)}) %collective-permute-start.26) | collective-permute-done | bytes 65568 | tf_op jit(solution)/shard_map/ppermute | solution.py:212
  76.4 3.3 %collective-permute-start.27 = (bf16[128,256]{1,0:T(8,128)(2,1)S(1)}, bf16[128,256]{1,0:T(8,128)(2,1)S(1)}, u32[]{:S(2)}, u32[]{:S(2)}) collective-permute-start(bf16[128,256]{1,0:T(8,128)(2,1)S(1)} %fusion.5), channel_id=1, source_target_pairs={{0,16},{2,18},{4,20},{6,22},{8,24},{10,26},{12,28},{14,30},{1,17},... | collective-permute-start | bytes 196616 | tf_op jit(solution)/shard_map/ppermute | solution.py:217
  79.8 1.8 %collective-permute-done.27 = bf16[128,256]{1,0:T(8,128)(2,1)S(1)} collective-permute-done((bf16[128,256]{1,0:T(8,128)(2,1)S(1)}, bf16[128,256]{1,0:T(8,128)(2,1)S(1)}, u32[]{:S(2)}, u32[]{:S(2)}) %collective-permute-start.27) | collective-permute-done | bytes 65568 | tf_op jit(solution)/shard_map/ppermute | solution.py:217
  82.7 3.7 %psum.7 = f32[256,2]{1,0:T(8,128)S(1)} all-reduce(f32[256,2]{1,0:T(8,128)S(1)} %get-tuple-element.31), channel_id=1, replica_groups=mesh['ctx'=16,'head'=2] {'head'}, use_global_device_ids=true, to_apply=%region_0.1 | all-reduce | flops 512 | bytes 4096 | tf_op jit(solution)/shard_map/psum | solution.py:366
  88.2 3.3 %collective-permute-start.14 = (bf16[256,256]{1,0:T(8,128)(2,1)S(1)}, bf16[256,256]{1,0:T(8,128)(2,1)S(1)}, u32[]{:S(2)}, u32[]{:S(2)}) collective-permute-start(bf16[256,256]{1,0:T(8,128)(2,1)S(1)} %get-tuple-element.44), channel_id=1, source_target_pairs={{0,8},{2,10},{4,12},{6,14},{8,0},{10,2},{12,4},{14,6},{16,24},{18,... | collective-permute-start | bytes 393224 | tf_op jit(solution)/shard_map/ppermute | solution.py:212
  91.6 4.2 %collective-permute-done.14 = bf16[256,256]{1,0:T(8,128)(2,1)S(1)} collective-permute-done((bf16[256,256]{1,0:T(8,128)(2,1)S(1)}, bf16[256,256]{1,0:T(8,128)(2,1)S(1)}, u32[]{:S(2)}, u32[]{:S(2)}) %collective-permute-start.14) | collective-permute-done | bytes 131104 | tf_op jit(solution)/shard_map/ppermute | solution.py:212
  95.8 3.3 %collective-permute-start.15 = (bf16[128,256]{1,0:T(8,128)(2,1)S(1)}, bf16[128,256]{1,0:T(8,128)(2,1)S(1)}, u32[]{:S(2)}, u32[]{:S(2)}) collective-permute-start(bf16[128,256]{1,0:T(8,128)(2,1)S(1)} %fusion.9), channel_id=1, source_target_pairs={{0,16},{2,18},{4,20},{6,22},{8,24},{10,26},{12,28},{14,30},{16,0},... | collective-permute-start | bytes 196616 | tf_op jit(solution)/shard_map/ppermute | solution.py:212
  99.1 2.8 %collective-permute-start.11 = (bf16[128,256]{1,0:T(8,128)(2,1)S(1)}, bf16[128,256]{1,0:T(8,128)(2,1)S(1)}, u32[]{:S(2)}, u32[]{:S(2)}) collective-permute-start(bf16[128,256]{1,0:T(8,128)(2,1)S(1)} %fusion.11), channel_id=1, source_target_pairs={{0,16},{2,18},{4,20},{6,22},{8,24},{10,26},{12,28},{14,30},{16,0},... | collective-permute-start | bytes 196616 | tf_op jit(solution)/shard_map/ppermute | solution.py:212
  102.1 2.8 %collective-permute-done.11 = bf16[128,256]{1,0:T(8,128)(2,1)S(1)} collective-permute-done((bf16[128,256]{1,0:T(8,128)(2,1)S(1)}, bf16[128,256]{1,0:T(8,128)(2,1)S(1)}, u32[]{:S(2)}, u32[]{:S(2)}) %collective-permute-start.11) | collective-permute-done | bytes 65568 | tf_op jit(solution)/shard_map/ppermute | solution.py:212
  (99 shorter events, 35.5 us)
Async XLA Ops:
  2.2 6.5 %collective-permute-start = (f32[128,256]{1,0:T(8,128)S(1)}, f32[128,256]{1,0:T(8,128)S(1)}, u32[]{:S(2)}, u32[]{:S(2)}) collective-permute-start(f32[128,256]{1,0:T(8,128)S(1)} %get-tuple-element.18), channel_id=1, source_target_pairs={{0,2},{2,0},{4,6},{6,4},{8,10},{10,8},{12,14},{14,12},{16,18},{18,... | collective-permute-start | bytes 393224 | tf_op jit(solution)/shard_map/ppermute | solution.py:212
  8.7 6.2 %collective-permute-start.1 = (f32[128,256]{1,0:T(8,128)S(1)}, f32[128,256]{1,0:T(8,128)S(1)}, u32[]{:S(2)}, u32[]{:S(2)}) collective-permute-start(f32[128,256]{1,0:T(8,128)S(1)} %add.116), channel_id=1, source_target_pairs={{0,4},{2,6},{4,0},{6,2},{8,12},{10,14},{12,8},{14,10},{16,20},{18,... | collective-permute-start | bytes 393224 | tf_op jit(solution)/shard_map/ppermute | solution.py:212
  10.6 8.7 %collective-permute-start.5 = (f32[128,256]{1,0:T(8,128)S(1)}, f32[128,256]{1,0:T(8,128)S(1)}, u32[]{:S(2)}, u32[]{:S(2)}) collective-permute-start(f32[128,256]{1,0:T(8,128)S(1)} %add.122), channel_id=1, source_target_pairs={{0,8},{2,10},{4,12},{6,14},{8,0},{10,2},{12,4},{14,6},{16,24},{18,... | collective-permute-start | bytes 393224 | tf_op jit(solution)/shard_map/ppermute | solution.py:212
  12.2 17.4 %collective-permute-start.17 = (bf16[256,512]{1,0:T(8,128)(2,1)S(1)}, bf16[256,512]{1,0:T(8,128)(2,1)S(1)}, u32[]{:S(2)}, u32[]{:S(2)}) collective-permute-start(bf16[256,512]{1,0:T(8,128)(2,1)S(1)} %pad_maximum_fusion.1), channel_id=1, source_target_pairs={{0,16},{2,18},{4,20},{6,22},{8,24},{10,26},{12,28},{14,30},{16,0},... | collective-permute-start | bytes 786440 | tf_op jit(solution)/shard_map/ppermute | solution.py:212
  15.0 19.4 %collective-permute-start.2 = (f32[128,256]{1,0:T(8,128)S(1)}, f32[128,256]{1,0:T(8,128)S(1)}, u32[]{:S(2)}, u32[]{:S(2)}) collective-permute-start(f32[128,256]{1,0:T(8,128)S(1)} %add.118), channel_id=1, source_target_pairs={{0,8},{2,10},{4,12},{6,14},{8,0},{10,2},{12,4},{14,6},{16,24},{18,... | collective-permute-start | bytes 393224 | tf_op jit(solution)/shard_map/ppermute | solution.py:212
  19.3 13.2 %collective-permute-start.6 = (f32[128,256]{1,0:T(8,128)S(1)}, f32[128,256]{1,0:T(8,128)S(1)}, u32[]{:S(2)}, u32[]{:S(2)}) collective-permute-start(f32[128,256]{1,0:T(8,128)S(1)} %add.123), channel_id=1, source_target_pairs={{16,0},{18,2},{20,4},{22,6},{24,8},{26,10},{28,12},{30,14},{17,1},... | collective-permute-start | bytes 393224 | tf_op jit(solution)/shard_map/ppermute | solution.py:217
  30.5 10.7 %collective-permute-start.21 = (bf16[512,256]{1,0:T(8,128)(2,1)}, bf16[512,256]{1,0:T(8,128)(2,1)S(1)}, u32[]{:S(2)}, u32[]{:S(2)}) collective-permute-start(bf16[512,256]{1,0:T(8,128)(2,1)} %get-tuple-element.46), channel_id=1, source_target_pairs={{0,2},{2,0},{4,6},{6,4},{8,10},{10,8},{12,14},{14,12},{16,18},{18,... | collective-permute-start | bytes 786440 | tf_op jit(solution)/shard_map/ppermute | solution.py:212
  32.0 9.8 %collective-permute-start.18 = (bf16[512,256]{1,0:T(8,128)(2,1)}, bf16[512,256]{1,0:T(8,128)(2,1)S(1)}, u32[]{:S(2)}, u32[]{:S(2)}) collective-permute-start(bf16[512,256]{1,0:T(8,128)(2,1)} %get-tuple-element.47), channel_id=1, source_target_pairs={{0,4},{2,6},{4,0},{6,2},{8,12},{10,14},{12,8},{14,10},{16,20},{18,... | collective-permute-start | bytes 786440 | tf_op jit(solution)/shard_map/ppermute | solution.py:212
  33.2 6.5 %collective-permute-start.7 = (f32[128,256]{1,0:T(8,128)}, f32[128,256]{1,0:T(8,128)S(1)}, u32[]{:S(2)}, u32[]{:S(2)}) collective-permute-start(f32[128,256]{1,0:T(8,128)} %get-tuple-element.36), channel_id=1, source_target_pairs={{0,2},{2,0},{4,6},{6,4},{8,10},{10,8},{12,14},{14,12},{16,18},{18,... | collective-permute-start | bytes 393224 | tf_op jit(solution)/shard_map/ppermute | solution.py:212
  34.4 8.5 %collective-permute-start.3 = (f32[128,256]{1,0:T(8,128)S(1)}, f32[128,256]{1,0:T(8,128)S(1)}, u32[]{:S(2)}, u32[]{:S(2)}) collective-permute-start(f32[128,256]{1,0:T(8,128)S(1)} %add.120), channel_id=1, source_target_pairs={{16,0},{18,2},{20,4},{22,6},{24,8},{26,10},{28,12},{30,14},{17,1},... | collective-permute-start | bytes 393224 | tf_op jit(solution)/shard_map/ppermute | solution.py:217
  37.4 9.5 %collective-permute-start.22 = (bf16[512,256]{1,0:T(8,128)(2,1)}, bf16[512,256]{1,0:T(8,128)(2,1)S(1)}, u32[]{:S(2)}, u32[]{:S(2)}) collective-permute-start(bf16[512,256]{1,0:T(8,128)(2,1)} %get-tuple-element.46), channel_id=1, source_target_pairs={{0,4},{2,6},{4,0},{6,2},{8,12},{10,14},{12,8},{14,10},{16,20},{18,... | collective-permute-start | bytes 786440 | tf_op jit(solution)/shard_map/ppermute | solution.py:212
  39.7 9.5 %collective-permute-start.19 = (bf16[512,256]{1,0:T(8,128)(2,1)}, bf16[512,256]{1,0:T(8,128)(2,1)S(1)}, u32[]{:S(2)}, u32[]{:S(2)}) collective-permute-start(bf16[512,256]{1,0:T(8,128)(2,1)} %get-tuple-element.47), channel_id=1, source_target_pairs={{0,2},{2,0},{4,6},{6,4},{8,10},{10,8},{12,14},{14,12},{16,18},{18,... | collective-permute-start | bytes 786440 | tf_op jit(solution)/shard_map/ppermute | solution.py:212
  41.3 11.3 %collective-permute-start.23 = (bf16[512,256]{1,0:T(8,128)(2,1)S(1)}, bf16[512,256]{1,0:T(8,128)(2,1)S(1)}, u32[]{:S(2)}, u32[]{:S(2)}) collective-permute-start(bf16[512,256]{1,0:T(8,128)(2,1)S(1)} %collective-permute-done.21.refs_5_), channel_id=1, source_target_pairs={{0,4},{2,6},{4,0},{6,2},{8,12},{10,14},{12,8},{14,10},{16,20},{18,... | collective-permute-start | bytes 786440 | tf_op jit(solution)/shard_map/ppermute | solution.py:212
  41.8 13.0 %collective-permute-start.20 = (bf16[512,256]{1,0:T(8,128)(2,1)S(1)}, bf16[512,256]{1,0:T(8,128)(2,1)S(1)}, u32[]{:S(2)}, u32[]{:S(2)}) collective-permute-start(bf16[512,256]{1,0:T(8,128)(2,1)S(1)} %collective-permute-done.18.refs_2_), channel_id=1, source_target_pairs={{0,2},{2,0},{4,6},{6,4},{8,10},{10,8},{12,14},{14,12},{16,18},{18,... | collective-permute-start | bytes 786440 | tf_op jit(solution)/shard_map/ppermute | solution.py:212
  43.8 21.3 %collective-permute-start.8 = (bf16[1024,256]{1,0:T(8,128)(2,1)S(1)}, bf16[1024,256]{1,0:T(8,128)(2,1)S(1)}, u32[]{:S(2)}, u32[]{:S(2)}) collective-permute-start(bf16[1024,256]{1,0:T(8,128)(2,1)S(1)} %get-tuple-element.22), channel_id=1, source_target_pairs={{0,2},{2,0},{4,6},{6,4},{8,10},{10,8},{12,14},{14,12},{16,18},{18,... | collective-permute-start | bytes 1572872 | tf_op jit(solution)/shard_map/ppermute | solution.py:212
  47.0 17.1 %collective-permute-start.12 = (bf16[1024,256]{1,0:T(8,128)(2,1)S(1)}, bf16[1024,256]{1,0:T(8,128)(2,1)S(1)}, u32[]{:S(2)}, u32[]{:S(2)}) collective-permute-start(bf16[1024,256]{1,0:T(8,128)(2,1)S(1)} %get-tuple-element.24), channel_id=1, source_target_pairs={{0,4},{2,6},{4,0},{6,2},{8,12},{10,14},{12,8},{14,10},{16,20},{18,... | collective-permute-start | bytes 1572872 | tf_op jit(solution)/shard_map/ppermute | solution.py:212
  56.3 6.1 %collective-permute-start.28 = (bf16[128,256]{1,0:T(8,128)(2,1)S(1)}, bf16[128,256]{1,0:T(8,128)(2,1)S(1)}, u32[]{:S(2)}, u32[]{:S(2)}) collective-permute-start(bf16[128,256]{1,0:T(8,128)(2,1)S(1)} %convert_element_type.136), channel_id=1, source_target_pairs={{0,4},{2,6},{4,0},{6,2},{8,12},{10,14},{12,8},{14,10},{16,20},{18,... | collective-permute-start | bytes 196616 | tf_op jit(solution)/shard_map/ppermute | solution.py:212
  62.7 9.3 %collective-permute-start.25 = (bf16[128,256]{1,0:T(8,128)(2,1)S(1)}, bf16[128,256]{1,0:T(8,128)(2,1)S(1)}, u32[]{:S(2)}, u32[]{:S(2)}) collective-permute-start(bf16[128,256]{1,0:T(8,128)(2,1)S(1)} %fusion.13), channel_id=1, source_target_pairs={{0,4},{2,6},{4,0},{6,2},{8,12},{10,14},{12,8},{14,10},{16,20},{18,... | collective-permute-start | bytes 196616 | tf_op jit(solution)/shard_map/ppermute | solution.py:212
  64.2 23.0 %collective-permute-start.13 = (bf16[512,256]{1,0:T(8,128)(2,1)S(1)}, bf16[512,256]{1,0:T(8,128)(2,1)}, u32[]{:S(2)}, u32[]{:S(2)}) collective-permute-start(bf16[512,256]{1,0:T(8,128)(2,1)S(1)} %get-tuple-element.40), channel_id=1, source_target_pairs={{0,2},{2,0},{4,6},{6,4},{8,10},{10,8},{12,14},{14,12},{16,18},{18,... | collective-permute-start | bytes 786440 | tf_op jit(solution)/shard_map/ppermute | solution.py:212
  65.1 26.3 %collective-permute-start.9 = (bf16[512,256]{1,0:T(8,128)(2,1)S(1)}, bf16[512,256]{1,0:T(8,128)(2,1)S(1)}, u32[]{:S(2)}, u32[]{:S(2)}) collective-permute-start(bf16[512,256]{1,0:T(8,128)(2,1)S(1)} %get-tuple-element.38), channel_id=1, source_target_pairs={{0,4},{2,6},{4,0},{6,2},{8,12},{10,14},{12,8},{14,10},{16,20},{18,... | collective-permute-start | bytes 786440 | tf_op jit(solution)/shard_map/ppermute | solution.py:212
  67.2 6.7 %collective-permute-start.30 = (bf16[128,256]{1,0:T(8,128)(2,1)S(1)}, bf16[128,256]{1,0:T(8,128)(2,1)S(1)}, u32[]{:S(2)}, u32[]{:S(2)}) collective-permute-start(bf16[128,256]{1,0:T(8,128)(2,1)S(1)} %fusion.8), channel_id=1, source_target_pairs={{0,16},{2,18},{4,20},{6,22},{8,24},{10,26},{12,28},{14,30},{1,17},... | collective-permute-start | bytes 196616 | tf_op jit(solution)/shard_map/ppermute | solution.py:217
  88.2 7.6 %collective-permute-start.14 = (bf16[256,256]{1,0:T(8,128)(2,1)S(1)}, bf16[256,256]{1,0:T(8,128)(2,1)S(1)}, u32[]{:S(2)}, u32[]{:S(2)}) collective-permute-start(bf16[256,256]{1,0:T(8,128)(2,1)S(1)} %get-tuple-element.44), channel_id=1, source_target_pairs={{0,8},{2,10},{4,12},{6,14},{8,0},{10,2},{12,4},{14,6},{16,24},{18,... | collective-permute-start | bytes 393224 | tf_op jit(solution)/shard_map/ppermute | solution.py:212
  91.5 7.6 %collective-permute-start.10 = (bf16[256,256]{1,0:T(8,128)(2,1)S(1)}, bf16[256,256]{1,0:T(8,128)(2,1)S(1)}, u32[]{:S(2)}, u32[]{:S(2)}) collective-permute-start(bf16[256,256]{1,0:T(8,128)(2,1)S(1)} %get-tuple-element.42), channel_id=1, source_target_pairs={{0,8},{2,10},{4,12},{6,14},{8,0},{10,2},{12,4},{14,6},{16,24},{18,... | collective-permute-start | bytes 393224 | tf_op jit(solution)/shard_map/ppermute | solution.py:212
  95.8 6.2 %collective-permute-start.15 = (bf16[128,256]{1,0:T(8,128)(2,1)S(1)}, bf16[128,256]{1,0:T(8,128)(2,1)S(1)}, u32[]{:S(2)}, u32[]{:S(2)}) collective-permute-start(bf16[128,256]{1,0:T(8,128)(2,1)S(1)} %fusion.9), channel_id=1, source_target_pairs={{0,16},{2,18},{4,20},{6,22},{8,24},{10,26},{12,28},{14,30},{16,0},... | collective-permute-start | bytes 196616 | tf_op jit(solution)/shard_map/ppermute | solution.py:212
  (14 other events, 56.3 us)

commit v2 on v0

v2 whole, which is shorter than its diff:
```python
import functools
import math

import jax
import jax.numpy as jnp
from jax import lax
from jax.experimental import pallas as pl
from jax.experimental.pallas import tpu as pltpu
from jax.sharding import PartitionSpec as P

F32 = jnp.float32
BF16 = jnp.bfloat16
F16 = jnp.float16
GROUP = 4
TAIL = 16


def split(x):
    high = x.astype(BF16)
    return high, (x - high.astype(F32)).astype(BF16)


def dot3(a, b, b_last=False):
    dims = (((1,), (1 if b_last else 0,)), ((), ()))

    def one(x, y):
        return lax.dot_general(x, y, dims, preferred_element_type=F32)

    return one(a[0], b[0]) + (one(a[0], b[1]) + one(a[1], b[0]))


def part(x, k, width):
    return x[:, k * width : (k + 1) * width]


def call(body, outs, *args, scratch=(), spaces=None, flops=0):
    vmem = pl.BlockSpec(memory_space=pltpu.VMEM)
    size = sum(a.size * a.dtype.itemsize for a in args)
    return pl.pallas_call(
        body,
        out_shape=outs,
        in_specs=[vmem] * len(args) if spaces is None else spaces,
        out_specs=jax.tree.map(lambda _: vmem, outs),
        scratch_shapes=list(scratch),
        cost_estimate=pl.CostEstimate(flops=flops, bytes_accessed=size, transcendentals=0),
        compiler_params=pltpu.CompilerParams(vmem_limit_bytes=40 * 1024 * 1024),
    )(*args)


def exponent(x):
    top = jnp.max(jnp.abs(x), axis=(0, 1), keepdims=True)
    return jnp.clip(jnp.ceil(jnp.log(jnp.maximum(top, 1e-30)) * (1.0 / math.log(2.0))), -90.0, 40.0) - 14.0


def power(k):
    return jnp.exp(k * math.log(2.0))


def messages(place_ref, q_ref, v_ref, dout_ref, routing_ref, gates_ref, own, near, far, both):
    count, width = q_ref.shape
    routing, gates = routing_ref[...], gates_ref[...]
    place = place_ref[0]
    q, v, dout = q_ref[...], v_ref[...], dout_ref[...]
    exponents = [exponent(x) for x in (q, v, dout)]
    scales = [1.0 / power(k) for k in exponents]
    for off, ref in enumerate((own, near, far, both)):
        hit = routing == (place ^ off)
        weight = jnp.sum(jnp.where(hit, gates, 0.0), axis=1, keepdims=True)
        routed = jnp.sum(hit.astype(F32), axis=1, keepdims=True)
        for k, x in enumerate((weight * q, routed * v, dout)):
            column = slice(k * width, (k + 1) * width)
            if off:
                ref[:count, column] = x * scales[k]
                ref[count:, column] = jnp.broadcast_to(exponents[k], (TAIL, width))
            else:
                ref[:, column] = x


def group_sums(place, states, sums_ref, total_ref, reverse):
    size = states[0].shape[0]
    for to in range(GROUP):
        total = jnp.zeros_like(states[0])
        for off in range(GROUP):
            counts = (place ^ off) > (place ^ to) if reverse else (place ^ off) < (place ^ to)
            total = total + jnp.where(counts, states[off], 0.0)
        sums_ref[to * size : (to + 1) * size, :] = total
    total_ref[...] = (states[0] + states[1]) + (states[2] + states[3])


def grad_states(scale, place_ref, own, near, far, both, all_ref, sums_ref, total_ref):
    count = own.shape[0]
    width = own.shape[1] // 3
    states = []
    for off, ref in enumerate((own, near, far, both)):
        for k in range(3):
            column = slice(k * width, (k + 1) * width)
            x = ref[:count, column]
            if off:
                x = x * power(ref[count : count + 1, column])
            all_ref[off * count : (off + 1) * count, column] = x
        rows = all_ref[off * count : (off + 1) * count, :]
        states.append(scale * dot3(split(part(rows, 2, width).T), split(part(rows, 0, width))))
    group_sums(place_ref[0], states, sums_ref, total_ref, True)


def inner_key(scale, all_ref, out_ref):
    width = all_ref.shape[1] // 3
    count = all_ref.shape[0] // GROUP
    places = lax.broadcasted_iota(jnp.int32, (count, count), 0)
    others = lax.broadcasted_iota(jnp.int32, (count, count), 1)
    for off in range(GROUP):
        rows = all_ref[off * count : (off + 1) * count, :]
        scores = dot3(split(part(rows, 1, width)), split(part(rows, 2, width)), True)
        scores = jnp.where(others >= places, scores, 0.0)
        out_ref[off * count : (off + 1) * count, :] = scale * dot3(split(scores), split(part(rows, 0, width)))


def key_low(all_ref, sums_ref, before_ref, inner_ref, low_ref, grad_ref):
    width = all_ref.shape[1] // 3
    count = all_ref.shape[0] // GROUP
    for off in range(GROUP):
        grad = sums_ref[off * width : (off + 1) * width, :] + before_ref[...]
        grad_ref[off * width : (off + 1) * width, :] = grad
        span = slice(off * count, (off + 1) * count)
        carried = dot3(split(all_ref[span, width : 2 * width]), split(grad))
        low_ref[span, :] = (carried + inner_ref[span, :]).astype(BF16)


def pieces_of(tokens_ref, first_ref, first_other, last_ref, last_other, core):
    count, width = tokens_ref.shape
    half, side = count // 2, width // 2
    found = []
    for column in range(2):
        found.append((0, 0, count, column, tokens_ref, 0, column * side))
        for ref, whose in ((first_ref, core), (first_other, 1 - core)):
            for off in (1, 2):
                row = ((off - 1) * 2 + column) * half
                found.append((off, whose * half, half, column, ref, row, 0))
        for ref, whose in ((last_ref, core), (last_other, 1 - core)):
            found.append((3, whose * half, half, column, ref, column * half, 0))
    return found


def products(high, place_ref, tokens_ref, first_ref, first_other, last_ref, last_other, low_ref, sent_ref, kept_ref, turned, low_t):
    count, width = tokens_ref.shape
    side = width // 2
    core = place_ref[1]
    group = place_ref[2]
    sums = [None, None]
    for block, row, size, column, ref, at, left in pieces_of(tokens_ref, first_ref, first_other, last_ref, last_other, core):
        start = block * count + row
        if not isinstance(row, int):
            start = pl.multiple_of(start, size)
        low = low_ref[pl.ds(start, size), :].T
        term = jnp.dot(low, ref[at : at + size, left : left + side], preferred_element_type=F32)
        sums[column] = term if sums[column] is None else sums[column] + term
    turned[:, :side] = sums[0]
    turned[:, side:] = sums[1]
    groups = 1 << len(high)
    span = width // groups
    order = halving_order(high)
    for k, off in enumerate(order):
        start = pl.multiple_of((group ^ off // GROUP) * span, span)
        rows = turned[:, pl.ds(start, span)].T
        if k < groups // 2:
            kept_ref[k * span : (k + 1) * span, :] = rows
        else:
            k -= groups // 2
            sent_ref[k * span : (k + 1) * span, :] = rows.astype(BF16)


def halving_order(high):
    order = [0]
    for bit in high:
        order = [off + more for off in order for more in (0, bit)]
    return order


def key_states(layout, parts, place_ref, *refs):
    chunks = len(layout)
    (tokens_ref, first_ref, first_other, last_ref, last_other, all_ref,
     keys_ref, sums_ref, total_ref, weights, sem) = refs[chunks:]
    rows = weights.shape[0] // parts
    here, core = place_ref[3], place_ref[1]
    copies = []
    for ref, offsets in zip(refs[:chunks], layout, strict=True):
        for k, off in enumerate(offsets):
            start = pl.multiple_of((here ^ off) * rows, rows)
            copy = pltpu.make_async_copy(
                ref.at[pl.ds(k * rows, rows), :], weights.at[pl.ds(start, rows), :], sem.at[len(copies)]
            )
            copy.start()
            copies.append(copy)
    for copy in copies:
        copy.wait()
    count, width = tokens_ref.shape
    side = width // 2
    for block, row, size, column, ref, at, left in pieces_of(tokens_ref, first_ref, first_other, last_ref, last_other, core):
        start = block * count + row
        if not isinstance(row, int):
            start = pl.multiple_of(start, size)
        term = jnp.dot(
            ref[at : at + size, left : left + side],
            weights[column * side : (column + 1) * side, :],
            preferred_element_type=F32,
        )
        if column:
            term = keys_ref[pl.ds(start, size), :] + term
        keys_ref[pl.ds(start, size), :] = term
    head_dim = keys_ref.shape[1]
    states = []
    for off in range(GROUP):
        span = slice(off * count, (off + 1) * count)
        values = all_ref[span, head_dim : 2 * head_dim]
        states.append(dot3(split(values.T), split(keys_ref[span, :])))
    group_sums(place_ref[0], states, sums_ref, total_ref, False)


def inner_rest(scale, all_ref, keys_ref, grad_ref, value_ref, state_ref):
    width = keys_ref.shape[1]
    count = keys_ref.shape[0] // GROUP
    places = lax.broadcasted_iota(jnp.int32, (count, count), 0)
    others = lax.broadcasted_iota(jnp.int32, (count, count), 1)
    for off in range(GROUP):
        span = slice(off * count, (off + 1) * count)
        rows = all_ref[span, :]
        lifted, values, dout = (split(part(rows, k, width)) for k in range(3))
        keys = split(keys_ref[span, :])
        mixed = jnp.where(others >= places, dot3(keys, lifted, True), 0.0)
        carried = dot3(keys, split(grad_ref[off * width : (off + 1) * width, :]), True)
        value_ref[span, :] = carried + scale * dot3(split(mixed), dout)
        scores = jnp.where(places >= others, dot3(dout, values, True), 0.0)
        state_ref[span, :] = dot3(split(scores), keys)


def results(all_ref, sums_ref, before_ref, state_ref, value_ref, own, near, far, both):
    width = before_ref.shape[1]
    count = state_ref.shape[0] // GROUP
    for off, ref in enumerate((own, near, far, both)):
        span = slice(off * count, (off + 1) * count)
        before = sums_ref[off * width : (off + 1) * width, :] + before_ref[...]
        state = state_ref[span, :] + dot3(split(all_ref[span, 2 * width :]), split(before))
        ref[:, :width] = state.astype(ref.dtype)
        ref[:, width:] = value_ref[span, :].astype(ref.dtype)


def at_home(scale, place_ref, q_ref, routing_ref, gates_ref, own, near, far, both, query_ref, value_ref, gate_ref):
    queries, routing, gates = q_ref[...], routing_ref[...], gates_ref[...]
    width = queries.shape[1]
    query = jnp.zeros_like(queries)
    value = jnp.zeros_like(queries)
    gate = jnp.zeros(gate_ref.shape, F32)
    for off, ref in enumerate((own, near, far, both)):
        hit = routing == (place_ref[0] ^ off)
        weight = jnp.sum(jnp.where(hit, gates, 0.0), axis=1, keepdims=True)
        routed = jnp.sum(hit.astype(F32), axis=1, keepdims=True)
        state = ref[:, :width].astype(F32)
        query = query + weight * state
        value = value + routed * ref[:, width:].astype(F32)
        gate = gate + jnp.where(hit, jnp.sum(queries * state, axis=1, keepdims=True), 0.0)
    query_ref[...] = scale * query
    value_ref[...] = value
    gate_ref[...] = scale * gate


def by_column(place_ref, x_ref, own, near, far, both):
    size = own.shape[1]
    for off, ref in enumerate((own, near, far, both)):
        ref[...] = x_ref[:, pl.ds(pl.multiple_of((place_ref[0] ^ off) * size, size), size)]


def by_row(place_ref, x_ref, got_ref, own, near, far, both, room):
    size = own.shape[0]
    room[...] = x_ref[...] + got_ref[...].astype(F32)
    for off, ref in enumerate((own, near, far, both)):
        ref[...] = room[pl.ds(pl.multiple_of((place_ref[0] ^ off) * size, size), size), :]


def in_columns(place_ref, own, near, far, both, out_ref):
    size = own.shape[1]
    for off, ref in enumerate((own, near, far, both)):
        out_ref[:, pl.ds(pl.multiple_of((place_ref[0] ^ off) * size, size), size)] = ref[...]


def swap(x, off, parts):
    return lax.ppermute(x, "ctx", [(i, i ^ off) for i in range(parts)])


def one_way(x, off, parts, reverse):
    sources = [i for i in range(parts) if bool(i & off) == reverse]
    return lax.ppermute(x, "ctx", [(i, i ^ off) for i in sources])


def other_core(x):
    return lax.ppermute(x, "head", [(i, i ^ 1) for i in range(lax.axis_size("head"))])


def prefix(total, bits, parts, here, reverse):
    before = jnp.zeros_like(total)
    for bit in bits[:-1]:
        got = swap(total, bit, parts)
        before = before + jnp.where(((here & bit) == 0) == reverse, got, 0.0)
        total = total + got
    return before + one_way(total, bits[-1], parts, reverse)


def on_device(tokens, queries, values, dout, key_weight, routing, gates):
    count, width = tokens.shape
    rows, memories, head_dim = key_weight.shape
    parts = lax.axis_size("ctx")
    high = [1 << k for k in range(2, parts.bit_length() - 1)]
    here = lax.axis_index("ctx").astype(jnp.int32)
    core = lax.axis_index("head").astype(jnp.int32) & 1
    at = jnp.stack([here & (GROUP - 1), core, here // GROUP, here])
    scale = 1.0 / math.sqrt(head_dim * count * parts)
    tall = GROUP * count
    smem = pl.BlockSpec(memory_space=pltpu.SMEM)
    vmem = pl.BlockSpec(memory_space=pltpu.VMEM)
    anywhere = pl.BlockSpec(memory_space=pl.ANY)

    def shape(r, c, dtype=F32):
        return jax.ShapeDtypeStruct((r, c), dtype)

    mine = call(
        by_column,
        [shape(rows, head_dim, BF16)] * 4,
        at, key_weight.reshape(rows, memories * head_dim),
        spaces=[smem, vmem],
    )
    weights = [mine[0]] + [swap(mine[off], off, parts) for off in (1, 2, 3)]

    half = lax.dynamic_slice(tokens, (core * (count // 2), jnp.int32(0)), (count // 2, width))
    left, right = half[:, : width // 2], half[:, width // 2 :]
    left_x, right_y = swap(left, 1, parts), swap(right, 2, parts)

    sent = call(
        messages,
        [shape(count, 3 * head_dim)] + [shape(count + TAIL, 3 * head_dim)] * 3,
        at, queries, values, dout, routing, gates,
        spaces=[smem] + [vmem] * 5,
    )
    got = [swap(sent[off].astype(F16), off, parts).astype(F32) for off in (1, 2, 3)]

    right_x, left_y = swap(right, 1, parts), swap(left, 2, parts)
    first = jnp.concatenate([left_x, right_x, left_y, right_y], axis=0)
    last = jnp.concatenate([swap(left_x, 2, parts), swap(right_y, 1, parts)], axis=0)

    block = jnp.concatenate(weights, axis=0)
    held = [0, 1, 2, 3]
    for bit in reversed(high):
        block = jnp.concatenate([block, swap(block, bit, parts)], axis=0)
        held = held + [off ^ bit for off in held]

    every, grad_sums, total = call(
        functools.partial(grad_states, scale),
        [shape(tall, 3 * head_dim), shape(GROUP * head_dim, head_dim), shape(head_dim, head_dim)],
        at, sent[0], *got,
        spaces=[smem] + [vmem] * 4,
        flops=6 * tall * head_dim * head_dim,
    )
    before = prefix(total, high, parts, here, True)
    inner_k = call(
        functools.partial(inner_key, scale),
        shape(tall, head_dim),
        every,
        flops=12 * tall * count * head_dim,
    )
    low, grad_in = call(
        key_low,
        [shape(tall, head_dim, BF16), shape(GROUP * head_dim, head_dim)],
        every, grad_sums, before, inner_k,
        flops=6 * tall * head_dim * head_dim,
    )

    first_other, last_other = other_core(first), other_core(last)
    group_tokens = (tokens, first, first_other, last, last_other)

    sent, kept = call(
        functools.partial(products, high),
        [shape(width // 2, head_dim, BF16), shape(width // 2, head_dim)],
        at, *group_tokens, low,
        spaces=[smem] + [vmem] * 6,
        scratch=[pltpu.VMEM((head_dim, width), F32), pltpu.VMEM((head_dim, tall), BF16)],
        flops=2 * tall * width * head_dim,
    )
    reduced = swap(sent, high[0], parts)
    for bit in high[1:]:
        size = kept.shape[0] // 2
        sent = (kept[size:] + reduced[size:].astype(F32)).astype(BF16)
        kept = kept[:size] + reduced[:size].astype(F32)
        reduced = swap(sent, bit, parts)
    mine = call(
        by_row,
        [shape(rows, head_dim)] * 4,
        at, kept, reduced,
        spaces=[smem, vmem, vmem],
        scratch=[pltpu.VMEM((GROUP * rows, head_dim), F32)],
    )
    key_grad = call(
        in_columns,
        shape(rows, memories * head_dim),
        at, mine[0], *[swap(mine[off], off, parts) for off in (1, 2, 3)],
        spaces=[smem] + [vmem] * 4,
    ).reshape(rows, memories, head_dim)

    keys, sums, total = call(
        functools.partial(key_states, [held], parts),
        [shape(tall, head_dim), shape(GROUP * head_dim, head_dim), shape(head_dim, head_dim)],
        at, block, *group_tokens, every,
        spaces=[smem, anywhere] + [vmem] * 6,
        scratch=[pltpu.VMEM((width, head_dim), BF16), pltpu.SemaphoreType.DMA((parts,))],
        flops=2 * tall * width * head_dim,
    )
    before = prefix(total, high, parts, here, False)
    inner_v, inner_state = call(
        functools.partial(inner_rest, scale),
        [shape(tall, head_dim)] * 2,
        every, keys, grad_in,
        flops=24 * tall * count * head_dim,
    )
    sent = call(
        results,
        [shape(count, 2 * head_dim)] + [shape(count, 2 * head_dim, BF16)] * 3,
        every, sums, before, inner_state, inner_v,
        flops=6 * tall * head_dim * head_dim,
    )
    query_grad, value_grad, gate_part = call(
        functools.partial(at_home, scale),
        [shape(count, head_dim), shape(count, head_dim), shape(count, routing.shape[1])],
        at, queries, routing, gates, sent[0], *[swap(sent[off], off, parts) for off in (1, 2, 3)],
        spaces=[smem] + [vmem] * 7,
    )
    gate_grad = lax.psum(gate_part, "head")
    return (key_grad, query_grad, value_grad, gate_grad)


def solution(mesh):
    return jax.shard_map(
        on_device,
        mesh=mesh,
        in_specs=(
            P("ctx", None),
            P("ctx", "head"),
            P("ctx", "head"),
            P("ctx", "head"),
            P("ctx", None, "head"),
            P("ctx", None),
            P("ctx", None),
        ),
        out_specs=(P("ctx", None, "head"), P("ctx", "head"), P("ctx", "head"), P("ctx", None)),
        check_vma=False,
    )
```

time: 412 us -> 97.4 us (0.24)
  waiting for transfers between devices: 324 us -> 17.5 us
  starting transfers between devices: 0.16 us -> 38.5 us
  other arithmetic: 35.4 us -> 2.08 us
  Pallas kernels: 0 us -> 18.7 us
  matrix products: 17.1 us -> 0 us
  between operations: 14.7 us -> 1.05 us
    all_gather x3 -> x0, waiting for transfers between devices: 176 us -> none  [the longest x2 114 us: prefix(): everything = lax.all_gather(x, axis)]
    unnamed x5 -> x0, waiting for transfers between devices: 148 us -> none
    ppermute x0 -> x28, starting transfers between devices: none -> 38.5 us  [the longest x24 31.6 us: swap(): return lax.ppermute(x, 'ctx', [(i, i ^ off) for i in range(parts)])]
    select_n x32 -> x0, other arithmetic: 33.4 us -> none  [step(): return jnp.where(reached, new, before)]
    pallas_call x0 -> x12, Pallas kernels: none -> 18.7 us  [call(): pl.pallas_call(body, out_shape=outs, in_specs=[vmem] * len(args) if space...]
    ppermute x0 -> x28, waiting for transfers between devices: none -> 17.5 us  [the longest x24 17.5 us: swap(): return lax.ppermute(x, 'ctx', [(i, i ^ off) for i in range(parts)])]
    dot_general x13 -> x0, matrix products: 17.1 us -> none  [the longest x1 2.66 us: on_device(): lax.dot_general(columns, key_low, (((0,), (0,)), ((), ())), preferred_ele...]
    reshape x2 -> x1, local copies, waits for them, and re-layouts: 9.67 us -> 0.79 us  [on_device(): key_grad = call(in_columns, shape(rows, memories * head_dim), at, mine[0]...]
  transfers between devices with their start and end apart: 4 -> 28, of which waited for: 4 -> 6; matrix products, arithmetic and copies ran while one was open for 16% -> 15% of each run, Pallas kernels for 0% -> 19%
where the time goes in v2:
time: 97.4 us; the launch traced here: 96.9 us
  starting transfers between devices  38.5 us (40%)
  Pallas kernels  18.7 us (19%)
  waiting for transfers between devices  17.5 us (18%)
  local copies, waits for them, and re-layouts  15.3 us (16%)
  blocking collectives  3.73 us (4%)
  other arithmetic  2.08 us (2%)
  between operations  1.05 us (1%)
    ppermute x24, starting transfers between devices, swap(): return lax.ppermute(x, 'ctx', [(i, i ^ off) for i in range(parts)])  31.6 us
    pallas_call x12, Pallas kernels, call(): pl.pallas_call(body, out_shape=outs, in_specs=[vmem] * len(args) if space...  18.7 us
    ppermute x24, waiting for transfers between devices, swap(): return lax.ppermute(x, 'ctx', [(i, i ^ off) for i in range(parts)])  17.5 us
    unnamed x32, local copies, waits for them, and re-layouts  10.1 us
    ppermute x2, starting transfers between devices, one_way(): return lax.ppermute(x, 'ctx', [(i, i ^ off) for i in sources])  6.74 us
    psum x1, blocking collectives, on_device(): gate_grad = lax.psum(gate_part, 'head')  3.73 us
  transfers between devices with their start and end apart: 28, of which 6 were waited for; matrix products, arithmetic and copies ran while one was open for 15% of the time, Pallas kernels for 19%

profile of v2, /device:TPU:0, one launch (start us, length us, event | category | flops | bytes accessed | tf_op | source)
XLA Modules:
  0.0 96.9 jit_solution(8921551284094531563)
XLA Ops:
  1.8 3.0 %collective-permute-start = (bf16[128,1024]{1,0:T(8,128)(2,1)S(1)}, bf16[128,1024]{1,0:T(8,128)(2,1)}, u32[]{:S(2)}, u32[]{:S(2)}) collective-permute-start(bf16[128,1024]{1,0:T(8,128)(2,1)S(1)} %get-tuple-element.71), channel_id=1, source_target_pairs={{0,2},{2,0},{4,6},{6,4},{8,10},{10,8},{12,14},{14,12},{16,18},{18,... | collective-permute-start | bytes 786440 | tf_op jit(solution)/shard_map/ppermute | solution.py:286
  8.5 2.0 %collective-permute-start.18 = (bf16[128,128]{1,0:T(8,128)(2,1)S(1)}, bf16[128,128]{1,0:T(8,128)(2,1)S(1)}, u32[]{:S(2)}, u32[]{:S(2)}) collective-permute-start(bf16[128,128]{1,0:T(8,128)(2,1)S(1)} %get-tuple-element.50), channel_id=1, source_target_pairs={{0,2},{2,0},{4,6},{6,4},{8,10},{10,8},{12,14},{14,12},{16,18},{18,... | collective-permute-start | bytes 98312 | tf_op jit(solution)/shard_map/ppermute | solution.py:286
  12.5 4.9 %collective-permute-done.18 = bf16[128,128]{1,0:T(8,128)(2,1)S(1)} collective-permute-done((bf16[128,128]{1,0:T(8,128)(2,1)S(1)}, bf16[128,128]{1,0:T(8,128)(2,1)S(1)}, u32[]{:S(2)}, u32[]{:S(2)}) %collective-permute-start.18) | collective-permute-done | bytes 32800 | tf_op jit(solution)/shard_map/ppermute | solution.py:286
  17.5 1.7 %collective-permute-start.8 = (f16[272,384]{1,0:T(8,128)(2,1)S(1)}, f16[272,384]{1,0:T(8,128)(2,1)S(1)}, u32[]{:S(2)}, u32[]{:S(2)}) collective-permute-start(f16[272,384]{1,0:T(8,128)(2,1)S(1)} %convert_element_type.27), channel_id=1, source_target_pairs={{0,2},{2,0},{4,6},{6,4},{8,10},{10,8},{12,14},{14,12},{16,18},{18,... | collective-permute-start | bytes 626696 | tf_op jit(solution)/shard_map/ppermute | solution.py:286
  19.8 1.5 %collective-permute-start.19 = (bf16[128,128]{1,0:T(8,128)(2,1)S(1)}, bf16[128,128]{1,0:T(8,128)(2,1)S(1)}, u32[]{:S(2)}, u32[]{:S(2)}) collective-permute-start(bf16[128,128]{1,0:T(8,128)(2,1)S(1)} %get-tuple-element.51), channel_id=1, source_target_pairs={{0,4},{2,6},{4,0},{6,2},{8,12},{10,14},{12,8},{14,10},{16,20},{18,... | collective-permute-start | bytes 98312 | tf_op jit(solution)/shard_map/ppermute | solution.py:286
  21.3 1.7 %constant_dynamic-update-slice_fusion.3 = bf16[512,1024]{1,0:T(8,128)(2,1)} fusion(bf16[128,1024]{1,0:T(8,128)(2,1)} %collective-permute-done), kind=kLoop, calls=%fused_computation.9 | loop fusion | bytes 524288
  23.2 1.7 %constant_dynamic-update-slice_fusion.2 = bf16[512,1024]{1,0:T(8,128)(2,1)} fusion(bf16[512,1024]{1,0:T(8,128)(2,1)} %constant_dynamic-update-slice_fusion.3, bf16[128,1024]{1,0:T(8,128)(2,1)} %collective-permute-done.1), kind=kLoop, calls=%fused_computation.8 | loop fusion | bytes 524288
  24.9 1.8 %collective-permute-start.5 = (bf16[128,1024]{1,0:T(8,128)(2,1)}, bf16[128,1024]{1,0:T(8,128)(2,1)S(1)}, u32[]{:S(2)}, u32[]{:S(2)}) collective-permute-start(bf16[128,1024]{1,0:T(8,128)(2,1)} %collective-permute-done), channel_id=1, source_target_pairs={{0,4},{2,6},{4,0},{6,2},{8,12},{10,14},{12,8},{14,10},{16,20},{18,... | collective-permute-start | bytes 786440 | tf_op jit(solution)/shard_map/ppermute | solution.py:286
  26.7 1.7 %constant_dynamic-update-slice_fusion.1 = bf16[512,1024]{1,0:T(8,128)(2,1)} fusion(bf16[512,1024]{1,0:T(8,128)(2,1)} %constant_dynamic-update-slice_fusion.2, bf16[128,1024]{1,0:T(8,128)(2,1)} %collective-permute-done.2), kind=kLoop, calls=%fused_computation.7 | loop fusion | bytes 524288
  28.4 1.7 %constant_dynamic-update-slice_fusion.first_ref.refs_2_ = bf16[512,1024]{1,0:T(8,128)(2,1)} fusion(bf16[512,1024]{1,0:T(8,128)(2,1)} %constant_dynamic-update-slice_fusion.1, bf16[128,1024]{1,0:T(8,128)(2,1)} %collective-permute-done.3), kind=kLoop, calls=%fused_computation.6 | loop fusion | bytes 524288 | tf_op jit(solution)/shard_map/concatenate | solution.py:345
  32.7 2.7 %collective-permute-start.21 = (bf16[512,128]{1,0:T(8,128)(2,1)S(1)}, bf16[512,128]{1,0:T(8,128)(2,1)S(1)}, u32[]{:S(2)}, u32[]{:S(2)}) collective-permute-start(bf16[512,128]{1,0:T(8,128)(2,1)S(1)} %pad_maximum_fusion), channel_id=1, source_target_pairs={{0,16},{2,18},{4,20},{6,22},{8,24},{10,26},{12,28},{14,30},{16,0},... | collective-permute-start | bytes 393224 | tf_op jit(solution)/shard_map/ppermute | solution.py:286
  35.3 3.6 %collective-permute-done.6 = bf16[128,1024]{1,0:T(8,128)(2,1)S(1)} collective-permute-done((bf16[128,1024]{1,0:T(8,128)(2,1)}, bf16[128,1024]{1,0:T(8,128)(2,1)S(1)}, u32[]{:S(2)}, u32[]{:S(2)}) %collective-permute-start.6) | collective-permute-done | bytes 262176 | tf_op jit(solution)/shard_map/ppermute | solution.py:286
  39.7 2.1 %collective-permute-done.21 = bf16[512,128]{1,0:T(8,128)(2,1)S(1)} collective-permute-done((bf16[512,128]{1,0:T(8,128)(2,1)S(1)}, bf16[512,128]{1,0:T(8,128)(2,1)S(1)}, u32[]{:S(2)}, u32[]{:S(2)}) %collective-permute-start.21) | collective-permute-done | bytes 131104 | tf_op jit(solution)/shard_map/ppermute | solution.py:286
  44.7 4.1 %collective-permute-done.10 = f16[272,384]{1,0:T(8,128)(2,1)S(1)} collective-permute-done((f16[272,384]{1,0:T(8,128)(2,1)S(1)}, f16[272,384]{1,0:T(8,128)(2,1)S(1)}, u32[]{:S(2)}, u32[]{:S(2)}) %collective-permute-start.10) | collective-permute-done | bytes 208928 | tf_op jit(solution)/shard_map/ppermute | solution.py:286
  48.9 1.7 %shard_map.103 = (f32[1024,384]{1,0:T(8,128)S(1)}, f32[512,128]{1,0:T(8,128)S(1)}, f32[128,128]{1,0:T(8,128)}) custom-call(s32[4]{0:T(128)S(1)} %pad_add_fusion.place_ref, f32[256,384]{1,0:T(8,128)S(1)} %get-tuple-element.35.own, f32[272,384]{1,0:T(8,128)S(1)} %convert_element_type.28.near, f32[272,384]{1,0:T(8,128)S(1)} %convert_element_type.30.far, ...), custom_call_target="tpu_custom_call" | custom-call | flops 100663296 | bytes 1646608 | tf_op jit(solution)/shard_map/pallas_call | solution.py:39
  51.3 1.6 %collective-permute-start.11 = (f32[128,128]{1,0:T(8,128)}, f32[128,128]{1,0:T(8,128)}, u32[]{:S(2)}, u32[]{:S(2)}) collective-permute-start(f32[128,128]{1,0:T(8,128)} %get-tuple-element.41), channel_id=1, source_target_pairs={{0,8},{2,10},{4,12},{6,14},{8,0},{10,2},{12,4},{14,6},{16,24},{18,... | collective-permute-start | bytes 196616 | tf_op jit(solution)/shard_map/ppermute | solution.py:286
  59.1 4.2 %shard_map.110 = (f32[1024,128]{1,0:T(8,128)S(1)}, f32[512,128]{1,0:T(8,128)S(1)}, f32[128,128]{1,0:T(8,128)S(1)}) custom-call(s32[4]{0:T(128)S(1)} %pad_add_fusion.place_ref, bf16[2048,128]{1,0:T(8,128)(2,1)S(1)} %constant_dynamic-update-slice_fusion.11.refs_0_, bf16[256,2048]{1,0:T(8,128)(2,1)S(1)} %copy-done, ...), custom_call_target="tpu_custom_call" | custom-call | flops 536870912 | bytes 6291472 | tf_op jit(solution)/shard_map/pallas_call | solution.py:39
  63.3 1.7 %collective-permute-start.23 = (f32[128,128]{1,0:T(8,128)S(1)}, f32[128,128]{1,0:T(8,128)S(1)}, u32[]{:S(2)}, u32[]{:S(2)}) collective-permute-start(f32[128,128]{1,0:T(8,128)S(1)} %get-tuple-element.54), channel_id=1, source_target_pairs={{0,8},{2,10},{4,12},{6,14},{8,0},{10,2},{12,4},{14,6},{16,24},{18,... | collective-permute-start | bytes 196616 | tf_op jit(solution)/shard_map/ppermute | solution.py:286
  66.2 3.1 %shard_map.106 = (bf16[1024,128]{1,0:T(8,128)(2,1)S(1)}, f32[1024,128]{1,0:T(8,128)S(1)}) custom-call(s32[4]{0:T(128)S(1)} %pad_add_fusion.place_ref, bf16[256,2048]{1,0:T(8,128)(2,1)S(1)} %copy-done, bf16[512,1024]{1,0:T(8,128)(2,1)} %constant_dynamic-update-slice_fusion.first_ref.refs_2_, bf16[512,1024]{1,0:T(8,128)(2,1)} %collective-permute-done.4.first_other.refs_3_, ...), custom_call_target="tpu_custom_call" | custom-call | flops 536870912 | bytes 4456464 | tf_op jit(solution)/shard_map/pallas_call | solution.py:39
  69.4 5.4 %collective-permute-start.24 = (f32[128,128]{1,0:T(8,128)S(1)}, f32[128,128]{1,0:T(8,128)S(1)}, u32[]{:S(2)}, u32[]{:S(2)}) collective-permute-start(f32[128,128]{1,0:T(8,128)S(1)} %add.29), channel_id=1, source_target_pairs={{0,16},{2,18},{4,20},{6,22},{8,24},{10,26},{12,28},{14,30},{1,17},... | collective-permute-start | bytes 196616 | tf_op jit(solution)/shard_map/ppermute | solution.py:291
  74.9 3.2 %shard_map.111 = (f32[1024,128]{1,0:T(8,128)S(1)}, f32[1024,128]{1,0:T(8,128)S(1)}) custom-call(f32[1024,384]{1,0:T(8,128)S(1)} %get-tuple-element.39.all_ref.refs_6_, f32[1024,128]{1,0:T(8,128)S(1)} %get-tuple-element.55.keys_ref, f32[512,128]{1,0:T(8,128)S(1)} %get-tuple-element.56.grad_ref), custom_call_target="tpu_custom_call" | custom-call | flops 805306368 | bytes 2359296 | tf_op jit(solution)/shard_map/pallas_call | solution.py:39
  78.2 2.0 %collective-permute-start.14 = (bf16[512,128]{1,0:T(8,128)(2,1)S(1)}, bf16[512,128]{1,0:T(8,128)(2,1)S(1)}, u32[]{:S(2)}, u32[]{:S(2)}) collective-permute-start(bf16[512,128]{1,0:T(8,128)(2,1)S(1)} %get-tuple-element.72), channel_id=1, source_target_pairs={{0,16},{2,18},{4,20},{6,22},{8,24},{10,26},{12,28},{14,30},{16,0},... | collective-permute-start | bytes 393224 | tf_op jit(solution)/shard_map/ppermute | solution.py:286
  89.4 1.7 %shard_map.113 = (f32[256,128]{1,0:T(8,128)}, f32[256,128]{1,0:T(8,128)}, f32[256,2]{1,0:T(8,128)S(1)}) custom-call(s32[4]{0:T(128)S(1)} %pad_add_fusion.place_ref, f32[256,128]{1,0:T(8,128)S(1)} %copy-done.3, s32[256,2]{1,0:T(8,128)S(1)} %copy.11.routing_ref, f32[256,2]{1,0:T(8,128)S(1)} %copy.12.gates_ref, f32[256,256]{1,0:T(8,128)S(1)} %get-tuple-element.59.own, ...), custom_call_target="tpu_custom_call" | custom-call | bytes 790544 | tf_op jit(solution)/shard_map/pallas_call | solution.py:39
  91.1 3.7 %psum.7 = f32[256,2]{1,0:T(8,128)S(1)} all-reduce(f32[256,2]{1,0:T(8,128)S(1)} %get-tuple-element.65), channel_id=1, replica_groups=mesh['ctx'=16,'head'=2] {'head'}, use_global_device_ids=true, to_apply=%region_0.1 | all-reduce | flops 512 | bytes 4096 | tf_op jit(solution)/shard_map/psum | solution.py:433
  (96 shorter events, 33.4 us)
Async XLA Ops:
  1.8 18.0 %collective-permute-start = (bf16[128,1024]{1,0:T(8,128)(2,1)S(1)}, bf16[128,1024]{1,0:T(8,128)(2,1)}, u32[]{:S(2)}, u32[]{:S(2)}) collective-permute-start(bf16[128,1024]{1,0:T(8,128)(2,1)S(1)} %get-tuple-element.71), channel_id=1, source_target_pairs={{0,2},{2,0},{4,6},{6,4},{8,10},{10,8},{12,14},{14,12},{16,18},{18,... | collective-permute-start | bytes 786440 | tf_op jit(solution)/shard_map/ppermute | solution.py:286
  4.8 20.1 %collective-permute-start.2 = (bf16[128,1024]{1,0:T(8,128)(2,1)S(1)}, bf16[128,1024]{1,0:T(8,128)(2,1)}, u32[]{:S(2)}, u32[]{:S(2)}) collective-permute-start(bf16[128,1024]{1,0:T(8,128)(2,1)S(1)} %get-tuple-element.71), channel_id=1, source_target_pairs={{0,4},{2,6},{4,0},{6,2},{8,12},{10,14},{12,8},{14,10},{16,20},{18,... | collective-permute-start | bytes 786440 | tf_op jit(solution)/shard_map/ppermute | solution.py:286
  6.4 16.7 %collective-permute-start.1 = (bf16[128,1024]{1,0:T(8,128)(2,1)S(1)}, bf16[128,1024]{1,0:T(8,128)(2,1)}, u32[]{:S(2)}, u32[]{:S(2)}) collective-permute-start(bf16[128,1024]{1,0:T(8,128)(2,1)S(1)} %get-tuple-element.70), channel_id=1, source_target_pairs={{0,2},{2,0},{4,6},{6,4},{8,10},{10,8},{12,14},{14,12},{16,18},{18,... | collective-permute-start | bytes 786440 | tf_op jit(solution)/shard_map/ppermute | solution.py:286
  6.9 21.5 %collective-permute-start.3 = (bf16[128,1024]{1,0:T(8,128)(2,1)S(1)}, bf16[128,1024]{1,0:T(8,128)(2,1)}, u32[]{:S(2)}, u32[]{:S(2)}) collective-permute-start(bf16[128,1024]{1,0:T(8,128)(2,1)S(1)} %get-tuple-element.70), channel_id=1, source_target_pairs={{0,4},{2,6},{4,0},{6,2},{8,12},{10,14},{12,8},{14,10},{16,20},{18,... | collective-permute-start | bytes 786440 | tf_op jit(solution)/shard_map/ppermute | solution.py:286
  8.5 8.9 %collective-permute-start.18 = (bf16[128,128]{1,0:T(8,128)(2,1)S(1)}, bf16[128,128]{1,0:T(8,128)(2,1)S(1)}, u32[]{:S(2)}, u32[]{:S(2)}) collective-permute-start(bf16[128,128]{1,0:T(8,128)(2,1)S(1)} %get-tuple-element.50), channel_id=1, source_target_pairs={{0,2},{2,0},{4,6},{6,4},{8,10},{10,8},{12,14},{14,12},{16,18},{18,... | collective-permute-start | bytes 98312 | tf_op jit(solution)/shard_map/ppermute | solution.py:286
  17.5 26.5 %collective-permute-start.8 = (f16[272,384]{1,0:T(8,128)(2,1)S(1)}, f16[272,384]{1,0:T(8,128)(2,1)S(1)}, u32[]{:S(2)}, u32[]{:S(2)}) collective-permute-start(f16[272,384]{1,0:T(8,128)(2,1)S(1)} %convert_element_type.27), channel_id=1, source_target_pairs={{0,2},{2,0},{4,6},{6,4},{8,10},{10,8},{12,14},{14,12},{16,18},{18,... | collective-permute-start | bytes 626696 | tf_op jit(solution)/shard_map/ppermute | solution.py:286
  19.8 10.2 %collective-permute-start.19 = (bf16[128,128]{1,0:T(8,128)(2,1)S(1)}, bf16[128,128]{1,0:T(8,128)(2,1)S(1)}, u32[]{:S(2)}, u32[]{:S(2)}) collective-permute-start(bf16[128,128]{1,0:T(8,128)(2,1)S(1)} %get-tuple-element.51), channel_id=1, source_target_pairs={{0,4},{2,6},{4,0},{6,2},{8,12},{10,14},{12,8},{14,10},{16,20},{18,... | collective-permute-start | bytes 98312 | tf_op jit(solution)/shard_map/ppermute | solution.py:286
  23.0 9.1 %collective-permute-start.20 = (bf16[128,128]{1,0:T(8,128)(2,1)S(1)}, bf16[128,128]{1,0:T(8,128)(2,1)S(1)}, u32[]{:S(2)}, u32[]{:S(2)}) collective-permute-start(bf16[128,128]{1,0:T(8,128)(2,1)S(1)} %get-tuple-element.52), channel_id=1, source_target_pairs={{0,6},{2,4},{4,2},{6,0},{8,14},{10,12},{12,10},{14,8},{16,22},{18,... | collective-permute-start | bytes 98312 | tf_op jit(solution)/shard_map/ppermute | solution.py:286
  24.9 7.7 %collective-permute-start.5 = (bf16[128,1024]{1,0:T(8,128)(2,1)}, bf16[128,1024]{1,0:T(8,128)(2,1)S(1)}, u32[]{:S(2)}, u32[]{:S(2)}) collective-permute-start(bf16[128,1024]{1,0:T(8,128)(2,1)} %collective-permute-done), channel_id=1, source_target_pairs={{0,4},{2,6},{4,0},{6,2},{8,12},{10,14},{12,8},{14,10},{16,20},{18,... | collective-permute-start | bytes 786440 | tf_op jit(solution)/shard_map/ppermute | solution.py:286
  30.0 29.0 %collective-permute-start.4 = (bf16[512,1024]{1,0:T(8,128)(2,1)}, bf16[512,1024]{1,0:T(8,128)(2,1)}, u32[]{:S(2)}, u32[]{:S(2)}) collective-permute-start(bf16[512,1024]{1,0:T(8,128)(2,1)} %constant_dynamic-update-slice_fusion.first_ref.refs_2_), channel_id=1, source_target_pairs={{0,1},{1,0},{2,3},{3,2},{4,5},{5,4},{6,7},{7,6},{8,9},{9,8},{10,11... | collective-permute-start | bytes 3145736 | tf_op jit(solution)/shard_map/ppermute | solution.py:295
  30.0 8.9 %collective-permute-start.6 = (bf16[128,1024]{1,0:T(8,128)(2,1)}, bf16[128,1024]{1,0:T(8,128)(2,1)S(1)}, u32[]{:S(2)}, u32[]{:S(2)}) collective-permute-start(bf16[128,1024]{1,0:T(8,128)(2,1)} %collective-permute-done.3), channel_id=1, source_target_pairs={{0,2},{2,0},{4,6},{6,4},{8,10},{10,8},{12,14},{14,12},{16,18},{18,... | collective-permute-start | bytes 786440 | tf_op jit(solution)/shard_map/ppermute | solution.py:286
  32.1 12.5 %collective-permute-start.9 = (f16[272,384]{1,0:T(8,128)(2,1)S(1)}, f16[272,384]{1,0:T(8,128)(2,1)S(1)}, u32[]{:S(2)}, u32[]{:S(2)}) collective-permute-start(f16[272,384]{1,0:T(8,128)(2,1)S(1)} %convert_element_type.29), channel_id=1, source_target_pairs={{0,4},{2,6},{4,0},{6,2},{8,12},{10,14},{12,8},{14,10},{16,20},{18,... | collective-permute-start | bytes 626696 | tf_op jit(solution)/shard_map/ppermute | solution.py:286
  32.7 9.1 %collective-permute-start.21 = (bf16[512,128]{1,0:T(8,128)(2,1)S(1)}, bf16[512,128]{1,0:T(8,128)(2,1)S(1)}, u32[]{:S(2)}, u32[]{:S(2)}) collective-permute-start(bf16[512,128]{1,0:T(8,128)(2,1)S(1)} %pad_maximum_fusion), channel_id=1, source_target_pairs={{0,16},{2,18},{4,20},{6,22},{8,24},{10,26},{12,28},{14,30},{16,0},... | collective-permute-start | bytes 393224 | tf_op jit(solution)/shard_map/ppermute | solution.py:286
  39.0 20.1 %collective-permute-start.7 = (bf16[256,1024]{1,0:T(8,128)(2,1)S(1)}, bf16[256,1024]{1,0:T(8,128)(2,1)}, u32[]{:S(2)}, u32[]{:S(2)}) collective-permute-start(bf16[256,1024]{1,0:T(8,128)(2,1)S(1)} %constant_dynamic-update-slice_fusion.4.last_ref.refs_4_), channel_id=1, source_target_pairs={{0,1},{1,0},{2,3},{3,2},{4,5},{5,4},{6,7},{7,6},{8,9},{9,8},{10,11... | collective-permute-start | bytes 1572872 | tf_op jit(solution)/shard_map/ppermute | solution.py:295
  41.8 7.1 %collective-permute-start.10 = (f16[272,384]{1,0:T(8,128)(2,1)S(1)}, f16[272,384]{1,0:T(8,128)(2,1)S(1)}, u32[]{:S(2)}, u32[]{:S(2)}) collective-permute-start(f16[272,384]{1,0:T(8,128)(2,1)S(1)} %convert_element_type.31), channel_id=1, source_target_pairs={{0,6},{2,4},{4,2},{6,0},{8,14},{10,12},{12,10},{14,8},{16,22},{18,... | collective-permute-start | bytes 626696 | tf_op jit(solution)/shard_map/ppermute | solution.py:286
  44.0 14.1 %collective-permute-start.22 = (bf16[1024,128]{1,0:T(8,128)(2,1)}, bf16[1024,128]{1,0:T(8,128)(2,1)}, u32[]{:S(2)}, u32[]{:S(2)}) collective-permute-start(bf16[1024,128]{1,0:T(8,128)(2,1)} %get-tuple-element.74), channel_id=1, source_target_pairs={{0,8},{2,10},{4,12},{6,14},{8,0},{10,2},{12,4},{14,6},{16,24},{18,... | collective-permute-start | bytes 786440 | tf_op jit(solution)/shard_map/ppermute | solution.py:286
  56.7 8.2 %collective-permute-start.12 = (f32[128,128]{1,0:T(8,128)S(1)}, f32[128,128]{1,0:T(8,128)S(1)}, u32[]{:S(2)}, u32[]{:S(2)}) collective-permute-start(f32[128,128]{1,0:T(8,128)S(1)} %add.25), channel_id=1, source_target_pairs={{16,0},{18,2},{20,4},{22,6},{24,8},{26,10},{28,12},{30,14},{17,1},... | collective-permute-start | bytes 196616 | tf_op jit(solution)/shard_map/ppermute | solution.py:291
  69.3 8.8 %collective-permute-start.13 = (bf16[1024,128]{1,0:T(8,128)(2,1)S(1)}, bf16[1024,128]{1,0:T(8,128)(2,1)S(1)}, u32[]{:S(2)}, u32[]{:S(2)}) collective-permute-start(bf16[1024,128]{1,0:T(8,128)(2,1)S(1)} %get-tuple-element.44), channel_id=1, source_target_pairs={{0,8},{2,10},{4,12},{6,14},{8,0},{10,2},{12,4},{14,6},{16,24},{18,... | collective-permute-start | bytes 786440 | tf_op jit(solution)/shard_map/ppermute | solution.py:286
  69.4 8.6 %collective-permute-start.24 = (f32[128,128]{1,0:T(8,128)S(1)}, f32[128,128]{1,0:T(8,128)S(1)}, u32[]{:S(2)}, u32[]{:S(2)}) collective-permute-start(f32[128,128]{1,0:T(8,128)S(1)} %add.29), channel_id=1, source_target_pairs={{0,16},{2,18},{4,20},{6,22},{8,24},{10,26},{12,28},{14,30},{1,17},... | collective-permute-start | bytes 196616 | tf_op jit(solution)/shard_map/ppermute | solution.py:291
  81.4 6.9 %collective-permute-start.26 = (bf16[256,256]{1,0:T(8,128)(2,1)S(1)}, bf16[256,256]{1,0:T(8,128)(2,1)S(1)}, u32[]{:S(2)}, u32[]{:S(2)}) collective-permute-start(bf16[256,256]{1,0:T(8,128)(2,1)S(1)} %get-tuple-element.61), channel_id=1, source_target_pairs={{0,4},{2,6},{4,0},{6,2},{8,12},{10,14},{12,8},{14,10},{16,20},{18,... | collective-permute-start | bytes 393224 | tf_op jit(solution)/shard_map/ppermute | solution.py:286
  82.7 6.7 %collective-permute-start.27 = (bf16[256,256]{1,0:T(8,128)(2,1)S(1)}, bf16[256,256]{1,0:T(8,128)(2,1)S(1)}, u32[]{:S(2)}, u32[]{:S(2)}) collective-permute-start(bf16[256,256]{1,0:T(8,128)(2,1)S(1)} %get-tuple-element.62), channel_id=1, source_target_pairs={{0,6},{2,4},{4,2},{6,0},{8,14},{10,12},{12,10},{14,8},{16,22},{18,... | collective-permute-start | bytes 393224 | tf_op jit(solution)/shard_map/ppermute | solution.py:286
  84.7 10.8 %collective-permute-start.15 = (f32[128,128]{1,0:T(8,128)S(1)}, f32[128,128]{1,0:T(8,128)S(1)}, u32[]{:S(2)}, u32[]{:S(2)}) collective-permute-start(f32[128,128]{1,0:T(8,128)S(1)} %get-tuple-element.46), channel_id=1, source_target_pairs={{0,2},{2,0},{4,6},{6,4},{8,10},{10,8},{12,14},{14,12},{16,18},{18,... | collective-permute-start | bytes 196616 | tf_op jit(solution)/shard_map/ppermute | solution.py:286
  85.6 9.9 %collective-permute-start.16 = (f32[128,128]{1,0:T(8,128)S(1)}, f32[128,128]{1,0:T(8,128)S(1)}, u32[]{:S(2)}, u32[]{:S(2)}) collective-permute-start(f32[128,128]{1,0:T(8,128)S(1)} %get-tuple-element.47), channel_id=1, source_target_pairs={{0,4},{2,6},{4,0},{6,2},{8,12},{10,14},{12,8},{14,10},{16,20},{18,... | collective-permute-start | bytes 196616 | tf_op jit(solution)/shard_map/ppermute | solution.py:286
  86.9 8.6 %collective-permute-start.17 = (f32[128,128]{1,0:T(8,128)S(1)}, f32[128,128]{1,0:T(8,128)S(1)}, u32[]{:S(2)}, u32[]{:S(2)}) collective-permute-start(f32[128,128]{1,0:T(8,128)S(1)} %get-tuple-element.48), channel_id=1, source_target_pairs={{0,6},{2,4},{4,2},{6,0},{8,14},{10,12},{12,10},{14,8},{16,22},{18,... | collective-permute-start | bytes 196616 | tf_op jit(solution)/shard_map/ppermute | solution.py:286
  (14 other events, 101.9 us)

commit v3 on v2

v3 whole, which is shorter than its diff:
```python
import functools
import math

import jax
import jax.numpy as jnp
from jax import lax
from jax.experimental import pallas as pl
from jax.experimental.pallas import tpu as pltpu
from jax.sharding import PartitionSpec as P

F32 = jnp.float32
BF16 = jnp.bfloat16
F16 = jnp.float16
GROUP = 4
TAIL = 16


def split(x):
    high = x.astype(BF16)
    return high, (x - high.astype(F32)).astype(BF16)


def dot3(a, b, b_last=False):
    dims = (((1,), (1 if b_last else 0,)), ((), ()))

    def one(x, y):
        return lax.dot_general(x, y, dims, preferred_element_type=F32)

    return one(a[0], b[0]) + (one(a[0], b[1]) + one(a[1], b[0]))


def part(x, k, width):
    return x[:, k * width : (k + 1) * width]


def call(body, outs, *args, scratch=(), spaces=None, flops=0, room=20):
    vmem = pl.BlockSpec(memory_space=pltpu.VMEM)
    size = sum(a.size * a.dtype.itemsize for a in args)
    return pl.pallas_call(
        body,
        out_shape=outs,
        in_specs=[vmem] * len(args) if spaces is None else spaces,
        out_specs=jax.tree.map(lambda _: vmem, outs),
        scratch_shapes=list(scratch),
        cost_estimate=pl.CostEstimate(flops=flops, bytes_accessed=size, transcendentals=0),
        compiler_params=pltpu.CompilerParams(vmem_limit_bytes=room * 1024 * 1024),
    )(*args)


def exponent(x):
    top = jnp.max(jnp.abs(x), axis=(0, 1), keepdims=True)
    return jnp.clip(jnp.ceil(jnp.log(jnp.maximum(top, 1e-30)) * (1.0 / math.log(2.0))), -90.0, 40.0) - 14.0


def power(k):
    return jnp.exp(k * math.log(2.0))


def fetch(refs, rooms, sem):
    copies = [pltpu.make_async_copy(ref, room, sem.at[k]) for k, (ref, room) in enumerate(zip(refs, rooms, strict=True))]
    for copy in copies:
        copy.start()
    for copy in copies:
        copy.wait()


def messages(place_ref, q_at, v_at, dout_at, routing_at, gates_at, own, near, far, both, q_ref, v_ref, dout_ref, routing_ref, gates_ref, sem):
    fetch((q_at, v_at, dout_at, routing_at, gates_at), (q_ref, v_ref, dout_ref, routing_ref, gates_ref), sem)
    count, width = q_ref.shape
    routing, gates = routing_ref[...].T, gates_ref[...].T
    place = place_ref[0]
    q, v, dout = q_ref[...], v_ref[...], dout_ref[...]
    exponents = [exponent(x) for x in (q, v, dout)]
    scales = [1.0 / power(k) for k in exponents]
    for off, ref in enumerate((own, near, far, both)):
        hit = routing == (place ^ off)
        weight = jnp.sum(jnp.where(hit, gates, 0.0), axis=1, keepdims=True)
        routed = jnp.sum(hit.astype(F32), axis=1, keepdims=True)
        for k, x in enumerate((weight * q, routed * v, dout)):
            column = slice(k * width, (k + 1) * width)
            if off:
                ref[:count, column] = x * scales[k]
                ref[count:, column] = jnp.broadcast_to(exponents[k], (TAIL, width))
            else:
                ref[:, column] = x


def group_sums(place, states, sums_ref, total_ref, reverse):
    size = states[0].shape[0]
    for to in range(GROUP):
        total = jnp.zeros_like(states[0])
        for off in range(GROUP):
            counts = (place ^ off) > (place ^ to) if reverse else (place ^ off) < (place ^ to)
            total = total + jnp.where(counts, states[off], 0.0)
        sums_ref[to * size : (to + 1) * size, :] = total
    total_ref[...] = (states[0] + states[1]) + (states[2] + states[3])


def grad_states(scale, place_ref, own, near, far, both, all_ref, sums_ref, total_ref):
    count = own.shape[0]
    width = own.shape[1] // 3
    states = []
    for off, ref in enumerate((own, near, far, both)):
        for k in range(3):
            column = slice(k * width, (k + 1) * width)
            x = ref[:count, column]
            if off:
                x = x * power(ref[count : count + 1, column])
            all_ref[off * count : (off + 1) * count, column] = x
        rows = all_ref[off * count : (off + 1) * count, :]
        states.append(scale * dot3(split(part(rows, 2, width).T), split(part(rows, 0, width))))
    group_sums(place_ref[0], states, sums_ref, total_ref, True)


def inner_key(scale, all_ref, out_ref):
    width = all_ref.shape[1] // 3
    count = all_ref.shape[0] // GROUP
    places = lax.broadcasted_iota(jnp.int32, (count, count), 0)
    others = lax.broadcasted_iota(jnp.int32, (count, count), 1)
    for off in range(GROUP):
        rows = all_ref[off * count : (off + 1) * count, :]
        scores = dot3(split(part(rows, 1, width)), split(part(rows, 2, width)), True)
        scores = jnp.where(others >= places, scores, 0.0)
        out_ref[off * count : (off + 1) * count, :] = scale * dot3(split(scores), split(part(rows, 0, width)))


def key_low(all_ref, sums_ref, before_ref, inner_ref, low_ref, grad_ref):
    width = all_ref.shape[1] // 3
    count = all_ref.shape[0] // GROUP
    for off in range(GROUP):
        grad = sums_ref[off * width : (off + 1) * width, :] + before_ref[...]
        grad_ref[off * width : (off + 1) * width, :] = grad
        span = slice(off * count, (off + 1) * count)
        carried = dot3(split(all_ref[span, width : 2 * width]), split(grad))
        low_ref[span, :] = (carried + inner_ref[span, :]).astype(BF16)


def pack(*refs):
    sources, out_ref, sem = refs[:-2], refs[-2], refs[-1]
    copies, at = [], 0
    for k, ref in enumerate(sources):
        copies.append(pltpu.make_async_copy(ref, out_ref.at[pl.ds(at, ref.shape[0]), :], sem.at[k]))
        at += ref.shape[0]
    for copy in copies:
        copy.start()
    for copy in copies:
        copy.wait()


def row_order(core, count):
    half = count // 2
    found = [(0, 0, count)]
    for whose in (core, 1 - core):
        for block in (1, 2):
            found.append((block, whose * half, half))
    for whose in (core, 1 - core):
        found.append((3, whose * half, half))
    return [
        (pl.multiple_of(block * count + row, size), size) if block else (0, size) for block, row, size in found
    ]


def first_products(place_ref, own, mine, other, low_ref, out_ref, last_low_ref, room):
    at = 0
    for start, size in row_order(place_ref[1], own.shape[0]):
        room[at : at + size, :] = low_ref[pl.ds(start, size), :]
        at += size
    low = room[...].T
    at, total = 0, None
    for ref in (own, mine, other):
        term = jnp.dot(low[:, at : at + ref.shape[0]], ref[...], preferred_element_type=F32)
        total = term if total is None else total + term
        at += ref.shape[0]
    out_ref[...] = total
    last_low_ref[...] = low[:, at:]


def products(steps, place_ref, first_ref, low_ref, last, last_other, *refs):
    outs, turned = refs[:-1], refs[-1]
    half, width = last.shape
    turned[...] = first_ref[...] + (
        jnp.dot(low_ref[:, :half], last[...], preferred_element_type=F32)
        + jnp.dot(low_ref[:, half:], last_other[...], preferred_element_type=F32)
    )
    group = place_ref[2]
    span = width // len(steps)
    for off, ref in zip(steps, outs, strict=True):
        start = pl.multiple_of((group ^ off // GROUP) * span, span)
        ref[...] = turned[:, pl.ds(start, span)].T.astype(ref.dtype)


def first_keys(layout, parts, place_ref, *refs):
    chunks = len(layout)
    own, mine, other, keys_ref, weights = refs[chunks:]
    rows = weights.shape[0] // parts
    here = place_ref[3]
    for ref, offsets in zip(refs[:chunks], layout, strict=True):
        for k, off in enumerate(offsets):
            start = pl.multiple_of((here ^ off) * rows, rows)
            weights[pl.ds(start, rows), :] = ref[k * rows : (k + 1) * rows, :]
    at = 0
    for ref in (own, mine, other):
        keys_ref[at : at + ref.shape[0], :] = jnp.dot(ref[...], weights[...], preferred_element_type=F32)
        at += ref.shape[0]


def key_states(place_ref, first_ref, weights, last, last_other, all_ref, keys_ref, sums_ref, total_ref):
    count = all_ref.shape[0] // GROUP
    half, head_dim = last.shape[0], keys_ref.shape[1]
    at = 0
    order = row_order(place_ref[1], count)
    for start, size in order[:-2]:
        keys_ref[pl.ds(start, size), :] = first_ref[at : at + size, :]
        at += size
    for (start, size), ref in zip(order[-2:], (last, last_other), strict=True):
        keys_ref[pl.ds(start, size), :] = jnp.dot(ref[...], weights[...], preferred_element_type=F32)
    states = []
    for off in range(GROUP):
        span = slice(off * count, (off + 1) * count)
        values = all_ref[span, head_dim : 2 * head_dim]
        states.append(dot3(split(values.T), split(keys_ref[span, :])))
    group_sums(place_ref[0], states, sums_ref, total_ref, False)


def inner_rest(scale, all_ref, keys_ref, grad_ref, value_ref, state_ref):
    width = keys_ref.shape[1]
    count = keys_ref.shape[0] // GROUP
    places = lax.broadcasted_iota(jnp.int32, (count, count), 0)
    others = lax.broadcasted_iota(jnp.int32, (count, count), 1)
    for off in range(GROUP):
        span = slice(off * count, (off + 1) * count)
        rows = all_ref[span, :]
        lifted, values, dout = (split(part(rows, k, width)) for k in range(3))
        keys = split(keys_ref[span, :])
        mixed = jnp.where(others >= places, dot3(keys, lifted, True), 0.0)
        carried = dot3(keys, split(grad_ref[off * width : (off + 1) * width, :]), True)
        value_ref[span, :] = carried + scale * dot3(split(mixed), dout)
        scores = jnp.where(places >= others, dot3(dout, values, True), 0.0)
        state_ref[span, :] = dot3(split(scores), keys)


def results(all_ref, sums_ref, before_ref, state_ref, value_ref, own, near, far, both):
    width = before_ref.shape[1]
    count = state_ref.shape[0] // GROUP
    for off, ref in enumerate((own, near, far, both)):
        span = slice(off * count, (off + 1) * count)
        before = sums_ref[off * width : (off + 1) * width, :] + before_ref[...]
        state = state_ref[span, :] + dot3(split(all_ref[span, 2 * width :]), split(before))
        ref[:, :width] = state.astype(ref.dtype)
        ref[:, width:] = value_ref[span, :].astype(ref.dtype)


def at_home(scale, place_ref, q_ref, routing_ref, gates_ref, own, near, far, both, query_ref, value_ref, gate_ref):
    queries, routing, gates = q_ref[...], routing_ref[...].T, gates_ref[...].T
    width = queries.shape[1]
    query = jnp.zeros_like(queries)
    value = jnp.zeros_like(queries)
    gate = jnp.zeros(gate_ref.shape[::-1], F32)
    for off, ref in enumerate((own, near, far, both)):
        hit = routing == (place_ref[0] ^ off)
        weight = jnp.sum(jnp.where(hit, gates, 0.0), axis=1, keepdims=True)
        routed = jnp.sum(hit.astype(F32), axis=1, keepdims=True)
        state = ref[:, :width].astype(F32)
        query = query + weight * state
        value = value + routed * ref[:, width:].astype(F32)
        gate = gate + jnp.where(hit, jnp.sum(queries * state, axis=1, keepdims=True), 0.0)
    query_ref[...] = scale * query
    value_ref[...] = value
    gate_ref[...] = (scale * gate).T


def by_column(place_ref, x_ref, own, near, far, both):
    size = own.shape[1]
    for off, ref in enumerate((own, near, far, both)):
        ref[...] = x_ref[:, pl.ds(pl.multiple_of((place_ref[0] ^ off) * size, size), size)]


def by_row(place_ref, *refs):
    parts, (own, near, far, both, room) = refs[:-5], refs[-5:]
    size = own.shape[0]
    total = parts[0][...]
    for ref in parts[1:]:
        total = total + ref[...].astype(F32)
    room[...] = total
    for off, ref in enumerate((own, near, far, both)):
        ref[...] = room[pl.ds(pl.multiple_of((place_ref[0] ^ off) * size, size), size), :]


def in_columns(place_ref, own, near, far, both, out_ref):
    size = own.shape[1]
    for off, ref in enumerate((own, near, far, both)):
        out_ref[:, pl.ds(pl.multiple_of((place_ref[0] ^ off) * size, size), size)] = ref[...]


def after(x, *others):
    return lax.optimization_barrier((x, *others))[0]


def swap(x, off, parts):
    return lax.ppermute(x, "ctx", [(i, i ^ off) for i in range(parts)])


def other_core(x):
    return lax.ppermute(x, "head", [(i, i ^ 1) for i in range(lax.axis_size("head"))])


def from_groups(total, steps, parts):
    return [swap(total, off, parts) for off in steps[1:]]


def prefix(total, got, steps, here, reverse):
    before = jnp.zeros_like(total)
    for off, x in zip(steps[1:], got, strict=True):
        other = here ^ off
        before = before + jnp.where(other > here if reverse else other < here, x, 0.0)
    return before


def over_heads(x):
    count = lax.axis_size("head")
    bit = 1
    while bit < count:
        x = x + lax.ppermute(x, "head", [(i, i ^ bit) for i in range(count)])
        bit *= 2
    return x


def on_device(tokens, queries, values, dout, key_weight, routing, gates):
    count, width = tokens.shape
    rows, memories, head_dim = key_weight.shape
    parts = lax.axis_size("ctx")
    steps = list(range(0, parts, GROUP))
    here = lax.axis_index("ctx").astype(jnp.int32)
    core = lax.axis_index("head").astype(jnp.int32) & 1
    at = jnp.stack([here & (GROUP - 1), core, here // GROUP, here])
    scale = 1.0 / math.sqrt(head_dim * count * parts)
    tall = GROUP * count
    smem = pl.BlockSpec(memory_space=pltpu.SMEM)
    vmem = pl.BlockSpec(memory_space=pltpu.VMEM)
    anywhere = pl.BlockSpec(memory_space=pl.ANY)

    def shape(r, c, dtype=F32):
        return jax.ShapeDtypeStruct((r, c), dtype)

    def stack(*blocks):
        size = sum(x.shape[0] for x in blocks)
        return call(
            pack,
            shape(size, blocks[0].shape[1], blocks[0].dtype),
            *blocks,
            spaces=[anywhere] * len(blocks),
            scratch=[pltpu.SemaphoreType.DMA((len(blocks),))],
        )

    half = lax.dynamic_slice(tokens, (core * (count // 2), jnp.int32(0)), (count // 2, width))
    from_x, from_y = swap(half, 1, parts), swap(half, 2, parts)

    mine = call(
        by_column,
        [shape(rows, head_dim, BF16)] * 4,
        at, key_weight.reshape(rows, memories * head_dim),
        spaces=[smem, vmem],
    )
    weights = [mine[0]] + [swap(mine[off], off, parts) for off in (1, 2, 3)]

    sent = call(
        messages,
        [shape(count, 3 * head_dim)] + [shape(count + TAIL, 3 * head_dim)] * 3,
        at, queries, values, dout, routing.T, gates.T,
        spaces=[smem] + [anywhere] * 5,
        scratch=[pltpu.VMEM((count, head_dim), F32)] * 3
        + [pltpu.VMEM(x.shape[::-1], x.dtype) for x in (routing, gates)]
        + [pltpu.SemaphoreType.DMA((5,))],
    )
    coded = [x.astype(F16) for x in sent[1:]]
    got = [swap(x, off, parts).astype(F32) for off, x in zip((1, 2, 3), coded)]

    neighbours = stack(after(from_x, *coded, *weights), from_y)
    neighbours_other = other_core(neighbours)

    block = stack(after(weights[0], *coded), *weights[1:])
    chunks, layout, held = [block], [list(range(GROUP))], list(range(GROUP))
    bit = parts // 2
    while bit >= GROUP:
        other = swap(block, bit, parts)
        chunks.append(other)
        layout.append([off ^ bit for off in held])
        held = held + layout[-1]
        if bit > GROUP:
            block = stack(block, after(other, neighbours_other))
        bit //= 2

    last_a = swap(after(from_x, neighbours_other, *got)[: count // 4], 2, parts)
    last_b = swap(after(from_y, neighbours_other, *got)[count // 4 :], 1, parts)

    every, grad_sums, total = call(
        functools.partial(grad_states, scale),
        [shape(tall, 3 * head_dim), shape(GROUP * head_dim, head_dim), shape(head_dim, head_dim)],
        at, after(sent[0], neighbours_other), *got,
        spaces=[smem] + [vmem] * 4,
        flops=6 * tall * head_dim * head_dim,
    )
    totals = from_groups(total, steps, parts)
    before = prefix(total, totals, steps, here, True)
    inner_k = call(
        functools.partial(inner_key, scale),
        shape(tall, head_dim),
        every,
        flops=12 * tall * count * head_dim,
    )
    low, grad_in = call(
        key_low,
        [shape(tall, head_dim, BF16), shape(GROUP * head_dim, head_dim)],
        every, grad_sums, before, inner_k,
        flops=6 * tall * head_dim * head_dim,
    )

    first, weights = call(
        functools.partial(first_keys, layout, parts),
        [shape(3 * count, head_dim), shape(width, head_dim, BF16)],
        at, *chunks, tokens, neighbours, neighbours_other,
        spaces=[smem] + [vmem] * (3 + len(chunks)),
        flops=2 * tall * width * head_dim,
    )
    product, last_low = call(
        first_products,
        [shape(head_dim, width), shape(head_dim, count, BF16)],
        at, tokens, neighbours, neighbours_other, low,
        spaces=[smem] + [vmem] * 4,
        scratch=[pltpu.VMEM((tall, head_dim), BF16)],
        flops=2 * tall * width * head_dim,
    )
    last = stack(after(last_a, first, *totals), last_b)
    last_other = other_core(last)

    keys, sums, key_total = call(
        key_states,
        [shape(tall, head_dim), shape(GROUP * head_dim, head_dim), shape(head_dim, head_dim)],
        at, first, weights, last, last_other, every,
        spaces=[smem] + [vmem] * 5,
        flops=2 * count * width * head_dim,
    )
    key_totals = from_groups(key_total, steps, parts)

    span = width // len(steps)
    sent = call(
        functools.partial(products, steps),
        [shape(span, head_dim)] + [shape(span, head_dim, BF16)] * (len(steps) - 1),
        at, product, after(last_low, key_total), last, last_other,
        spaces=[smem] + [vmem] * 4,
        scratch=[pltpu.VMEM((head_dim, width), F32)],
        flops=2 * count * width * head_dim,
    )
    parts_of_sum = [sent[0]] + [swap(x, off, parts) for off, x in zip(steps[1:], sent[1:], strict=True)]
    inner_v, inner_state = call(
        functools.partial(inner_rest, scale),
        [shape(tall, head_dim)] * 2,
        every, after(keys, sent[0]), grad_in,
        flops=24 * tall * count * head_dim,
    )

    mine = call(
        by_row,
        [shape(rows, head_dim)] * 4,
        at, *parts_of_sum,
        spaces=[smem] + [vmem] * len(steps),
        scratch=[pltpu.VMEM((GROUP * rows, head_dim), F32)],
    )
    others = [swap(mine[off], off, parts) for off in (1, 2, 3)]

    before = prefix(key_total, key_totals, steps, here, False)
    sent = call(
        results,
        [shape(count, 2 * head_dim)] + [shape(count, 2 * head_dim, BF16)] * 3,
        every, sums, before, inner_state, inner_v,
        flops=6 * tall * head_dim * head_dim,
    )
    query_grad, value_grad, gate_part = call(
        functools.partial(at_home, scale),
        [shape(count, head_dim), shape(count, head_dim), shape(routing.shape[1], count)],
        at, queries, routing.T, gates.T, sent[0], *[swap(sent[off], off, parts) for off in (1, 2, 3)],
        spaces=[smem] + [vmem] * 7,
    )
    gate_grad = over_heads(after(gate_part, *mine)).T
    key_grad = call(
        in_columns,
        shape(rows, memories * head_dim),
        at, mine[0], *others,
        spaces=[smem] + [vmem] * 4,
    ).reshape(rows, memories, head_dim)
    return (key_grad, query_grad, value_grad, gate_grad)


def solution(mesh):
    return jax.shard_map(
        on_device,
        mesh=mesh,
        in_specs=(
            P("ctx", None),
            P("ctx", "head"),
            P("ctx", "head"),
            P("ctx", "head"),
            P("ctx", None, "head"),
            P("ctx", None),
            P("ctx", None),
        ),
        out_specs=(P("ctx", None, "head"), P("ctx", "head"), P("ctx", "head"), P("ctx", None)),
        check_vma=False,
    )
```

time: 97.4 us -> 85.2 us (0.87)
  local copies, waits for them, and re-layouts: 15.3 us -> 8.43 us
  blocking collectives: 3.73 us -> 0 us
  other arithmetic: 2.08 us -> 0.87 us
    ppermute x2 -> x1, starting transfers between devices: 6.74 us -> 0.01 us  [over_heads(): x = x + lax.ppermute(x, 'head', [(i, i ^ bit) for i in range(count)])]
    ppermute x24 -> x27, starting transfers between devices: 31.6 us -> 38.2 us  [swap(): return lax.ppermute(x, 'ctx', [(i, i ^ off) for i in range(parts)])]
    unnamed x32 -> x43, local copies, waits for them, and re-layouts: 10.1 us -> 5.65 us
    psum x1 -> x0, blocking collectives: 3.73 us -> none  [on_device(): gate_grad = lax.psum(gate_part, 'head')]
    concatenate x4 -> x0, local copies, waits for them, and re-layouts: 3.34 us -> none  [the longest x1 1.66 us: on_device(): first = jnp.concatenate([left_x, right_x, left_y, right_y], axis=0)]
    dynamic_slice x0 -> x1, local copies, waits for them, and re-layouts: none -> 1.95 us  [on_device(): lax.dynamic_slice(tokens, (core * (count // 2), jnp.int32(0)), (count //...]
    add x4 -> x2, other arithmetic: 1.76 us -> 0.04 us  [prefix(): before + jnp.where(other > here if reverse else other < here, x, 0.0)]
    slice x1 -> x2, local copies, waits for them, and re-layouts: 1.14 us -> 0.04 us  [the longest x1 0.02 us: on_device(): last_a = swap(after(from_x, neighbours_other, *got)[:count // 4], 2, parts)]
  transfers between devices with their start and end apart: 28 -> 30, of which waited for: 6 -> 7; matrix products, arithmetic and copies ran while one was open for 15% -> 2% of each run, Pallas kernels for 19% -> 19%
where the time goes in v3:
time: 85.2 us; the launch traced here: 84.9 us
  starting transfers between devices  38.4 us (45%)
  Pallas kernels  18.5 us (22%)
  waiting for transfers between devices  17.5 us (21%)
  local copies, waits for them, and re-layouts  8.43 us (10%)
  between operations  1.11 us (1%)
  other arithmetic  0.87 us (1%)
    ppermute x27, starting transfers between devices, swap(): return lax.ppermute(x, 'ctx', [(i, i ^ off) for i in range(parts)])  38.2 us
    pallas_call x18, Pallas kernels, call(): pl.pallas_call(body, out_shape=outs, in_specs=[vmem] * len(args) if space...  18.5 us
    ppermute x27, waiting for transfers between devices, swap(): return lax.ppermute(x, 'ctx', [(i, i ^ off) for i in range(parts)])  17.5 us
    unnamed x43, local copies, waits for them, and re-layouts  5.65 us
    dynamic_slice x1, local copies, waits for them, and re-layouts, on_device(): lax.dynamic_slice(tokens, (core * (count // 2), jnp.int32(0)), (count //...  1.95 us
  transfers between devices with their start and end apart: 30, of which 7 were waited for; matrix products, arithmetic and copies ran while one was open for 2% of the time, Pallas kernels for 19%

profile of v3, /device:TPU:0, one launch (start us, length us, event | category | flops | bytes accessed | tf_op | source)
XLA Modules:
  0.0 84.9 jit_solution(18444669110547365412)
XLA Ops:
  0.7 2.0 %constant_dynamic-slice_fusion = bf16[128,2048]{1,0:T(8,128)(2,1)} fusion(bf16[256,2048]{1,0:T(8,128)(2,1)} %refs_3_.1, s32[]{:T(128)S(6)} %select_n.47), kind=kLoop, calls=%fused_computation.5 | loop fusion | bytes 1048580 | tf_op jit(solution)/shard_map/dynamic_slice | solution.py:355
  2.6 2.9 %collective-permute-start = (bf16[128,2048]{1,0:T(8,128)(2,1)}, bf16[128,2048]{1,0:T(8,128)(2,1)S(1)}, u32[]{:S(2)}, u32[]{:S(2)}) collective-permute-start(bf16[128,2048]{1,0:T(8,128)(2,1)} %constant_dynamic-slice_fusion), channel_id=1, source_target_pairs={{0,2},{2,0},{4,6},{6,4},{8,10},{10,8},{12,14},{14,12},{16,18},{18,... | collective-permute-start | bytes 1572872 | tf_op jit(solution)/shard_map/ppermute | solution.py:300
  5.6 1.5 %collective-permute-start.4 = (bf16[128,2048]{1,0:T(8,128)(2,1)}, bf16[128,2048]{1,0:T(8,128)(2,1)S(1)}, u32[]{:S(2)}, u32[]{:S(2)}) collective-permute-start(bf16[128,2048]{1,0:T(8,128)(2,1)} %constant_dynamic-slice_fusion), channel_id=1, source_target_pairs={{0,4},{2,6},{4,0},{6,2},{8,12},{10,14},{12,8},{14,10},{16,20},{18,... | collective-permute-start | bytes 1572872 | tf_op jit(solution)/shard_map/ppermute | solution.py:300
  9.3 2.9 %collective-permute-start.3 = (bf16[128,128]{1,0:T(8,128)(2,1)S(1)}, bf16[128,128]{1,0:T(8,128)(2,1)S(1)}, u32[]{:S(2)}, u32[]{:S(2)}) collective-permute-start(bf16[128,128]{1,0:T(8,128)(2,1)S(1)} %get-tuple-element.57), channel_id=1, source_target_pairs={{0,6},{2,4},{4,2},{6,0},{8,14},{10,12},{12,10},{14,8},{16,22},{18,... | collective-permute-start | bytes 98312 | tf_op jit(solution)/shard_map/ppermute | solution.py:300
  13.6 1.6 %shard_map.102 = (f32[256,384]{1,0:T(8,128)S(1)}, f32[272,384]{1,0:T(8,128)S(1)}, f32[272,384]{1,0:T(8,128)S(1)}, f32[272,384]{1,0:T(8,128)S(1)}) custom-call(s32[4]{0:T(128)S(1)} %pad_add_fusion.place_ref, f32[256,128]{1,0:T(8,128)S(1)} %copy-done.4, f32[256,128]{1,0:T(8,128)S(1)} %copy-done.9, f32[256,128]{1,0:T(8,128)S(1)} %copy-done.10, ...), custom_call_target="tpu_custom_call" | custom-call | bytes 397328 | tf_op jit(solution)/shard_map/pallas_call | solution.py:39
  15.3 3.4 %collective-permute-done.1.refs_1_ = bf16[128,128]{1,0:T(8,128)(2,1)S(1)} collective-permute-done((bf16[128,128]{1,0:T(8,128)(2,1)S(1)}, bf16[128,128]{1,0:T(8,128)(2,1)S(1)}, u32[]{:S(2)}, u32[]{:S(2)}) %collective-permute-start.1) | collective-permute-done | bytes 32800 | tf_op jit(solution)/shard_map/ppermute | solution.py:300
  18.7 1.8 %collective-permute-done.2.refs_2_ = bf16[128,128]{1,0:T(8,128)(2,1)S(1)} collective-permute-done((bf16[128,128]{1,0:T(8,128)(2,1)S(1)}, bf16[128,128]{1,0:T(8,128)(2,1)S(1)}, u32[]{:S(2)}, u32[]{:S(2)}) %collective-permute-start.2) | collective-permute-done | bytes 32800 | tf_op jit(solution)/shard_map/ppermute | solution.py:300
  20.7 1.6 %collective-permute-start.8 = (f16[272,384]{1,0:T(8,128)(2,1)S(1)}, f16[272,384]{1,0:T(8,128)(2,1)S(1)}, u32[]{:S(2)}, u32[]{:S(2)}) collective-permute-start(f16[272,384]{1,0:T(8,128)(2,1)S(1)} %convert_element_type.20), channel_id=1, source_target_pairs={{0,6},{2,4},{4,2},{6,0},{8,14},{10,12},{12,10},{14,8},{16,22},{18,... | collective-permute-start | bytes 626696 | tf_op jit(solution)/shard_map/ppermute | solution.py:300
  24.5 2.7 %collective-permute-start.12 = (bf16[512,128]{1,0:T(8,128)(2,1)S(1)}, bf16[512,128]{1,0:T(8,128)(2,1)S(1)}, u32[]{:S(2)}, u32[]{:S(2)}) collective-permute-start(bf16[512,128]{1,0:T(8,128)(2,1)S(1)} %shard_map.109.refs_0_), channel_id=1, source_target_pairs={{0,16},{2,18},{4,20},{6,22},{8,24},{10,26},{12,28},{14,30},{16,0},... | collective-permute-start | bytes 393224 | tf_op jit(solution)/shard_map/ppermute | solution.py:300
  27.1 6.1 %collective-permute-done.12.refs_1_ = bf16[512,128]{1,0:T(8,128)(2,1)S(1)} collective-permute-done((bf16[512,128]{1,0:T(8,128)(2,1)S(1)}, bf16[512,128]{1,0:T(8,128)(2,1)S(1)}, u32[]{:S(2)}, u32[]{:S(2)}) %collective-permute-start.12) | collective-permute-done | bytes 131104 | tf_op jit(solution)/shard_map/ppermute | solution.py:300
  34.5 1.6 %collective-permute-start.14 = (bf16[64,2048]{1,0:T(8,128)(2,1)S(1)}, bf16[64,2048]{1,0:T(8,128)(2,1)S(1)}, u32[]{:S(2)}, u32[]{:S(2)}) collective-permute-start(bf16[64,2048]{1,0:T(8,128)(2,1)S(1)} %slice.6), channel_id=1, source_target_pairs={{0,4},{2,6},{4,0},{6,2},{8,12},{10,14},{12,8},{14,10},{16,20},{18,... | collective-permute-start | bytes 786440 | tf_op jit(solution)/shard_map/ppermute | solution.py:300
  37.8 3.0 %collective-permute-start.11 = (f32[128,128]{1,0:T(8,128)S(1)}, f32[128,128]{1,0:T(8,128)S(1)}, u32[]{:S(2)}, u32[]{:S(2)}) collective-permute-start(f32[128,128]{1,0:T(8,128)S(1)} %get-tuple-element.63), channel_id=1, source_target_pairs={{0,24},{2,26},{4,28},{6,30},{8,16},{10,18},{12,20},{14,22},{16,8},... | collective-permute-start | bytes 196616 | tf_op jit(solution)/shard_map/ppermute | solution.py:300
  42.6 1.6 %shard_map.111 = (f32[768,128]{1,0:T(8,128)S(1)}, bf16[2048,128]{1,0:T(8,128)(2,1)S(1)}) custom-call(s32[4]{0:T(128)S(1)} %pad_add_fusion.place_ref, bf16[512,128]{1,0:T(8,128)(2,1)S(1)} %shard_map.109.refs_0_, bf16[512,128]{1,0:T(8,128)(2,1)S(1)} %collective-permute-done.12.refs_1_, bf16[1024,128]{1,0:T(8,128)(2,1)S(1)} %collective-permute-done.13.refs_2_, ...), custom_call_target="tpu_custom_call" | custom-call | flops 536870912 | bytes 3670032 | tf_op jit(solution)/shard_map/pallas_call | solution.py:39
  45.8 1.9 %collective-permute-done.10 = f32[128,128]{1,0:T(8,128)S(1)} collective-permute-done((f32[128,128]{1,0:T(8,128)S(1)}, f32[128,128]{1,0:T(8,128)S(1)}, u32[]{:S(2)}, u32[]{:S(2)}) %collective-permute-start.10) | collective-permute-done | bytes 65568 | tf_op jit(solution)/shard_map/ppermute | solution.py:300
  52.8 1.9 %shard_map.113 = (f32[1024,128]{1,0:T(8,128)S(1)}, f32[512,128]{1,0:T(8,128)S(1)}, f32[128,128]{1,0:T(8,128)S(1)}) custom-call(s32[4]{0:T(128)S(1)} %pad_add_fusion.place_ref, f32[768,128]{1,0:T(8,128)S(1)} %copy-done.8, bf16[2048,128]{1,0:T(8,128)(2,1)S(1)} %copy-done.6, bf16[128,2048]{1,0:T(8,128)(2,1)S(1)} %shard_map.112.last, ...), custom_call_target="tpu_custom_call" | custom-call | flops 134217728 | bytes 3538960 | tf_op jit(solution)/shard_map/pallas_call | solution.py:39
  54.7 3.2 %collective-permute-start.25 = (f32[128,128]{1,0:T(8,128)S(1)}, f32[128,128]{1,0:T(8,128)S(1)}, u32[]{:S(2)}, u32[]{:S(2)}) collective-permute-start(f32[128,128]{1,0:T(8,128)S(1)} %get-tuple-element.74), channel_id=1, source_target_pairs={{0,24},{2,26},{4,28},{6,30},{8,16},{10,18},{12,20},{14,22},{16,8},... | collective-permute-start | bytes 196616 | tf_op jit(solution)/shard_map/ppermute | solution.py:300
  59.1 1.7 %shard_map.114 = (f32[512,128]{1,0:T(8,128)S(1)}, bf16[512,128]{1,0:T(8,128)(2,1)S(1)}, bf16[512,128]{1,0:T(8,128)(2,1)S(1)}, bf16[512,128]{1,0:T(8,128)(2,1)S(1)}) custom-call(s32[4]{0:T(128)S(1)} %pad_add_fusion.place_ref, f32[128,2048]{1,0:T(8,128)S(1)} %get-tuple-element.65.first_ref, bf16[128,256]{1,0:T(8,128)(2,1)S(1)} %get-tuple-element.75.low_ref, ...), custom_call_target="tpu_custom_call" | custom-call | flops 134217728 | bytes 2162704 | tf_op jit(solution)/shard_map/pallas_call | solution.py:39
  61.7 2.9 %collective-permute-start.18 = (bf16[512,128]{1,0:T(8,128)(2,1)S(1)}, bf16[512,128]{1,0:T(8,128)(2,1)S(1)}, u32[]{:S(2)}, u32[]{:S(2)}) collective-permute-start(bf16[512,128]{1,0:T(8,128)(2,1)S(1)} %get-tuple-element.78), channel_id=1, source_target_pairs={{0,16},{2,18},{4,20},{6,22},{8,24},{10,26},{12,28},{14,30},{16,0},... | collective-permute-start | bytes 393224 | tf_op jit(solution)/shard_map/ppermute | solution.py:300
  64.7 3.2 %shard_map.117 = (f32[1024,128]{1,0:T(8,128)S(1)}, f32[1024,128]{1,0:T(8,128)S(1)}) custom-call(f32[1024,384]{1,0:T(8,128)S(1)} %get-tuple-element.61.all_ref, f32[1024,128]{1,0:T(8,128)S(1)} %get-tuple-element.86.keys_ref, f32[512,128]{1,0:T(8,128)S(1)} %get-tuple-element.87.grad_ref), custom_call_target="tpu_custom_call" | custom-call | flops 805306368 | bytes 2359296 | tf_op jit(solution)/shard_map/pallas_call | solution.py:39
  69.0 1.6 %collective-permute-start.26 = (bf16[256,256]{1,0:T(8,128)(2,1)S(1)}, bf16[256,256]{1,0:T(8,128)(2,1)S(1)}, u32[]{:S(2)}, u32[]{:S(2)}) collective-permute-start(bf16[256,256]{1,0:T(8,128)(2,1)S(1)} %get-tuple-element.91), channel_id=1, source_target_pairs={{0,2},{2,0},{4,6},{6,4},{8,10},{10,8},{12,14},{14,12},{16,18},{18,... | collective-permute-start | bytes 393224 | tf_op jit(solution)/shard_map/ppermute | solution.py:300
  72.6 2.2 %collective-permute-done.19.refs_3_ = bf16[512,128]{1,0:T(8,128)(2,1)S(1)} collective-permute-done((bf16[512,128]{1,0:T(8,128)(2,1)S(1)}, bf16[512,128]{1,0:T(8,128)(2,1)S(1)}, u32[]{:S(2)}, u32[]{:S(2)}) %collective-permute-start.19) | collective-permute-done | bytes 131104 | tf_op jit(solution)/shard_map/ppermute | solution.py:300
  76.3 1.5 %collective-permute-start.21 = (f32[128,128]{1,0:T(8,128)S(1)}, f32[128,128]{1,0:T(8,128)S(1)}, u32[]{:S(2)}, u32[]{:S(2)}) collective-permute-start(f32[128,128]{1,0:T(8,128)S(1)} %get-tuple-element.82), channel_id=1, source_target_pairs={{0,4},{2,6},{4,0},{6,2},{8,12},{10,14},{12,8},{14,10},{16,20},{18,... | collective-permute-start | bytes 196616 | tf_op jit(solution)/shard_map/ppermute | solution.py:300
  79.2 1.8 %shard_map.119 = (f32[256,128]{1,0:T(8,128)}, f32[256,128]{1,0:T(8,128)}, f32[2,256]{1,0:T(2,128)S(1)}) custom-call(s32[4]{0:T(128)S(1)} %pad_add_fusion.place_ref, f32[256,128]{1,0:T(8,128)S(1)} %copy-done.4, s32[2,256]{1,0:T(2,128)S(1)} %bitcast.14, f32[2,256]{1,0:T(2,128)S(1)} %bitcast.16, f32[256,256]{1,0:T(8,128)S(1)} %get-tuple-element.90.own, ...), custom_call_target="tpu_custom_call" | custom-call | bytes 790544 | tf_op jit(solution)/shard_map/pallas_call | solution.py:39
  81.0 2.0 %collective-permute-done.22.both = f32[128,128]{1,0:T(8,128)S(1)} collective-permute-done((f32[128,128]{1,0:T(8,128)S(1)}, f32[128,128]{1,0:T(8,128)S(1)}, u32[]{:S(2)}, u32[]{:S(2)}) %collective-permute-start.22) | collective-permute-done | bytes 65568 | tf_op jit(solution)/shard_map/ppermute | solution.py:300
  (111 shorter events, 27.4 us)
Async XLA Ops:
  2.6 17.9 %collective-permute-start = (bf16[128,2048]{1,0:T(8,128)(2,1)}, bf16[128,2048]{1,0:T(8,128)(2,1)S(1)}, u32[]{:S(2)}, u32[]{:S(2)}) collective-permute-start(bf16[128,2048]{1,0:T(8,128)(2,1)} %constant_dynamic-slice_fusion), channel_id=1, source_target_pairs={{0,2},{2,0},{4,6},{6,4},{8,10},{10,8},{12,14},{14,12},{16,18},{18,... | collective-permute-start | bytes 1572872 | tf_op jit(solution)/shard_map/ppermute | solution.py:300
  5.6 15.0 %collective-permute-start.4 = (bf16[128,2048]{1,0:T(8,128)(2,1)}, bf16[128,2048]{1,0:T(8,128)(2,1)S(1)}, u32[]{:S(2)}, u32[]{:S(2)}) collective-permute-start(bf16[128,2048]{1,0:T(8,128)(2,1)} %constant_dynamic-slice_fusion), channel_id=1, source_target_pairs={{0,4},{2,6},{4,0},{6,2},{8,12},{10,14},{12,8},{14,10},{16,20},{18,... | collective-permute-start | bytes 1572872 | tf_op jit(solution)/shard_map/ppermute | solution.py:300
  8.7 10.1 %collective-permute-start.1 = (bf16[128,128]{1,0:T(8,128)(2,1)S(1)}, bf16[128,128]{1,0:T(8,128)(2,1)S(1)}, u32[]{:S(2)}, u32[]{:S(2)}) collective-permute-start(bf16[128,128]{1,0:T(8,128)(2,1)S(1)} %get-tuple-element.55), channel_id=1, source_target_pairs={{0,2},{2,0},{4,6},{6,4},{8,10},{10,8},{12,14},{14,12},{16,18},{18,... | collective-permute-start | bytes 98312 | tf_op jit(solution)/shard_map/ppermute | solution.py:300
  9.3 11.3 %collective-permute-start.2 = (bf16[128,128]{1,0:T(8,128)(2,1)S(1)}, bf16[128,128]{1,0:T(8,128)(2,1)S(1)}, u32[]{:S(2)}, u32[]{:S(2)}) collective-permute-start(bf16[128,128]{1,0:T(8,128)(2,1)S(1)} %get-tuple-element.56), channel_id=1, source_target_pairs={{0,4},{2,6},{4,0},{6,2},{8,12},{10,14},{12,8},{14,10},{16,20},{18,... | collective-permute-start | bytes 98312 | tf_op jit(solution)/shard_map/ppermute | solution.py:300
  9.3 11.2 %collective-permute-start.3 = (bf16[128,128]{1,0:T(8,128)(2,1)S(1)}, bf16[128,128]{1,0:T(8,128)(2,1)S(1)}, u32[]{:S(2)}, u32[]{:S(2)}) collective-permute-start(bf16[128,128]{1,0:T(8,128)(2,1)S(1)} %get-tuple-element.57), channel_id=1, source_target_pairs={{0,6},{2,4},{4,2},{6,0},{8,14},{10,12},{12,10},{14,8},{16,22},{18,... | collective-permute-start | bytes 98312 | tf_op jit(solution)/shard_map/ppermute | solution.py:300
  20.7 12.6 %collective-permute-start.5 = (bf16[256,2048]{1,0:T(8,128)(2,1)S(1)}, bf16[256,2048]{1,0:T(8,128)(2,1)S(1)}, u32[]{:S(2)}, u32[]{:S(2)}) collective-permute-start(bf16[256,2048]{1,0:T(8,128)(2,1)S(1)} %shard_map.104.mine.refs_4_), channel_id=1, source_target_pairs={{0,1},{1,0},{2,3},{3,2},{4,5},{5,4},{6,7},{7,6},{8,9},{9,8},{10,11... | collective-permute-start | bytes 3145736 | tf_op jit(solution)/shard_map/ppermute | solution.py:304
  20.7 13.6 %collective-permute-start.8 = (f16[272,384]{1,0:T(8,128)(2,1)S(1)}, f16[272,384]{1,0:T(8,128)(2,1)S(1)}, u32[]{:S(2)}, u32[]{:S(2)}) collective-permute-start(f16[272,384]{1,0:T(8,128)(2,1)S(1)} %convert_element_type.20), channel_id=1, source_target_pairs={{0,6},{2,4},{4,2},{6,0},{8,14},{10,12},{12,10},{14,8},{16,22},{18,... | collective-permute-start | bytes 626696 | tf_op jit(solution)/shard_map/ppermute | solution.py:300
  22.3 12.1 %collective-permute-start.7 = (f16[272,384]{1,0:T(8,128)(2,1)S(1)}, f16[272,384]{1,0:T(8,128)(2,1)S(1)}, u32[]{:S(2)}, u32[]{:S(2)}) collective-permute-start(f16[272,384]{1,0:T(8,128)(2,1)S(1)} %convert_element_type.19), channel_id=1, source_target_pairs={{0,4},{2,6},{4,0},{6,2},{8,12},{10,14},{12,8},{14,10},{16,20},{18,... | collective-permute-start | bytes 626696 | tf_op jit(solution)/shard_map/ppermute | solution.py:300
  23.5 11.0 %collective-permute-start.6 = (f16[272,384]{1,0:T(8,128)(2,1)S(1)}, f16[272,384]{1,0:T(8,128)(2,1)S(1)}, u32[]{:S(2)}, u32[]{:S(2)}) collective-permute-start(f16[272,384]{1,0:T(8,128)(2,1)S(1)} %convert_element_type.18), channel_id=1, source_target_pairs={{0,2},{2,0},{4,6},{6,4},{8,10},{10,8},{12,14},{14,12},{16,18},{18,... | collective-permute-start | bytes 626696 | tf_op jit(solution)/shard_map/ppermute | solution.py:300
  24.5 8.8 %collective-permute-start.12 = (bf16[512,128]{1,0:T(8,128)(2,1)S(1)}, bf16[512,128]{1,0:T(8,128)(2,1)S(1)}, u32[]{:S(2)}, u32[]{:S(2)}) collective-permute-start(bf16[512,128]{1,0:T(8,128)(2,1)S(1)} %shard_map.109.refs_0_), channel_id=1, source_target_pairs={{0,16},{2,18},{4,20},{6,22},{8,24},{10,26},{12,28},{14,30},{16,0},... | collective-permute-start | bytes 393224 | tf_op jit(solution)/shard_map/ppermute | solution.py:300
  33.6 7.7 %collective-permute-start.13 = (bf16[1024,128]{1,0:T(8,128)(2,1)S(1)}, bf16[1024,128]{1,0:T(8,128)(2,1)S(1)}, u32[]{:S(2)}, u32[]{:S(2)}) collective-permute-start(bf16[1024,128]{1,0:T(8,128)(2,1)S(1)} %shard_map.110), channel_id=1, source_target_pairs={{0,8},{2,10},{4,12},{6,14},{8,0},{10,2},{12,4},{14,6},{16,24},{18,... | collective-permute-start | bytes 786440 | tf_op jit(solution)/shard_map/ppermute | solution.py:300
  34.5 13.2 %collective-permute-start.14 = (bf16[64,2048]{1,0:T(8,128)(2,1)S(1)}, bf16[64,2048]{1,0:T(8,128)(2,1)S(1)}, u32[]{:S(2)}, u32[]{:S(2)}) collective-permute-start(bf16[64,2048]{1,0:T(8,128)(2,1)S(1)} %slice.6), channel_id=1, source_target_pairs={{0,4},{2,6},{4,0},{6,2},{8,12},{10,14},{12,8},{14,10},{16,20},{18,... | collective-permute-start | bytes 786440 | tf_op jit(solution)/shard_map/ppermute | solution.py:300
  36.1 12.2 %collective-permute-start.15 = (bf16[64,2048]{1,0:T(8,128)(2,1)S(1)}, bf16[64,2048]{1,0:T(8,128)(2,1)S(1)}, u32[]{:S(2)}, u32[]{:S(2)}) collective-permute-start(bf16[64,2048]{1,0:T(8,128)(2,1)S(1)} %slice.7), channel_id=1, source_target_pairs={{0,2},{2,0},{4,6},{6,4},{8,10},{10,8},{12,14},{14,12},{16,18},{18,... | collective-permute-start | bytes 786440 | tf_op jit(solution)/shard_map/ppermute | solution.py:300
  37.8 8.0 %collective-permute-start.11 = (f32[128,128]{1,0:T(8,128)S(1)}, f32[128,128]{1,0:T(8,128)S(1)}, u32[]{:S(2)}, u32[]{:S(2)}) collective-permute-start(f32[128,128]{1,0:T(8,128)S(1)} %get-tuple-element.63), channel_id=1, source_target_pairs={{0,24},{2,26},{4,28},{6,30},{8,16},{10,18},{12,20},{14,22},{16,8},... | collective-permute-start | bytes 196616 | tf_op jit(solution)/shard_map/ppermute | solution.py:300
  40.7 7.0 %collective-permute-start.10 = (f32[128,128]{1,0:T(8,128)S(1)}, f32[128,128]{1,0:T(8,128)S(1)}, u32[]{:S(2)}, u32[]{:S(2)}) collective-permute-start(f32[128,128]{1,0:T(8,128)S(1)} %get-tuple-element.63), channel_id=1, source_target_pairs={{0,16},{2,18},{4,20},{6,22},{8,24},{10,26},{12,28},{14,30},{16,0},... | collective-permute-start | bytes 196616 | tf_op jit(solution)/shard_map/ppermute | solution.py:300
  54.7 13.2 %collective-permute-start.25 = (f32[128,128]{1,0:T(8,128)S(1)}, f32[128,128]{1,0:T(8,128)S(1)}, u32[]{:S(2)}, u32[]{:S(2)}) collective-permute-start(f32[128,128]{1,0:T(8,128)S(1)} %get-tuple-element.74), channel_id=1, source_target_pairs={{0,24},{2,26},{4,28},{6,30},{8,16},{10,18},{12,20},{14,22},{16,8},... | collective-permute-start | bytes 196616 | tf_op jit(solution)/shard_map/ppermute | solution.py:300
  57.9 10.6 %collective-permute-start.24 = (f32[128,128]{1,0:T(8,128)S(1)}, f32[128,128]{1,0:T(8,128)S(1)}, u32[]{:S(2)}, u32[]{:S(2)}) collective-permute-start(f32[128,128]{1,0:T(8,128)S(1)} %get-tuple-element.74), channel_id=1, source_target_pairs={{0,16},{2,18},{4,20},{6,22},{8,24},{10,26},{12,28},{14,30},{16,0},... | collective-permute-start | bytes 196616 | tf_op jit(solution)/shard_map/ppermute | solution.py:300
  57.9 10.6 %collective-permute-start.23 = (f32[128,128]{1,0:T(8,128)S(1)}, f32[128,128]{1,0:T(8,128)S(1)}, u32[]{:S(2)}, u32[]{:S(2)}) collective-permute-start(f32[128,128]{1,0:T(8,128)S(1)} %get-tuple-element.74), channel_id=1, source_target_pairs={{0,8},{2,10},{4,12},{6,14},{8,0},{10,2},{12,4},{14,6},{16,24},{18,... | collective-permute-start | bytes 196616 | tf_op jit(solution)/shard_map/ppermute | solution.py:300
  60.9 10.2 %collective-permute-start.17 = (bf16[512,128]{1,0:T(8,128)(2,1)S(1)}, bf16[512,128]{1,0:T(8,128)(2,1)S(1)}, u32[]{:S(2)}, u32[]{:S(2)}) collective-permute-start(bf16[512,128]{1,0:T(8,128)(2,1)S(1)} %get-tuple-element.77), channel_id=1, source_target_pairs={{0,8},{2,10},{4,12},{6,14},{8,0},{10,2},{12,4},{14,6},{16,24},{18,... | collective-permute-start | bytes 393224 | tf_op jit(solution)/shard_map/ppermute | solution.py:300
  61.7 10.8 %collective-permute-start.18 = (bf16[512,128]{1,0:T(8,128)(2,1)S(1)}, bf16[512,128]{1,0:T(8,128)(2,1)S(1)}, u32[]{:S(2)}, u32[]{:S(2)}) collective-permute-start(bf16[512,128]{1,0:T(8,128)(2,1)S(1)} %get-tuple-element.78), channel_id=1, source_target_pairs={{0,16},{2,18},{4,20},{6,22},{8,24},{10,26},{12,28},{14,30},{16,0},... | collective-permute-start | bytes 393224 | tf_op jit(solution)/shard_map/ppermute | solution.py:300
  67.9 6.9 %collective-permute-start.19 = (bf16[512,128]{1,0:T(8,128)(2,1)S(1)}, bf16[512,128]{1,0:T(8,128)(2,1)S(1)}, u32[]{:S(2)}, u32[]{:S(2)}) collective-permute-start(bf16[512,128]{1,0:T(8,128)(2,1)S(1)} %get-tuple-element.79), channel_id=1, source_target_pairs={{0,24},{2,26},{4,28},{6,30},{8,16},{10,18},{12,20},{14,22},{16,8},... | collective-permute-start | bytes 393224 | tf_op jit(solution)/shard_map/ppermute | solution.py:300
  69.0 8.8 %collective-permute-start.26 = (bf16[256,256]{1,0:T(8,128)(2,1)S(1)}, bf16[256,256]{1,0:T(8,128)(2,1)S(1)}, u32[]{:S(2)}, u32[]{:S(2)}) collective-permute-start(bf16[256,256]{1,0:T(8,128)(2,1)S(1)} %get-tuple-element.91), channel_id=1, source_target_pairs={{0,2},{2,0},{4,6},{6,4},{8,10},{10,8},{12,14},{14,12},{16,18},{18,... | collective-permute-start | bytes 393224 | tf_op jit(solution)/shard_map/ppermute | solution.py:300
  70.6 8.6 %collective-permute-start.27 = (bf16[256,256]{1,0:T(8,128)(2,1)S(1)}, bf16[256,256]{1,0:T(8,128)(2,1)S(1)}, u32[]{:S(2)}, u32[]{:S(2)}) collective-permute-start(bf16[256,256]{1,0:T(8,128)(2,1)S(1)} %get-tuple-element.92), channel_id=1, source_target_pairs={{0,4},{2,6},{4,0},{6,2},{8,12},{10,14},{12,8},{14,10},{16,20},{18,... | collective-permute-start | bytes 393224 | tf_op jit(solution)/shard_map/ppermute | solution.py:300
  71.1 8.1 %collective-permute-start.28 = (bf16[256,256]{1,0:T(8,128)(2,1)S(1)}, bf16[256,256]{1,0:T(8,128)(2,1)S(1)}, u32[]{:S(2)}, u32[]{:S(2)}) collective-permute-start(bf16[256,256]{1,0:T(8,128)(2,1)S(1)} %get-tuple-element.93), channel_id=1, source_target_pairs={{0,6},{2,4},{4,2},{6,0},{8,14},{10,12},{12,10},{14,8},{16,22},{18,... | collective-permute-start | bytes 393224 | tf_op jit(solution)/shard_map/ppermute | solution.py:300
  (27 other events, 118.8 us)

commit v4 on v3

--- a/solution.py
+++ b/solution.py
@@ -33,18 +33,23 @@
     return x[:, k * width : (k + 1) * width]
 
 
-def call(body, outs, *args, scratch=(), spaces=None, flops=0, room=20):
+def call(body, outs, *args, scratch=(), spaces=None, flops=0, waits=()):
     vmem = pl.BlockSpec(memory_space=pltpu.VMEM)
     size = sum(a.size * a.dtype.itemsize for a in args)
+    count = len(args)
+
+    def kernel(*refs):
+        body(*refs[:count], *refs[count + len(waits) :])
+
     return pl.pallas_call(
-        body,
+        kernel,
         out_shape=outs,
-        in_specs=[vmem] * len(args) if spaces is None else spaces,
+        in_specs=([vmem] * count if spaces is None else spaces) + [pl.BlockSpec(memory_space=pl.ANY)] * len(waits),
         out_specs=jax.tree.map(lambda _: vmem, outs),
         scratch_shapes=list(scratch),
         cost_estimate=pl.CostEstimate(flops=flops, bytes_accessed=size, transcendentals=0),
-        compiler_params=pltpu.CompilerParams(vmem_limit_bytes=room * 1024 * 1024),
-    )(*args)
+        compiler_params=pltpu.CompilerParams(vmem_limit_bytes=20 * 1024 * 1024),
+    )(*args, *waits)
 
 
 def exponent(x):
@@ -141,6 +146,18 @@
     for k, ref in enumerate(sources):
         copies.append(pltpu.make_async_copy(ref, out_ref.at[pl.ds(at, ref.shape[0]), :], sem.at[k]))
         at += ref.shape[0]
+    for copy in copies:
+        copy.start()
+    for copy in copies:
+        copy.wait()
+
+
+def cut(x_ref, y_ref, a_ref, b_ref, sem):
+    size = a_ref.shape[0]
+    copies = [
+        pltpu.make_async_copy(x_ref.at[pl.ds(0, size), :], a_ref, sem.at[0]),
+        pltpu.make_async_copy(y_ref.at[pl.ds(size, size), :], b_ref, sem.at[1]),
+    ]
     for copy in copies:
         copy.start()
     for copy in copies:
@@ -292,10 +309,6 @@
         out_ref[:, pl.ds(pl.multiple_of((place_ref[0] ^ off) * size, size), size)] = ref[...]
 
 
-def after(x, *others):
-    return lax.optimization_barrier((x, *others))[0]
-
-
 def swap(x, off, parts):
     return lax.ppermute(x, "ctx", [(i, i ^ off) for i in range(parts)])
 
@@ -342,7 +355,7 @@
     def shape(r, c, dtype=F32):
         return jax.ShapeDtypeStruct((r, c), dtype)
 
-    def stack(*blocks):
+    def stack(*blocks, waits=()):
         size = sum(x.shape[0] for x in blocks)
         return call(
             pack,
@@ -350,6 +363,7 @@
             *blocks,
             spaces=[anywhere] * len(blocks),
             scratch=[pltpu.SemaphoreType.DMA((len(blocks),))],
+            waits=waits,
         )
 
     half = lax.dynamic_slice(tokens, (core * (count // 2), jnp.int32(0)), (count // 2, width))
@@ -375,10 +389,10 @@
     coded = [x.astype(F16) for x in sent[1:]]
     got = [swap(x, off, parts).astype(F32) for off, x in zip((1, 2, 3), coded)]
 
-    neighbours = stack(after(from_x, *coded, *weights), from_y)
+    neighbours = stack(from_x, from_y, waits=(*sent[1:], *weights))
     neighbours_other = other_core(neighbours)
 
-    block = stack(after(weights[0], *coded), *weights[1:])
+    block = stack(*weights, waits=sent[1:])
     chunks, layout, held = [block], [list(range(GROUP))], list(range(GROUP))
     bit = parts // 2
     while bit >= GROUP:
@@ -387,17 +401,26 @@
         layout.append([off ^ bit for off in held])
         held = held + layout[-1]
         if bit > GROUP:
-            block = stack(block, after(other, neighbours_other))
+            block = stack(block, other)
         bit //= 2
 
-    last_a = swap(after(from_x, neighbours_other, *got)[: count // 4], 2, parts)
-    last_b = swap(after(from_y, neighbours_other, *got)[count // 4 :], 1, parts)
+    quarter = count // 4
+    last_a, last_b = call(
+        cut,
+        [shape(quarter, width, BF16)] * 2,
+        from_x, from_y,
+        spaces=[anywhere] * 2,
+        scratch=[pltpu.SemaphoreType.DMA((2,))],
+        waits=(*got, neighbours_other),
+    )
+    last_a, last_b = swap(last_a, 2, parts), swap(last_b, 1, parts)
 
     every, grad_sums, total = call(
         functools.partial(grad_states, scale),
         [shape(tall, 3 * head_dim), shape(GROUP * head_dim, head_dim), shape(head_dim, head_dim)],
-        at, after(sent[0], neighbours_other), *got,
+        at, sent[0], *got,
         spaces=[smem] + [vmem] * 4,
+        waits=(neighbours_other,),
         flops=6 * tall * head_dim * head_dim,
     )
     totals = from_groups(total, steps, parts)
@@ -420,6 +443,7 @@
         [shape(3 * count, head_dim), shape(width, head_dim, BF16)],
         at, *chunks, tokens, neighbours, neighbours_other,
         spaces=[smem] + [vmem] * (3 + len(chunks)),
+        waits=(inner_k,),
         flops=2 * tall * width * head_dim,
     )
     product, last_low = call(
@@ -430,7 +454,7 @@
         scratch=[pltpu.VMEM((tall, head_dim), BF16)],
         flops=2 * tall * width * head_dim,
     )
-    last = stack(after(last_a, first, *totals), last_b)
+    last = stack(last_a, last_b, waits=(first, *totals))
     last_other = other_core(last)
 
     keys, sums, key_total = call(
@@ -446,8 +470,9 @@
     sent = call(
         functools.partial(products, steps),
         [shape(span, head_dim)] + [shape(span, head_dim, BF16)] * (len(steps) - 1),
-        at, product, after(last_low, key_total), last, last_other,
+        at, product, last_low, last, last_other,
         spaces=[smem] + [vmem] * 4,
+        waits=(key_total,),
         scratch=[pltpu.VMEM((head_dim, width), F32)],
         flops=2 * count * width * head_dim,
     )
@@ -455,7 +480,8 @@
     inner_v, inner_state = call(
         functools.partial(inner_rest, scale),
         [shape(tall, head_dim)] * 2,
-        every, after(keys, sent[0]), grad_in,
+        every, keys, grad_in,
+        waits=(sent[0],),
         flops=24 * tall * count * head_dim,
     )
 
@@ -480,8 +506,9 @@
         [shape(count, head_dim), shape(count, head_dim), shape(routing.shape[1], count)],
         at, queries, routing.T, gates.T, sent[0], *[swap(sent[off], off, parts) for off in (1, 2, 3)],
         spaces=[smem] + [vmem] * 7,
-    )
-    gate_grad = over_heads(after(gate_part, *mine)).T
+        waits=mine,
+    )
+    gate_grad = over_heads(gate_part).T
     key_grad = call(
         in_columns,
         shape(rows, memories * head_dim),

time: 85.2 us -> 82.7 us (0.971)
  local copies, waits for them, and re-layouts: 8.43 us -> 6.02 us
  waiting for transfers between devices: 17.5 us -> 15.1 us
  Pallas kernels: 18.5 us -> 19.7 us
  other arithmetic: 0.87 us -> 1.91 us
    ppermute x27, waiting for transfers between devices: 17.5 us -> 15.1 us  [swap(): return lax.ppermute(x, 'ctx', [(i, i ^ off) for i in range(parts)])]
    unnamed x43 -> x39, local copies, waits for them, and re-layouts: 5.65 us -> 4.1 us
    pallas_call x18 -> x19, Pallas kernels: 18.5 us -> 19.7 us  [call(): pl.pallas_call(kernel, out_shape=outs, in_specs=([vmem] * count if spaces...]
    add x2, other arithmetic: 0.04 us -> 1.08 us  [prefix(): before + jnp.where(other > here if reverse else other < here, x, 0.0)]
  transfers between devices with their start and end apart: 30 -> 30, of which waited for: 7 -> 10; matrix products, arithmetic and copies ran while one was open for 2% -> 4% of each run, Pallas kernels for 19% -> 20%
where the time goes in v4:
time: 82.7 us; the launch traced here: 82.3 us
  starting transfers between devices  38.4 us (46%)
  Pallas kernels  19.7 us (24%)
  waiting for transfers between devices  15.1 us (18%)
  local copies, waits for them, and re-layouts  6.02 us (7%)
  other arithmetic  1.91 us (2%)
  between operations  1.14 us (1%)
    ppermute x27, starting transfers between devices, swap(): return lax.ppermute(x, 'ctx', [(i, i ^ off) for i in range(parts)])  38.3 us
    pallas_call x19, Pallas kernels, call(): pl.pallas_call(kernel, out_shape=outs, in_specs=([vmem] * count if spaces...  19.7 us
    ppermute x27, waiting for transfers between devices, swap(): return lax.ppermute(x, 'ctx', [(i, i ^ off) for i in range(parts)])  15.1 us
    unnamed x39, local copies, waits for them, and re-layouts  4.1 us
  transfers between devices with their start and end apart: 30, of which 10 were waited for; matrix products, arithmetic and copies ran while one was open for 4% of the time, Pallas kernels for 20%

profile of v4, /device:TPU:0, one launch (start us, length us, event | category | flops | bytes accessed | tf_op | source)
XLA Modules:
  0.0 82.3 jit_solution(5267778339777928804)
XLA Ops:
  1.8 3.0 %collective-permute-start.1 = (bf16[128,2048]{1,0:T(8,128)(2,1)S(1)}, bf16[128,2048]{1,0:T(8,128)(2,1)S(1)}, u32[]{:S(2)}, u32[]{:S(2)}) collective-permute-start(bf16[128,2048]{1,0:T(8,128)(2,1)S(1)} %constant_dynamic-slice_fusion), channel_id=1, source_target_pairs={{0,4},{2,6},{4,0},{6,2},{8,12},{10,14},{12,8},{14,10},{16,20},{18,... | collective-permute-start | bytes 1572872 | tf_op jit(solution)/shard_map/ppermute | solution.py:313
  4.8 1.5 %collective-permute-start = (bf16[128,2048]{1,0:T(8,128)(2,1)S(1)}, bf16[128,2048]{1,0:T(8,128)(2,1)S(1)}, u32[]{:S(2)}, u32[]{:S(2)}) collective-permute-start(bf16[128,2048]{1,0:T(8,128)(2,1)S(1)} %constant_dynamic-slice_fusion), channel_id=1, source_target_pairs={{0,2},{2,0},{4,6},{6,4},{8,10},{10,8},{12,14},{14,12},{16,18},{18,... | collective-permute-start | bytes 1572872 | tf_op jit(solution)/shard_map/ppermute | solution.py:313
  8.6 2.9 %collective-permute-start.4 = (bf16[128,128]{1,0:T(8,128)(2,1)S(1)}, bf16[128,128]{1,0:T(8,128)(2,1)S(1)}, u32[]{:S(2)}, u32[]{:S(2)}) collective-permute-start(bf16[128,128]{1,0:T(8,128)(2,1)S(1)} %get-tuple-element.49), channel_id=1, source_target_pairs={{0,6},{2,4},{4,2},{6,0},{8,14},{10,12},{12,10},{14,8},{16,22},{18,... | collective-permute-start | bytes 98312 | tf_op jit(solution)/shard_map/ppermute | solution.py:313
  12.9 1.6 %shard_map.102 = (f32[256,384]{1,0:T(8,128)S(1)}, f32[272,384]{1,0:T(8,128)S(1)}, f32[272,384]{1,0:T(8,128)S(1)}, f32[272,384]{1,0:T(8,128)S(1)}) custom-call(s32[4]{0:T(128)S(1)} %pad_add_fusion.refs_0_, f32[256,128]{1,0:T(8,128)S(1)} %copy-done.4, f32[256,128]{1,0:T(8,128)S(1)} %copy-done.13, f32[256,128]{1,0:T(8,128)S(1)} %copy-done.14, ...), custom_call_target="tpu_custom_call" | custom-call | bytes 397328 | tf_op jit(solution)/shard_map/pallas_call | solution.py:44
  14.4 4.8 %collective-permute-done.2.refs_6_.refs_1_ = bf16[128,128]{1,0:T(8,128)(2,1)S(1)} collective-permute-done((bf16[128,128]{1,0:T(8,128)(2,1)S(1)}, bf16[128,128]{1,0:T(8,128)(2,1)S(1)}, u32[]{:S(2)}, u32[]{:S(2)}) %collective-permute-start.2) | collective-permute-done | bytes 32800 | tf_op jit(solution)/shard_map/ppermute | solution.py:313
  19.8 2.8 %collective-permute-start.14 = (bf16[512,128]{1,0:T(8,128)(2,1)S(1)}, bf16[512,128]{1,0:T(8,128)(2,1)S(1)}, u32[]{:S(2)}, u32[]{:S(2)}) collective-permute-start(bf16[512,128]{1,0:T(8,128)(2,1)S(1)} %shard_map.110.refs_0_.refs_1_), channel_id=1, source_target_pairs={{0,16},{2,18},{4,20},{6,22},{8,24},{10,26},{12,28},{14,30},{16,0},... | collective-permute-start | bytes 393224 | tf_op jit(solution)/shard_map/ppermute | solution.py:313
  22.7 2.5 %collective-permute-start.8 = (f16[272,384]{1,0:T(8,128)(2,1)S(1)}, f16[272,384]{1,0:T(8,128)(2,1)S(1)}, u32[]{:S(2)}, u32[]{:S(2)}) collective-permute-start(f16[272,384]{1,0:T(8,128)(2,1)S(1)} %convert_element_type.22), channel_id=1, source_target_pairs={{0,6},{2,4},{4,2},{6,0},{8,14},{10,12},{12,10},{14,8},{16,22},{18,... | collective-permute-start | bytes 626696 | tf_op jit(solution)/shard_map/ppermute | solution.py:313
  26.4 3.2 %collective-permute-done.14.refs_1_.refs_2_ = bf16[512,128]{1,0:T(8,128)(2,1)S(1)} collective-permute-done((bf16[512,128]{1,0:T(8,128)(2,1)S(1)}, bf16[512,128]{1,0:T(8,128)(2,1)S(1)}, u32[]{:S(2)}, u32[]{:S(2)}) %collective-permute-start.14) | collective-permute-done | bytes 131104 | tf_op jit(solution)/shard_map/ppermute | solution.py:313
  31.7 3.6 %collective-permute-done.7 = f16[272,384]{1,0:T(8,128)(2,1)S(1)} collective-permute-done((f16[272,384]{1,0:T(8,128)(2,1)S(1)}, f16[272,384]{1,0:T(8,128)(2,1)S(1)}, u32[]{:S(2)}, u32[]{:S(2)}) %collective-permute-start.7) | collective-permute-done | bytes 208928 | tf_op jit(solution)/shard_map/ppermute | solution.py:313
  35.6 1.5 %collective-permute-start.12 = (bf16[64,2048]{1,0:T(8,128)(2,1)S(1)}, bf16[64,2048]{1,0:T(8,128)(2,1)S(1)}, u32[]{:S(2)}, u32[]{:S(2)}) collective-permute-start(bf16[64,2048]{1,0:T(8,128)(2,1)S(1)} %get-tuple-element.57), channel_id=1, source_target_pairs={{0,4},{2,6},{4,0},{6,2},{8,12},{10,14},{12,8},{14,10},{16,20},{18,... | collective-permute-start | bytes 786440 | tf_op jit(solution)/shard_map/ppermute | solution.py:313
  39.0 1.4 %collective-permute-start.11 = (f32[128,128]{1,0:T(8,128)S(1)}, f32[128,128]{1,0:T(8,128)S(1)}, u32[]{:S(2)}, u32[]{:S(2)}) collective-permute-start(f32[128,128]{1,0:T(8,128)S(1)} %get-tuple-element.53), channel_id=1, source_target_pairs={{0,24},{2,26},{4,28},{6,30},{8,16},{10,18},{12,20},{14,22},{16,8},... | collective-permute-start | bytes 196616 | tf_op jit(solution)/shard_map/ppermute | solution.py:313
  40.5 1.7 %collective-permute-start.10 = (f32[128,128]{1,0:T(8,128)S(1)}, f32[128,128]{1,0:T(8,128)S(1)}, u32[]{:S(2)}, u32[]{:S(2)}) collective-permute-start(f32[128,128]{1,0:T(8,128)S(1)} %get-tuple-element.53), channel_id=1, source_target_pairs={{0,16},{2,18},{4,20},{6,22},{8,24},{10,26},{12,28},{14,30},{16,0},... | collective-permute-start | bytes 196616 | tf_op jit(solution)/shard_map/ppermute | solution.py:313
  43.5 1.5 %shard_map.106.refs_3_.refs_7_ = f32[1024,128]{1,0:T(8,128)S(1)} custom-call(f32[1024,384]{1,0:T(8,128)S(1)} %get-tuple-element.51.refs_0_.refs_5_), custom_call_target="tpu_custom_call" | custom-call | flops 402653184 | bytes 1572864 | tf_op jit(solution)/shard_map/pallas_call | solution.py:44
  45.0 1.6 %shard_map.112 = (f32[768,128]{1,0:T(8,128)S(1)}, bf16[2048,128]{1,0:T(8,128)(2,1)S(1)}) custom-call(s32[4]{0:T(128)S(1)} %pad_add_fusion.refs_0_, bf16[512,128]{1,0:T(8,128)(2,1)S(1)} %shard_map.110.refs_0_.refs_1_, bf16[512,128]{1,0:T(8,128)(2,1)S(1)} %collective-permute-done.14.refs_1_.refs_2_, bf16[1024,128]{1,0:T(8,128)(2,1)S(1)} %collective-permute-done.15.refs_3_, ...), custom_call_target="tpu_custom_call" | custom-call | flops 536870912 | bytes 3670032 | tf_op jit(solution)/shard_map/pallas_call | solution.py:44
  52.1 2.0 %shard_map.114 = (f32[1024,128]{1,0:T(8,128)S(1)}, f32[512,128]{1,0:T(8,128)S(1)}, f32[128,128]{1,0:T(8,128)S(1)}) custom-call(s32[4]{0:T(128)S(1)} %pad_add_fusion.refs_0_, f32[768,128]{1,0:T(8,128)S(1)} %get-tuple-element.59.refs_2_.refs_1_, bf16[2048,128]{1,0:T(8,128)(2,1)S(1)} %copy-done.7, bf16[128,2048]{1,0:T(8,128)(2,1)} %shard_map.113.refs_3_, ...), custom_call_target="tpu_custom_call" | custom-call | flops 134217728 | bytes 3538960 | tf_op jit(solution)/shard_map/pallas_call | solution.py:44
  54.7 1.5 %collective-permute-start.24 = (f32[128,128]{1,0:T(8,128)S(1)}, f32[128,128]{1,0:T(8,128)S(1)}, u32[]{:S(2)}, u32[]{:S(2)}) collective-permute-start(f32[128,128]{1,0:T(8,128)S(1)} %get-tuple-element.61.refs_5_), channel_id=1, source_target_pairs={{0,16},{2,18},{4,20},{6,22},{8,24},{10,26},{12,28},{14,30},{16,0},... | collective-permute-start | bytes 196616 | tf_op jit(solution)/shard_map/ppermute | solution.py:313
  56.3 2.3 %collective-permute-start.23 = (f32[128,128]{1,0:T(8,128)S(1)}, f32[128,128]{1,0:T(8,128)S(1)}, u32[]{:S(2)}, u32[]{:S(2)}) collective-permute-start(f32[128,128]{1,0:T(8,128)S(1)} %get-tuple-element.61.refs_5_), channel_id=1, source_target_pairs={{0,8},{2,10},{4,12},{6,14},{8,0},{10,2},{12,4},{14,6},{16,24},{18,... | collective-permute-start | bytes 196616 | tf_op jit(solution)/shard_map/ppermute | solution.py:313
  58.5 1.9 %shard_map.115 = (f32[512,128]{1,0:T(8,128)S(1)}, bf16[512,128]{1,0:T(8,128)(2,1)S(1)}, bf16[512,128]{1,0:T(8,128)(2,1)S(1)}, bf16[512,128]{1,0:T(8,128)(2,1)S(1)}) custom-call(s32[4]{0:T(128)S(1)} %pad_add_fusion.refs_0_, f32[128,2048]{1,0:T(8,128)S(1)} %get-tuple-element.55.refs_1_, bf16[128,256]{1,0:T(8,128)(2,1)S(1)} %get-tuple-element.56.refs_2_, ...), custom_call_target="tpu_custom_call" | custom-call | flops 134217728 | bytes 2162704 | tf_op jit(solution)/shard_map/pallas_call | solution.py:44
  61.6 3.2 %shard_map.118 = (f32[1024,128]{1,0:T(8,128)S(1)}, f32[1024,128]{1,0:T(8,128)S(1)}) custom-call(f32[1024,384]{1,0:T(8,128)S(1)} %get-tuple-element.51.refs_0_.refs_5_, f32[1024,128]{1,0:T(8,128)S(1)} %get-tuple-element.71.refs_1_, f32[512,128]{1,0:T(8,128)S(1)} %get-tuple-element.72.refs_2_, f32[512,128]{1,0:T(8,128)S(1)} %get-tuple-element.62.refs_1_.refs_3_), custom_call_target="tpu_custom_call" | custom-call | flops 805306368 | bytes 2359296 | tf_op jit(solution)/shard_map/pallas_call | solution.py:44
  64.8 3.3 %collective-permute-start.19 = (bf16[512,128]{1,0:T(8,128)(2,1)S(1)}, bf16[512,128]{1,0:T(8,128)(2,1)S(1)}, u32[]{:S(2)}, u32[]{:S(2)}) collective-permute-start(bf16[512,128]{1,0:T(8,128)(2,1)S(1)} %get-tuple-element.65), channel_id=1, source_target_pairs={{0,24},{2,26},{4,28},{6,30},{8,16},{10,18},{12,20},{14,22},{16,8},... | collective-permute-start | bytes 393224 | tf_op jit(solution)/shard_map/ppermute | solution.py:313
  68.6 1.7 %collective-permute-start.26 = (bf16[256,256]{1,0:T(8,128)(2,1)S(1)}, bf16[256,256]{1,0:T(8,128)(2,1)S(1)}, u32[]{:S(2)}, u32[]{:S(2)}) collective-permute-start(bf16[256,256]{1,0:T(8,128)(2,1)S(1)} %get-tuple-element.76), channel_id=1, source_target_pairs={{0,2},{2,0},{4,6},{6,4},{8,10},{10,8},{12,14},{14,12},{16,18},{18,... | collective-permute-start | bytes 393224 | tf_op jit(solution)/shard_map/ppermute | solution.py:313
  73.1 1.7 %collective-permute-start.20 = (f32[128,128]{1,0:T(8,128)S(1)}, f32[128,128]{1,0:T(8,128)S(1)}, u32[]{:S(2)}, u32[]{:S(2)}) collective-permute-start(f32[128,128]{1,0:T(8,128)S(1)} %get-tuple-element.67.refs_9_), channel_id=1, source_target_pairs={{0,2},{2,0},{4,6},{6,4},{8,10},{10,8},{12,14},{14,12},{16,18},{18,... | collective-permute-start | bytes 196616 | tf_op jit(solution)/shard_map/ppermute | solution.py:313
  75.2 1.4 %collective-permute-start.22 = (f32[128,128]{1,0:T(8,128)S(1)}, f32[128,128]{1,0:T(8,128)S(1)}, u32[]{:S(2)}, u32[]{:S(2)}) collective-permute-start(f32[128,128]{1,0:T(8,128)S(1)} %get-tuple-element.69.refs_11_), channel_id=1, source_target_pairs={{0,6},{2,4},{4,2},{6,0},{8,14},{10,12},{12,10},{14,8},{16,22},{18,... | collective-permute-start | bytes 196616 | tf_op jit(solution)/shard_map/ppermute | solution.py:313
  78.2 1.8 %shard_map.120 = (f32[256,128]{1,0:T(8,128)}, f32[256,128]{1,0:T(8,128)}, f32[2,256]{1,0:T(2,128)S(1)}) custom-call(s32[4]{0:T(128)S(1)} %pad_add_fusion.refs_0_, f32[256,128]{1,0:T(8,128)S(1)} %copy-done.5, s32[2,256]{1,0:T(2,128)S(1)} %bitcast.14, f32[2,256]{1,0:T(2,128)S(1)} %bitcast.16, f32[256,256]{1,0:T(8,128)S(1)} %get-tuple-element.75.refs_4_, ...), custom_call_target="tpu_custom_call" | custom-call | bytes 790544 | tf_op jit(solution)/shard_map/pallas_call | solution.py:44
  (106 shorter events, 26.9 us)
Async XLA Ops:
  1.8 17.6 %collective-permute-start.1 = (bf16[128,2048]{1,0:T(8,128)(2,1)S(1)}, bf16[128,2048]{1,0:T(8,128)(2,1)S(1)}, u32[]{:S(2)}, u32[]{:S(2)}) collective-permute-start(bf16[128,2048]{1,0:T(8,128)(2,1)S(1)} %constant_dynamic-slice_fusion), channel_id=1, source_target_pairs={{0,4},{2,6},{4,0},{6,2},{8,12},{10,14},{12,8},{14,10},{16,20},{18,... | collective-permute-start | bytes 1572872 | tf_op jit(solution)/shard_map/ppermute | solution.py:313
  4.8 14.6 %collective-permute-start = (bf16[128,2048]{1,0:T(8,128)(2,1)S(1)}, bf16[128,2048]{1,0:T(8,128)(2,1)S(1)}, u32[]{:S(2)}, u32[]{:S(2)}) collective-permute-start(bf16[128,2048]{1,0:T(8,128)(2,1)S(1)} %constant_dynamic-slice_fusion), channel_id=1, source_target_pairs={{0,2},{2,0},{4,6},{6,4},{8,10},{10,8},{12,14},{14,12},{16,18},{18,... | collective-permute-start | bytes 1572872 | tf_op jit(solution)/shard_map/ppermute | solution.py:313
  7.9 11.3 %collective-permute-start.2 = (bf16[128,128]{1,0:T(8,128)(2,1)S(1)}, bf16[128,128]{1,0:T(8,128)(2,1)S(1)}, u32[]{:S(2)}, u32[]{:S(2)}) collective-permute-start(bf16[128,128]{1,0:T(8,128)(2,1)S(1)} %get-tuple-element.47), channel_id=1, source_target_pairs={{0,2},{2,0},{4,6},{6,4},{8,10},{10,8},{12,14},{14,12},{16,18},{18,... | collective-permute-start | bytes 98312 | tf_op jit(solution)/shard_map/ppermute | solution.py:313
  8.5 10.7 %collective-permute-start.3 = (bf16[128,128]{1,0:T(8,128)(2,1)S(1)}, bf16[128,128]{1,0:T(8,128)(2,1)S(1)}, u32[]{:S(2)}, u32[]{:S(2)}) collective-permute-start(bf16[128,128]{1,0:T(8,128)(2,1)S(1)} %get-tuple-element.48), channel_id=1, source_target_pairs={{0,4},{2,6},{4,0},{6,2},{8,12},{10,14},{12,8},{14,10},{16,20},{18,... | collective-permute-start | bytes 98312 | tf_op jit(solution)/shard_map/ppermute | solution.py:313
  8.6 10.8 %collective-permute-start.4 = (bf16[128,128]{1,0:T(8,128)(2,1)S(1)}, bf16[128,128]{1,0:T(8,128)(2,1)S(1)}, u32[]{:S(2)}, u32[]{:S(2)}) collective-permute-start(bf16[128,128]{1,0:T(8,128)(2,1)S(1)} %get-tuple-element.49), channel_id=1, source_target_pairs={{0,6},{2,4},{4,2},{6,0},{8,14},{10,12},{12,10},{14,8},{16,22},{18,... | collective-permute-start | bytes 98312 | tf_op jit(solution)/shard_map/ppermute | solution.py:313
  19.5 16.0 %collective-permute-start.5 = (bf16[256,2048]{1,0:T(8,128)(2,1)S(1)}, bf16[256,2048]{1,0:T(8,128)(2,1)S(1)}, u32[]{:S(2)}, u32[]{:S(2)}) collective-permute-start(bf16[256,2048]{1,0:T(8,128)(2,1)S(1)} %shard_map.104.refs_2_.refs_5_), channel_id=1, source_target_pairs={{0,1},{1,0},{2,3},{3,2},{4,5},{5,4},{6,7},{7,6},{8,9},{9,8},{10,11... | collective-permute-start | bytes 3145736 | tf_op jit(solution)/shard_map/ppermute | solution.py:317
  19.8 9.7 %collective-permute-start.14 = (bf16[512,128]{1,0:T(8,128)(2,1)S(1)}, bf16[512,128]{1,0:T(8,128)(2,1)S(1)}, u32[]{:S(2)}, u32[]{:S(2)}) collective-permute-start(bf16[512,128]{1,0:T(8,128)(2,1)S(1)} %shard_map.110.refs_0_.refs_1_), channel_id=1, source_target_pairs={{0,16},{2,18},{4,20},{6,22},{8,24},{10,26},{12,28},{14,30},{16,0},... | collective-permute-start | bytes 393224 | tf_op jit(solution)/shard_map/ppermute | solution.py:313
  22.7 9.0 %collective-permute-start.8 = (f16[272,384]{1,0:T(8,128)(2,1)S(1)}, f16[272,384]{1,0:T(8,128)(2,1)S(1)}, u32[]{:S(2)}, u32[]{:S(2)}) collective-permute-start(f16[272,384]{1,0:T(8,128)(2,1)S(1)} %convert_element_type.22), channel_id=1, source_target_pairs={{0,6},{2,4},{4,2},{6,0},{8,14},{10,12},{12,10},{14,8},{16,22},{18,... | collective-permute-start | bytes 626696 | tf_op jit(solution)/shard_map/ppermute | solution.py:313
  25.2 10.1 %collective-permute-start.7 = (f16[272,384]{1,0:T(8,128)(2,1)S(1)}, f16[272,384]{1,0:T(8,128)(2,1)S(1)}, u32[]{:S(2)}, u32[]{:S(2)}) collective-permute-start(f16[272,384]{1,0:T(8,128)(2,1)S(1)} %convert_element_type.20), channel_id=1, source_target_pairs={{0,4},{2,6},{4,0},{6,2},{8,12},{10,14},{12,8},{14,10},{16,20},{18,... | collective-permute-start | bytes 626696 | tf_op jit(solution)/shard_map/ppermute | solution.py:313
  25.8 9.6 %collective-permute-start.6 = (f16[272,384]{1,0:T(8,128)(2,1)S(1)}, f16[272,384]{1,0:T(8,128)(2,1)S(1)}, u32[]{:S(2)}, u32[]{:S(2)}) collective-permute-start(f16[272,384]{1,0:T(8,128)(2,1)S(1)} %convert_element_type.18), channel_id=1, source_target_pairs={{0,2},{2,0},{4,6},{6,4},{8,10},{10,8},{12,14},{14,12},{16,18},{18,... | collective-permute-start | bytes 626696 | tf_op jit(solution)/shard_map/ppermute | solution.py:313
  29.9 12.2 %collective-permute-start.15 = (bf16[1024,128]{1,0:T(8,128)(2,1)S(1)}, bf16[1024,128]{1,0:T(8,128)(2,1)S(1)}, u32[]{:S(2)}, u32[]{:S(2)}) collective-permute-start(bf16[1024,128]{1,0:T(8,128)(2,1)S(1)} %shard_map.111), channel_id=1, source_target_pairs={{0,8},{2,10},{4,12},{6,14},{8,0},{10,2},{12,4},{14,6},{16,24},{18,... | collective-permute-start | bytes 786440 | tf_op jit(solution)/shard_map/ppermute | solution.py:313
  35.6 11.9 %collective-permute-start.12 = (bf16[64,2048]{1,0:T(8,128)(2,1)S(1)}, bf16[64,2048]{1,0:T(8,128)(2,1)S(1)}, u32[]{:S(2)}, u32[]{:S(2)}) collective-permute-start(bf16[64,2048]{1,0:T(8,128)(2,1)S(1)} %get-tuple-element.57), channel_id=1, source_target_pairs={{0,4},{2,6},{4,0},{6,2},{8,12},{10,14},{12,8},{14,10},{16,20},{18,... | collective-permute-start | bytes 786440 | tf_op jit(solution)/shard_map/ppermute | solution.py:313
  37.1 10.3 %collective-permute-start.13 = (bf16[64,2048]{1,0:T(8,128)(2,1)S(1)}, bf16[64,2048]{1,0:T(8,128)(2,1)S(1)}, u32[]{:S(2)}, u32[]{:S(2)}) collective-permute-start(bf16[64,2048]{1,0:T(8,128)(2,1)S(1)} %get-tuple-element.58), channel_id=1, source_target_pairs={{0,2},{2,0},{4,6},{6,4},{8,10},{10,8},{12,14},{14,12},{16,18},{18,... | collective-permute-start | bytes 786440 | tf_op jit(solution)/shard_map/ppermute | solution.py:313
  39.0 8.3 %collective-permute-start.11 = (f32[128,128]{1,0:T(8,128)S(1)}, f32[128,128]{1,0:T(8,128)S(1)}, u32[]{:S(2)}, u32[]{:S(2)}) collective-permute-start(f32[128,128]{1,0:T(8,128)S(1)} %get-tuple-element.53), channel_id=1, source_target_pairs={{0,24},{2,26},{4,28},{6,30},{8,16},{10,18},{12,20},{14,22},{16,8},... | collective-permute-start | bytes 196616 | tf_op jit(solution)/shard_map/ppermute | solution.py:313
  40.5 6.9 %collective-permute-start.10 = (f32[128,128]{1,0:T(8,128)S(1)}, f32[128,128]{1,0:T(8,128)S(1)}, u32[]{:S(2)}, u32[]{:S(2)}) collective-permute-start(f32[128,128]{1,0:T(8,128)S(1)} %get-tuple-element.53), channel_id=1, source_target_pairs={{0,16},{2,18},{4,20},{6,22},{8,24},{10,26},{12,28},{14,30},{16,0},... | collective-permute-start | bytes 196616 | tf_op jit(solution)/shard_map/ppermute | solution.py:313
  54.1 10.7 %collective-permute-start.25 = (f32[128,128]{1,0:T(8,128)S(1)}, f32[128,128]{1,0:T(8,128)S(1)}, u32[]{:S(2)}, u32[]{:S(2)}) collective-permute-start(f32[128,128]{1,0:T(8,128)S(1)} %get-tuple-element.61.refs_5_), channel_id=1, source_target_pairs={{0,24},{2,26},{4,28},{6,30},{8,16},{10,18},{12,20},{14,22},{16,8},... | collective-permute-start | bytes 196616 | tf_op jit(solution)/shard_map/ppermute | solution.py:313
  54.7 13.4 %collective-permute-start.24 = (f32[128,128]{1,0:T(8,128)S(1)}, f32[128,128]{1,0:T(8,128)S(1)}, u32[]{:S(2)}, u32[]{:S(2)}) collective-permute-start(f32[128,128]{1,0:T(8,128)S(1)} %get-tuple-element.61.refs_5_), channel_id=1, source_target_pairs={{0,16},{2,18},{4,20},{6,22},{8,24},{10,26},{12,28},{14,30},{16,0},... | collective-permute-start | bytes 196616 | tf_op jit(solution)/shard_map/ppermute | solution.py:313
  56.3 11.9 %collective-permute-start.23 = (f32[128,128]{1,0:T(8,128)S(1)}, f32[128,128]{1,0:T(8,128)S(1)}, u32[]{:S(2)}, u32[]{:S(2)}) collective-permute-start(f32[128,128]{1,0:T(8,128)S(1)} %get-tuple-element.61.refs_5_), channel_id=1, source_target_pairs={{0,8},{2,10},{4,12},{6,14},{8,0},{10,2},{12,4},{14,6},{16,24},{18,... | collective-permute-start | bytes 196616 | tf_op jit(solution)/shard_map/ppermute | solution.py:313
  60.4 10.3 %collective-permute-start.17 = (bf16[512,128]{1,0:T(8,128)(2,1)S(1)}, bf16[512,128]{1,0:T(8,128)(2,1)S(1)}, u32[]{:S(2)}, u32[]{:S(2)}) collective-permute-start(bf16[512,128]{1,0:T(8,128)(2,1)S(1)} %get-tuple-element.63), channel_id=1, source_target_pairs={{0,8},{2,10},{4,12},{6,14},{8,0},{10,2},{12,4},{14,6},{16,24},{18,... | collective-permute-start | bytes 393224 | tf_op jit(solution)/shard_map/ppermute | solution.py:313
  60.5 11.9 %collective-permute-start.18 = (bf16[512,128]{1,0:T(8,128)(2,1)S(1)}, bf16[512,128]{1,0:T(8,128)(2,1)S(1)}, u32[]{:S(2)}, u32[]{:S(2)}) collective-permute-start(bf16[512,128]{1,0:T(8,128)(2,1)S(1)} %get-tuple-element.64), channel_id=1, source_target_pairs={{0,16},{2,18},{4,20},{6,22},{8,24},{10,26},{12,28},{14,30},{16,0},... | collective-permute-start | bytes 393224 | tf_op jit(solution)/shard_map/ppermute | solution.py:313
  64.8 7.6 %collective-permute-start.19 = (bf16[512,128]{1,0:T(8,128)(2,1)S(1)}, bf16[512,128]{1,0:T(8,128)(2,1)S(1)}, u32[]{:S(2)}, u32[]{:S(2)}) collective-permute-start(bf16[512,128]{1,0:T(8,128)(2,1)S(1)} %get-tuple-element.65), channel_id=1, source_target_pairs={{0,24},{2,26},{4,28},{6,30},{8,16},{10,18},{12,20},{14,22},{16,8},... | collective-permute-start | bytes 393224 | tf_op jit(solution)/shard_map/ppermute | solution.py:313
  70.2 6.9 %collective-permute-start.27 = (bf16[256,256]{1,0:T(8,128)(2,1)S(1)}, bf16[256,256]{1,0:T(8,128)(2,1)S(1)}, u32[]{:S(2)}, u32[]{:S(2)}) collective-permute-start(bf16[256,256]{1,0:T(8,128)(2,1)S(1)} %get-tuple-element.77), channel_id=1, source_target_pairs={{0,4},{2,6},{4,0},{6,2},{8,12},{10,14},{12,8},{14,10},{16,20},{18,... | collective-permute-start | bytes 393224 | tf_op jit(solution)/shard_map/ppermute | solution.py:313
  70.8 7.4 %collective-permute-start.28 = (bf16[256,256]{1,0:T(8,128)(2,1)S(1)}, bf16[256,256]{1,0:T(8,128)(2,1)S(1)}, u32[]{:S(2)}, u32[]{:S(2)}) collective-permute-start(bf16[256,256]{1,0:T(8,128)(2,1)S(1)} %get-tuple-element.78), channel_id=1, source_target_pairs={{0,6},{2,4},{4,2},{6,0},{8,14},{10,12},{12,10},{14,8},{16,22},{18,... | collective-permute-start | bytes 393224 | tf_op jit(solution)/shard_map/ppermute | solution.py:313
  73.1 6.9 %collective-permute-start.20 = (f32[128,128]{1,0:T(8,128)S(1)}, f32[128,128]{1,0:T(8,128)S(1)}, u32[]{:S(2)}, u32[]{:S(2)}) collective-permute-start(f32[128,128]{1,0:T(8,128)S(1)} %get-tuple-element.67.refs_9_), channel_id=1, source_target_pairs={{0,2},{2,0},{4,6},{6,4},{8,10},{10,8},{12,14},{14,12},{16,18},{18,... | collective-permute-start | bytes 196616 | tf_op jit(solution)/shard_map/ppermute | solution.py:313
  (25 other events, 141.4 us)

commit v5 on v4

--- a/solution.py
+++ b/solution.py
@@ -21,12 +21,10 @@
 
 
 def dot3(a, b, b_last=False):
-    dims = (((1,), (1 if b_last else 0,)), ((), ()))
-
-    def one(x, y):
-        return lax.dot_general(x, y, dims, preferred_element_type=F32)
-
-    return one(a[0], b[0]) + (one(a[0], b[1]) + one(a[1], b[0]))
+    side = 1 if b_last else 0
+    left = jnp.concatenate([a[0], a[0], a[1]], axis=1)
+    right = jnp.concatenate([b[0], b[1], b[0]], axis=side)
+    return lax.dot_general(left, right, (((1,), (side,)), ((), ())), preferred_element_type=F32)
 
 
 def part(x, k, width):
@@ -69,18 +67,23 @@
         copy.wait()
 
 
+def router_columns(place, routing, gates):
+    hits = [routing == (place ^ off) for off in range(GROUP)]
+    rows = [jnp.sum(jnp.where(hit, gates, 0.0), axis=0, keepdims=True) for hit in hits]
+    rows += [jnp.sum(hit.astype(F32), axis=0, keepdims=True) for hit in hits]
+    columns = jnp.concatenate(rows, axis=0).T
+    return [(columns[:, off : off + 1], columns[:, GROUP + off : GROUP + off + 1], hit) for off, hit in enumerate(hits)]
+
+
 def messages(place_ref, q_at, v_at, dout_at, routing_at, gates_at, own, near, far, both, q_ref, v_ref, dout_ref, routing_ref, gates_ref, sem):
     fetch((q_at, v_at, dout_at, routing_at, gates_at), (q_ref, v_ref, dout_ref, routing_ref, gates_ref), sem)
     count, width = q_ref.shape
-    routing, gates = routing_ref[...].T, gates_ref[...].T
-    place = place_ref[0]
+    routers = router_columns(place_ref[0], routing_ref[...], gates_ref[...])
     q, v, dout = q_ref[...], v_ref[...], dout_ref[...]
     exponents = [exponent(x) for x in (q, v, dout)]
     scales = [1.0 / power(k) for k in exponents]
     for off, ref in enumerate((own, near, far, both)):
-        hit = routing == (place ^ off)
-        weight = jnp.sum(jnp.where(hit, gates, 0.0), axis=1, keepdims=True)
-        routed = jnp.sum(hit.astype(F32), axis=1, keepdims=True)
+        weight, routed, _ = routers[off]
         for k, x in enumerate((weight * q, routed * v, dout)):
             column = slice(k * width, (k + 1) * width)
             if off:
@@ -268,22 +271,23 @@
 
 
 def at_home(scale, place_ref, q_ref, routing_ref, gates_ref, own, near, far, both, query_ref, value_ref, gate_ref):
-    queries, routing, gates = q_ref[...], routing_ref[...].T, gates_ref[...].T
+    queries = q_ref[...]
     width = queries.shape[1]
     query = jnp.zeros_like(queries)
     value = jnp.zeros_like(queries)
-    gate = jnp.zeros(gate_ref.shape[::-1], F32)
-    for off, ref in enumerate((own, near, far, both)):
-        hit = routing == (place_ref[0] ^ off)
-        weight = jnp.sum(jnp.where(hit, gates, 0.0), axis=1, keepdims=True)
-        routed = jnp.sum(hit.astype(F32), axis=1, keepdims=True)
+    gate = jnp.zeros(gate_ref.shape, F32)
+    ones = jnp.ones((gate.shape[0], 2 * width), BF16)
+    routers = router_columns(place_ref[0], routing_ref[...], gates_ref[...])
+    for (weight, routed, hit), ref in zip(routers, (own, near, far, both), strict=True):
         state = ref[:, :width].astype(F32)
         query = query + weight * state
         value = value + routed * ref[:, width:].astype(F32)
-        gate = gate + jnp.where(hit, jnp.sum(queries * state, axis=1, keepdims=True), 0.0)
+        terms = jnp.concatenate(split(queries * state), axis=1)
+        mine = lax.dot_general(ones, terms, (((1,), (1,)), ((), ())), preferred_element_type=F32)
+        gate = gate + jnp.where(hit, mine, 0.0)
     query_ref[...] = scale * query
     value_ref[...] = value
-    gate_ref[...] = (scale * gate).T
+    gate_ref[...] = scale * gate
 
 
 def by_column(place_ref, x_ref, own, near, far, both):
@@ -454,7 +458,7 @@
         scratch=[pltpu.VMEM((tall, head_dim), BF16)],
         flops=2 * tall * width * head_dim,
     )
-    last = stack(last_a, last_b, waits=(first, *totals))
+    last = stack(last_a, last_b, waits=(first[:8], *totals))
     last_other = other_core(last)
 
     keys, sums, key_total = call(

time: 82.7 us -> 82.2 us (level)
    unnamed x39 -> x37, local copies, waits for them, and re-layouts: 4.1 us -> 4.05 us
  transfers between devices with their start and end apart: 30 -> 30, of which waited for: 10 -> 9; matrix products, arithmetic and copies ran while one was open for 4% -> 4% of each run, Pallas kernels for 20% -> 20%
where the time goes in v5:
time: 82.2 us; the launch traced here: 81.8 us
  starting transfers between devices  38.4 us (47%)
  Pallas kernels  19.2 us (23%)
  waiting for transfers between devices  15.2 us (18%)
  local copies, waits for them, and re-layouts  5.97 us (7%)
  other arithmetic  1.91 us (2%)
  between operations  1.1 us (1%)
    ppermute x27, starting transfers between devices, swap(): return lax.ppermute(x, 'ctx', [(i, i ^ off) for i in range(parts)])  38.3 us
    pallas_call x19, Pallas kernels, call(): pl.pallas_call(kernel, out_shape=outs, in_specs=([vmem] * count if spaces...  19.2 us
    ppermute x27, waiting for transfers between devices, swap(): return lax.ppermute(x, 'ctx', [(i, i ^ off) for i in range(parts)])  15.1 us
    unnamed x37, local copies, waits for them, and re-layouts  4.05 us
  transfers between devices with their start and end apart: 30, of which 9 were waited for; matrix products, arithmetic and copies ran while one was open for 4% of the time, Pallas kernels for 20%

profile of v5, /device:TPU:0, one launch (start us, length us, event | category | flops | bytes accessed | tf_op | source)
XLA Modules:
  0.0 81.8 jit_solution(10572507144187737603)
XLA Ops:
  1.8 3.0 %collective-permute-start.1 = (bf16[128,2048]{1,0:T(8,128)(2,1)S(1)}, bf16[128,2048]{1,0:T(8,128)(2,1)S(1)}, u32[]{:S(2)}, u32[]{:S(2)}) collective-permute-start(bf16[128,2048]{1,0:T(8,128)(2,1)S(1)} %constant_dynamic-slice_fusion), channel_id=1, source_target_pairs={{0,4},{2,6},{4,0},{6,2},{8,12},{10,14},{12,8},{14,10},{16,20},{18,... | collective-permute-start | bytes 1572872 | tf_op jit(solution)/shard_map/ppermute | solution.py:317
  4.8 1.5 %collective-permute-start = (bf16[128,2048]{1,0:T(8,128)(2,1)S(1)}, bf16[128,2048]{1,0:T(8,128)(2,1)S(1)}, u32[]{:S(2)}, u32[]{:S(2)}) collective-permute-start(bf16[128,2048]{1,0:T(8,128)(2,1)S(1)} %constant_dynamic-slice_fusion), channel_id=1, source_target_pairs={{0,2},{2,0},{4,6},{6,4},{8,10},{10,8},{12,14},{14,12},{16,18},{18,... | collective-permute-start | bytes 1572872 | tf_op jit(solution)/shard_map/ppermute | solution.py:317
  8.6 2.9 %collective-permute-start.4 = (bf16[128,128]{1,0:T(8,128)(2,1)S(1)}, bf16[128,128]{1,0:T(8,128)(2,1)S(1)}, u32[]{:S(2)}, u32[]{:S(2)}) collective-permute-start(bf16[128,128]{1,0:T(8,128)(2,1)S(1)} %get-tuple-element.49), channel_id=1, source_target_pairs={{0,6},{2,4},{4,2},{6,0},{8,14},{10,12},{12,10},{14,8},{16,22},{18,... | collective-permute-start | bytes 98312 | tf_op jit(solution)/shard_map/ppermute | solution.py:317
  12.9 1.6 %shard_map.102 = (f32[256,384]{1,0:T(8,128)S(1)}, f32[272,384]{1,0:T(8,128)S(1)}, f32[272,384]{1,0:T(8,128)S(1)}, f32[272,384]{1,0:T(8,128)S(1)}) custom-call(s32[4]{0:T(128)S(1)} %pad_add_fusion.refs_0_, f32[256,128]{1,0:T(8,128)S(1)} %copy-done.4, f32[256,128]{1,0:T(8,128)S(1)} %copy-done.12, f32[256,128]{1,0:T(8,128)S(1)} %copy-done.13, ...), custom_call_target="tpu_custom_call" | custom-call | bytes 397328 | tf_op jit(solution)/shard_map/pallas_call | solution.py:42
  14.5 4.8 %collective-permute-done.2.refs_6_.refs_1_ = bf16[128,128]{1,0:T(8,128)(2,1)S(1)} collective-permute-done((bf16[128,128]{1,0:T(8,128)(2,1)S(1)}, bf16[128,128]{1,0:T(8,128)(2,1)S(1)}, u32[]{:S(2)}, u32[]{:S(2)}) %collective-permute-start.2) | collective-permute-done | bytes 32800 | tf_op jit(solution)/shard_map/ppermute | solution.py:317
  19.8 2.8 %collective-permute-start.14 = (bf16[512,128]{1,0:T(8,128)(2,1)S(1)}, bf16[512,128]{1,0:T(8,128)(2,1)S(1)}, u32[]{:S(2)}, u32[]{:S(2)}) collective-permute-start(bf16[512,128]{1,0:T(8,128)(2,1)S(1)} %shard_map.110.refs_0_.refs_1_), channel_id=1, source_target_pairs={{0,16},{2,18},{4,20},{6,22},{8,24},{10,26},{12,28},{14,30},{16,0},... | collective-permute-start | bytes 393224 | tf_op jit(solution)/shard_map/ppermute | solution.py:317
  22.7 2.5 %collective-permute-start.8 = (f16[272,384]{1,0:T(8,128)(2,1)S(1)}, f16[272,384]{1,0:T(8,128)(2,1)S(1)}, u32[]{:S(2)}, u32[]{:S(2)}) collective-permute-start(f16[272,384]{1,0:T(8,128)(2,1)S(1)} %convert_element_type.22), channel_id=1, source_target_pairs={{0,6},{2,4},{4,2},{6,0},{8,14},{10,12},{12,10},{14,8},{16,22},{18,... | collective-permute-start | bytes 626696 | tf_op jit(solution)/shard_map/ppermute | solution.py:317
  26.4 3.2 %collective-permute-done.14.refs_1_.refs_2_ = bf16[512,128]{1,0:T(8,128)(2,1)S(1)} collective-permute-done((bf16[512,128]{1,0:T(8,128)(2,1)S(1)}, bf16[512,128]{1,0:T(8,128)(2,1)S(1)}, u32[]{:S(2)}, u32[]{:S(2)}) %collective-permute-start.14) | collective-permute-done | bytes 131104 | tf_op jit(solution)/shard_map/ppermute | solution.py:317
  31.7 3.6 %collective-permute-done.7 = f16[272,384]{1,0:T(8,128)(2,1)S(1)} collective-permute-done((f16[272,384]{1,0:T(8,128)(2,1)S(1)}, f16[272,384]{1,0:T(8,128)(2,1)S(1)}, u32[]{:S(2)}, u32[]{:S(2)}) %collective-permute-start.7) | collective-permute-done | bytes 208928 | tf_op jit(solution)/shard_map/ppermute | solution.py:317
  35.6 1.5 %collective-permute-start.12 = (bf16[64,2048]{1,0:T(8,128)(2,1)S(1)}, bf16[64,2048]{1,0:T(8,128)(2,1)S(1)}, u32[]{:S(2)}, u32[]{:S(2)}) collective-permute-start(bf16[64,2048]{1,0:T(8,128)(2,1)S(1)} %get-tuple-element.57), channel_id=1, source_target_pairs={{0,4},{2,6},{4,0},{6,2},{8,12},{10,14},{12,8},{14,10},{16,20},{18,... | collective-permute-start | bytes 786440 | tf_op jit(solution)/shard_map/ppermute | solution.py:317
  39.0 1.4 %collective-permute-start.11 = (f32[128,128]{1,0:T(8,128)S(1)}, f32[128,128]{1,0:T(8,128)S(1)}, u32[]{:S(2)}, u32[]{:S(2)}) collective-permute-start(f32[128,128]{1,0:T(8,128)S(1)} %get-tuple-element.53), channel_id=1, source_target_pairs={{0,24},{2,26},{4,28},{6,30},{8,16},{10,18},{12,20},{14,22},{16,8},... | collective-permute-start | bytes 196616 | tf_op jit(solution)/shard_map/ppermute | solution.py:317
  40.4 1.7 %collective-permute-start.10 = (f32[128,128]{1,0:T(8,128)S(1)}, f32[128,128]{1,0:T(8,128)S(1)}, u32[]{:S(2)}, u32[]{:S(2)}) collective-permute-start(f32[128,128]{1,0:T(8,128)S(1)} %get-tuple-element.53), channel_id=1, source_target_pairs={{0,16},{2,18},{4,20},{6,22},{8,24},{10,26},{12,28},{14,30},{16,0},... | collective-permute-start | bytes 196616 | tf_op jit(solution)/shard_map/ppermute | solution.py:317
  42.1 1.3 %collective-permute-start.9 = (f32[128,128]{1,0:T(8,128)S(1)}, f32[128,128]{1,0:T(8,128)S(1)}, u32[]{:S(2)}, u32[]{:S(2)}) collective-permute-start(f32[128,128]{1,0:T(8,128)S(1)} %get-tuple-element.53), channel_id=1, source_target_pairs={{0,8},{2,10},{4,12},{6,14},{8,0},{10,2},{12,4},{14,6},{16,24},{18,... | collective-permute-start | bytes 196616 | tf_op jit(solution)/shard_map/ppermute | solution.py:317
  43.5 1.5 %shard_map.106.refs_3_.refs_7_ = f32[1024,128]{1,0:T(8,128)S(1)} custom-call(f32[1024,384]{1,0:T(8,128)S(1)} %get-tuple-element.51.refs_0_.refs_5_), custom_call_target="tpu_custom_call" | custom-call | flops 402653184 | bytes 1572864 | tf_op jit(solution)/shard_map/pallas_call | solution.py:42
  45.0 1.5 %shard_map.112 = (f32[768,128]{1,0:T(8,128)S(1)}, bf16[2048,128]{1,0:T(8,128)(2,1)S(1)}) custom-call(s32[4]{0:T(128)S(1)} %pad_add_fusion.refs_0_, bf16[512,128]{1,0:T(8,128)(2,1)S(1)} %shard_map.110.refs_0_.refs_1_, bf16[512,128]{1,0:T(8,128)(2,1)S(1)} %collective-permute-done.14.refs_1_.refs_2_, bf16[1024,128]{1,0:T(8,128)(2,1)S(1)} %collective-permute-done.15.refs_3_, ...), custom_call_target="tpu_custom_call" | custom-call | flops 536870912 | bytes 3670032 | tf_op jit(solution)/shard_map/pallas_call | solution.py:42
  52.0 2.0 %shard_map.114 = (f32[1024,128]{1,0:T(8,128)S(1)}, f32[512,128]{1,0:T(8,128)S(1)}, f32[128,128]{1,0:T(8,128)S(1)}) custom-call(s32[4]{0:T(128)S(1)} %pad_add_fusion.refs_0_, f32[768,128]{1,0:T(8,128)S(1)} %copy-done.8, bf16[2048,128]{1,0:T(8,128)(2,1)S(1)} %copy-done.6, bf16[128,2048]{1,0:T(8,128)(2,1)} %shard_map.113.refs_3_, ...), custom_call_target="tpu_custom_call" | custom-call | flops 134217728 | bytes 3538960 | tf_op jit(solution)/shard_map/pallas_call | solution.py:42
  56.2 2.3 %collective-permute-start.23 = (f32[128,128]{1,0:T(8,128)S(1)}, f32[128,128]{1,0:T(8,128)S(1)}, u32[]{:S(2)}, u32[]{:S(2)}) collective-permute-start(f32[128,128]{1,0:T(8,128)S(1)} %get-tuple-element.61.refs_5_), channel_id=1, source_target_pairs={{0,8},{2,10},{4,12},{6,14},{8,0},{10,2},{12,4},{14,6},{16,24},{18,... | collective-permute-start | bytes 196616 | tf_op jit(solution)/shard_map/ppermute | solution.py:317
  58.5 1.9 %shard_map.115 = (f32[512,128]{1,0:T(8,128)S(1)}, bf16[512,128]{1,0:T(8,128)(2,1)S(1)}, bf16[512,128]{1,0:T(8,128)(2,1)S(1)}, bf16[512,128]{1,0:T(8,128)(2,1)S(1)}) custom-call(s32[4]{0:T(128)S(1)} %pad_add_fusion.refs_0_, f32[128,2048]{1,0:T(8,128)S(1)} %get-tuple-element.55.refs_1_, bf16[128,256]{1,0:T(8,128)(2,1)S(1)} %get-tuple-element.56.refs_2_, ...), custom_call_target="tpu_custom_call" | custom-call | flops 134217728 | bytes 2162704 | tf_op jit(solution)/shard_map/pallas_call | solution.py:42
  60.4 1.8 %collective-permute-start.18 = (bf16[512,128]{1,0:T(8,128)(2,1)S(1)}, bf16[512,128]{1,0:T(8,128)(2,1)S(1)}, u32[]{:S(2)}, u32[]{:S(2)}) collective-permute-start(bf16[512,128]{1,0:T(8,128)(2,1)S(1)} %get-tuple-element.64), channel_id=1, source_target_pairs={{0,16},{2,18},{4,20},{6,22},{8,24},{10,26},{12,28},{14,30},{16,0},... | collective-permute-start | bytes 393224 | tf_op jit(solution)/shard_map/ppermute | solution.py:317
  62.2 2.7 %shard_map.118 = (f32[1024,128]{1,0:T(8,128)S(1)}, f32[1024,128]{1,0:T(8,128)S(1)}) custom-call(f32[1024,384]{1,0:T(8,128)S(1)} %get-tuple-element.51.refs_0_.refs_5_, f32[1024,128]{1,0:T(8,128)S(1)} %get-tuple-element.71.refs_1_, f32[512,128]{1,0:T(8,128)S(1)} %get-tuple-element.72.refs_2_, f32[512,128]{1,0:T(8,128)S(1)} %get-tuple-element.62.refs_1_.refs_3_), custom_call_target="tpu_custom_call" | custom-call | flops 805306368 | bytes 2359296 | tf_op jit(solution)/shard_map/pallas_call | solution.py:42
  65.0 2.6 %collective-permute-start.19 = (bf16[512,128]{1,0:T(8,128)(2,1)S(1)}, bf16[512,128]{1,0:T(8,128)(2,1)S(1)}, u32[]{:S(2)}, u32[]{:S(2)}) collective-permute-start(bf16[512,128]{1,0:T(8,128)(2,1)S(1)} %get-tuple-element.65), channel_id=1, source_target_pairs={{0,24},{2,26},{4,28},{6,30},{8,16},{10,18},{12,20},{14,22},{16,8},... | collective-permute-start | bytes 393224 | tf_op jit(solution)/shard_map/ppermute | solution.py:317
  69.8 1.8 %collective-permute-start.28 = (bf16[256,256]{1,0:T(8,128)(2,1)S(1)}, bf16[256,256]{1,0:T(8,128)(2,1)S(1)}, u32[]{:S(2)}, u32[]{:S(2)}) collective-permute-start(bf16[256,256]{1,0:T(8,128)(2,1)S(1)} %get-tuple-element.78), channel_id=1, source_target_pairs={{0,6},{2,4},{4,2},{6,0},{8,14},{10,12},{12,10},{14,8},{16,22},{18,... | collective-permute-start | bytes 393224 | tf_op jit(solution)/shard_map/ppermute | solution.py:317
  74.7 1.8 %collective-permute-start.22 = (f32[128,128]{1,0:T(8,128)S(1)}, f32[128,128]{1,0:T(8,128)S(1)}, u32[]{:S(2)}, u32[]{:S(2)}) collective-permute-start(f32[128,128]{1,0:T(8,128)S(1)} %get-tuple-element.69.refs_11_), channel_id=1, source_target_pairs={{0,6},{2,4},{4,2},{6,0},{8,14},{10,12},{12,10},{14,8},{16,22},{18,... | collective-permute-start | bytes 196616 | tf_op jit(solution)/shard_map/ppermute | solution.py:317
  77.3 1.7 %shard_map.120 = (f32[256,128]{1,0:T(8,128)}, f32[256,128]{1,0:T(8,128)}, f32[2,256]{1,0:T(2,128)S(1)}) custom-call(s32[4]{0:T(128)S(1)} %pad_add_fusion.refs_0_, f32[256,128]{1,0:T(8,128)S(1)} %copy-done.4, s32[2,256]{1,0:T(2,128)S(1)} %bitcast.14, f32[2,256]{1,0:T(2,128)S(1)} %bitcast.16, f32[256,256]{1,0:T(8,128)S(1)} %get-tuple-element.75.refs_4_, ...), custom_call_target="tpu_custom_call" | custom-call | bytes 790544 | tf_op jit(solution)/shard_map/pallas_call | solution.py:42
  (105 shorter events, 27.1 us)
Async XLA Ops:
  1.8 17.6 %collective-permute-start.1 = (bf16[128,2048]{1,0:T(8,128)(2,1)S(1)}, bf16[128,2048]{1,0:T(8,128)(2,1)S(1)}, u32[]{:S(2)}, u32[]{:S(2)}) collective-permute-start(bf16[128,2048]{1,0:T(8,128)(2,1)S(1)} %constant_dynamic-slice_fusion), channel_id=1, source_target_pairs={{0,4},{2,6},{4,0},{6,2},{8,12},{10,14},{12,8},{14,10},{16,20},{18,... | collective-permute-start | bytes 1572872 | tf_op jit(solution)/shard_map/ppermute | solution.py:317
  4.8 14.6 %collective-permute-start = (bf16[128,2048]{1,0:T(8,128)(2,1)S(1)}, bf16[128,2048]{1,0:T(8,128)(2,1)S(1)}, u32[]{:S(2)}, u32[]{:S(2)}) collective-permute-start(bf16[128,2048]{1,0:T(8,128)(2,1)S(1)} %constant_dynamic-slice_fusion), channel_id=1, source_target_pairs={{0,2},{2,0},{4,6},{6,4},{8,10},{10,8},{12,14},{14,12},{16,18},{18,... | collective-permute-start | bytes 1572872 | tf_op jit(solution)/shard_map/ppermute | solution.py:317
  7.9 11.3 %collective-permute-start.2 = (bf16[128,128]{1,0:T(8,128)(2,1)S(1)}, bf16[128,128]{1,0:T(8,128)(2,1)S(1)}, u32[]{:S(2)}, u32[]{:S(2)}) collective-permute-start(bf16[128,128]{1,0:T(8,128)(2,1)S(1)} %get-tuple-element.47), channel_id=1, source_target_pairs={{0,2},{2,0},{4,6},{6,4},{8,10},{10,8},{12,14},{14,12},{16,18},{18,... | collective-permute-start | bytes 98312 | tf_op jit(solution)/shard_map/ppermute | solution.py:317
  8.5 10.7 %collective-permute-start.3 = (bf16[128,128]{1,0:T(8,128)(2,1)S(1)}, bf16[128,128]{1,0:T(8,128)(2,1)S(1)}, u32[]{:S(2)}, u32[]{:S(2)}) collective-permute-start(bf16[128,128]{1,0:T(8,128)(2,1)S(1)} %get-tuple-element.48), channel_id=1, source_target_pairs={{0,4},{2,6},{4,0},{6,2},{8,12},{10,14},{12,8},{14,10},{16,20},{18,... | collective-permute-start | bytes 98312 | tf_op jit(solution)/shard_map/ppermute | solution.py:317
  8.6 10.8 %collective-permute-start.4 = (bf16[128,128]{1,0:T(8,128)(2,1)S(1)}, bf16[128,128]{1,0:T(8,128)(2,1)S(1)}, u32[]{:S(2)}, u32[]{:S(2)}) collective-permute-start(bf16[128,128]{1,0:T(8,128)(2,1)S(1)} %get-tuple-element.49), channel_id=1, source_target_pairs={{0,6},{2,4},{4,2},{6,0},{8,14},{10,12},{12,10},{14,8},{16,22},{18,... | collective-permute-start | bytes 98312 | tf_op jit(solution)/shard_map/ppermute | solution.py:317
  19.5 16.0 %collective-permute-start.5 = (bf16[256,2048]{1,0:T(8,128)(2,1)S(1)}, bf16[256,2048]{1,0:T(8,128)(2,1)S(1)}, u32[]{:S(2)}, u32[]{:S(2)}) collective-permute-start(bf16[256,2048]{1,0:T(8,128)(2,1)S(1)} %shard_map.104.refs_2_.refs_5_), channel_id=1, source_target_pairs={{0,1},{1,0},{2,3},{3,2},{4,5},{5,4},{6,7},{7,6},{8,9},{9,8},{10,11... | collective-permute-start | bytes 3145736 | tf_op jit(solution)/shard_map/ppermute | solution.py:321
  19.8 9.7 %collective-permute-start.14 = (bf16[512,128]{1,0:T(8,128)(2,1)S(1)}, bf16[512,128]{1,0:T(8,128)(2,1)S(1)}, u32[]{:S(2)}, u32[]{:S(2)}) collective-permute-start(bf16[512,128]{1,0:T(8,128)(2,1)S(1)} %shard_map.110.refs_0_.refs_1_), channel_id=1, source_target_pairs={{0,16},{2,18},{4,20},{6,22},{8,24},{10,26},{12,28},{14,30},{16,0},... | collective-permute-start | bytes 393224 | tf_op jit(solution)/shard_map/ppermute | solution.py:317
  22.7 9.0 %collective-permute-start.8 = (f16[272,384]{1,0:T(8,128)(2,1)S(1)}, f16[272,384]{1,0:T(8,128)(2,1)S(1)}, u32[]{:S(2)}, u32[]{:S(2)}) collective-permute-start(f16[272,384]{1,0:T(8,128)(2,1)S(1)} %convert_element_type.22), channel_id=1, source_target_pairs={{0,6},{2,4},{4,2},{6,0},{8,14},{10,12},{12,10},{14,8},{16,22},{18,... | collective-permute-start | bytes 626696 | tf_op jit(solution)/shard_map/ppermute | solution.py:317
  25.2 10.1 %collective-permute-start.7 = (f16[272,384]{1,0:T(8,128)(2,1)S(1)}, f16[272,384]{1,0:T(8,128)(2,1)S(1)}, u32[]{:S(2)}, u32[]{:S(2)}) collective-permute-start(f16[272,384]{1,0:T(8,128)(2,1)S(1)} %convert_element_type.20), channel_id=1, source_target_pairs={{0,4},{2,6},{4,0},{6,2},{8,12},{10,14},{12,8},{14,10},{16,20},{18,... | collective-permute-start | bytes 626696 | tf_op jit(solution)/shard_map/ppermute | solution.py:317
  25.8 9.6 %collective-permute-start.6 = (f16[272,384]{1,0:T(8,128)(2,1)S(1)}, f16[272,384]{1,0:T(8,128)(2,1)S(1)}, u32[]{:S(2)}, u32[]{:S(2)}) collective-permute-start(f16[272,384]{1,0:T(8,128)(2,1)S(1)} %convert_element_type.18), channel_id=1, source_target_pairs={{0,2},{2,0},{4,6},{6,4},{8,10},{10,8},{12,14},{14,12},{16,18},{18,... | collective-permute-start | bytes 626696 | tf_op jit(solution)/shard_map/ppermute | solution.py:317
  29.9 12.2 %collective-permute-start.15 = (bf16[1024,128]{1,0:T(8,128)(2,1)S(1)}, bf16[1024,128]{1,0:T(8,128)(2,1)S(1)}, u32[]{:S(2)}, u32[]{:S(2)}) collective-permute-start(bf16[1024,128]{1,0:T(8,128)(2,1)S(1)} %shard_map.111), channel_id=1, source_target_pairs={{0,8},{2,10},{4,12},{6,14},{8,0},{10,2},{12,4},{14,6},{16,24},{18,... | collective-permute-start | bytes 786440 | tf_op jit(solution)/shard_map/ppermute | solution.py:317
  35.6 12.6 %collective-permute-start.12 = (bf16[64,2048]{1,0:T(8,128)(2,1)S(1)}, bf16[64,2048]{1,0:T(8,128)(2,1)S(1)}, u32[]{:S(2)}, u32[]{:S(2)}) collective-permute-start(bf16[64,2048]{1,0:T(8,128)(2,1)S(1)} %get-tuple-element.57), channel_id=1, source_target_pairs={{0,4},{2,6},{4,0},{6,2},{8,12},{10,14},{12,8},{14,10},{16,20},{18,... | collective-permute-start | bytes 786440 | tf_op jit(solution)/shard_map/ppermute | solution.py:317
  37.1 11.1 %collective-permute-start.13 = (bf16[64,2048]{1,0:T(8,128)(2,1)S(1)}, bf16[64,2048]{1,0:T(8,128)(2,1)S(1)}, u32[]{:S(2)}, u32[]{:S(2)}) collective-permute-start(bf16[64,2048]{1,0:T(8,128)(2,1)S(1)} %get-tuple-element.58), channel_id=1, source_target_pairs={{0,2},{2,0},{4,6},{6,4},{8,10},{10,8},{12,14},{14,12},{16,18},{18,... | collective-permute-start | bytes 786440 | tf_op jit(solution)/shard_map/ppermute | solution.py:317
  39.0 9.1 %collective-permute-start.11 = (f32[128,128]{1,0:T(8,128)S(1)}, f32[128,128]{1,0:T(8,128)S(1)}, u32[]{:S(2)}, u32[]{:S(2)}) collective-permute-start(f32[128,128]{1,0:T(8,128)S(1)} %get-tuple-element.53), channel_id=1, source_target_pairs={{0,24},{2,26},{4,28},{6,30},{8,16},{10,18},{12,20},{14,22},{16,8},... | collective-permute-start | bytes 196616 | tf_op jit(solution)/shard_map/ppermute | solution.py:317
  40.4 7.7 %collective-permute-start.10 = (f32[128,128]{1,0:T(8,128)S(1)}, f32[128,128]{1,0:T(8,128)S(1)}, u32[]{:S(2)}, u32[]{:S(2)}) collective-permute-start(f32[128,128]{1,0:T(8,128)S(1)} %get-tuple-element.53), channel_id=1, source_target_pairs={{0,16},{2,18},{4,20},{6,22},{8,24},{10,26},{12,28},{14,30},{16,0},... | collective-permute-start | bytes 196616 | tf_op jit(solution)/shard_map/ppermute | solution.py:317
  54.0 10.9 %collective-permute-start.25 = (f32[128,128]{1,0:T(8,128)S(1)}, f32[128,128]{1,0:T(8,128)S(1)}, u32[]{:S(2)}, u32[]{:S(2)}) collective-permute-start(f32[128,128]{1,0:T(8,128)S(1)} %get-tuple-element.61.refs_5_), channel_id=1, source_target_pairs={{0,24},{2,26},{4,28},{6,30},{8,16},{10,18},{12,20},{14,22},{16,8},... | collective-permute-start | bytes 196616 | tf_op jit(solution)/shard_map/ppermute | solution.py:317
  55.4 12.3 %collective-permute-start.24 = (f32[128,128]{1,0:T(8,128)S(1)}, f32[128,128]{1,0:T(8,128)S(1)}, u32[]{:S(2)}, u32[]{:S(2)}) collective-permute-start(f32[128,128]{1,0:T(8,128)S(1)} %get-tuple-element.61.refs_5_), channel_id=1, source_target_pairs={{0,16},{2,18},{4,20},{6,22},{8,24},{10,26},{12,28},{14,30},{16,0},... | collective-permute-start | bytes 196616 | tf_op jit(solution)/shard_map/ppermute | solution.py:317
  56.2 11.4 %collective-permute-start.23 = (f32[128,128]{1,0:T(8,128)S(1)}, f32[128,128]{1,0:T(8,128)S(1)}, u32[]{:S(2)}, u32[]{:S(2)}) collective-permute-start(f32[128,128]{1,0:T(8,128)S(1)} %get-tuple-element.61.refs_5_), channel_id=1, source_target_pairs={{0,8},{2,10},{4,12},{6,14},{8,0},{10,2},{12,4},{14,6},{16,24},{18,... | collective-permute-start | bytes 196616 | tf_op jit(solution)/shard_map/ppermute | solution.py:317
  60.4 9.4 %collective-permute-start.17 = (bf16[512,128]{1,0:T(8,128)(2,1)S(1)}, bf16[512,128]{1,0:T(8,128)(2,1)S(1)}, u32[]{:S(2)}, u32[]{:S(2)}) collective-permute-start(bf16[512,128]{1,0:T(8,128)(2,1)S(1)} %get-tuple-element.63), channel_id=1, source_target_pairs={{0,8},{2,10},{4,12},{6,14},{8,0},{10,2},{12,4},{14,6},{16,24},{18,... | collective-permute-start | bytes 393224 | tf_op jit(solution)/shard_map/ppermute | solution.py:317
  60.4 11.9 %collective-permute-start.18 = (bf16[512,128]{1,0:T(8,128)(2,1)S(1)}, bf16[512,128]{1,0:T(8,128)(2,1)S(1)}, u32[]{:S(2)}, u32[]{:S(2)}) collective-permute-start(bf16[512,128]{1,0:T(8,128)(2,1)S(1)} %get-tuple-element.64), channel_id=1, source_target_pairs={{0,16},{2,18},{4,20},{6,22},{8,24},{10,26},{12,28},{14,30},{16,0},... | collective-permute-start | bytes 393224 | tf_op jit(solution)/shard_map/ppermute | solution.py:317
  65.0 7.3 %collective-permute-start.19 = (bf16[512,128]{1,0:T(8,128)(2,1)S(1)}, bf16[512,128]{1,0:T(8,128)(2,1)S(1)}, u32[]{:S(2)}, u32[]{:S(2)}) collective-permute-start(bf16[512,128]{1,0:T(8,128)(2,1)S(1)} %get-tuple-element.65), channel_id=1, source_target_pairs={{0,24},{2,26},{4,28},{6,30},{8,16},{10,18},{12,20},{14,22},{16,8},... | collective-permute-start | bytes 393224 | tf_op jit(solution)/shard_map/ppermute | solution.py:317
  68.0 6.7 %collective-permute-start.26 = (bf16[256,256]{1,0:T(8,128)(2,1)S(1)}, bf16[256,256]{1,0:T(8,128)(2,1)S(1)}, u32[]{:S(2)}, u32[]{:S(2)}) collective-permute-start(bf16[256,256]{1,0:T(8,128)(2,1)S(1)} %get-tuple-element.76), channel_id=1, source_target_pairs={{0,2},{2,0},{4,6},{6,4},{8,10},{10,8},{12,14},{14,12},{16,18},{18,... | collective-permute-start | bytes 393224 | tf_op jit(solution)/shard_map/ppermute | solution.py:317
  69.2 7.3 %collective-permute-start.27 = (bf16[256,256]{1,0:T(8,128)(2,1)S(1)}, bf16[256,256]{1,0:T(8,128)(2,1)S(1)}, u32[]{:S(2)}, u32[]{:S(2)}) collective-permute-start(bf16[256,256]{1,0:T(8,128)(2,1)S(1)} %get-tuple-element.77), channel_id=1, source_target_pairs={{0,4},{2,6},{4,0},{6,2},{8,12},{10,14},{12,8},{14,10},{16,20},{18,... | collective-permute-start | bytes 393224 | tf_op jit(solution)/shard_map/ppermute | solution.py:317
  69.8 7.5 %collective-permute-start.28 = (bf16[256,256]{1,0:T(8,128)(2,1)S(1)}, bf16[256,256]{1,0:T(8,128)(2,1)S(1)}, u32[]{:S(2)}, u32[]{:S(2)}) collective-permute-start(bf16[256,256]{1,0:T(8,128)(2,1)S(1)} %get-tuple-element.78), channel_id=1, source_target_pairs={{0,6},{2,4},{4,2},{6,0},{8,14},{10,12},{12,10},{14,8},{16,22},{18,... | collective-permute-start | bytes 393224 | tf_op jit(solution)/shard_map/ppermute | solution.py:317
  (24 other events, 121.8 us)

commit v6 on v5

--- a/solution.py
+++ b/solution.py
@@ -391,7 +391,7 @@
         + [pltpu.SemaphoreType.DMA((5,))],
     )
     coded = [x.astype(F16) for x in sent[1:]]
-    got = [swap(x, off, parts).astype(F32) for off, x in zip((1, 2, 3), coded)]
+    got = [swap(x, off, parts).astype(F32) for off, x in zip((3, 2, 1), coded[::-1])][::-1]
 
     neighbours = stack(from_x, from_y, waits=(*sent[1:], *weights))
     neighbours_other = other_core(neighbours)
@@ -508,7 +508,7 @@
     query_grad, value_grad, gate_part = call(
         functools.partial(at_home, scale),
         [shape(count, head_dim), shape(count, head_dim), shape(routing.shape[1], count)],
-        at, queries, routing.T, gates.T, sent[0], *[swap(sent[off], off, parts) for off in (1, 2, 3)],
+        at, queries, routing.T, gates.T, sent[0], *[swap(sent[off], off, parts) for off in (3, 2, 1)][::-1],
         spaces=[smem] + [vmem] * 7,
         waits=mine,
     )

time: 82.2 us -> 82.2 us (level)
  no operation moved by 1% of the time
where the time goes in v6:
time: 82.2 us; the launch traced here: 81.8 us
  starting transfers between devices  38.4 us (47%)
  Pallas kernels  19.2 us (23%)
  waiting for transfers between devices  15.2 us (18%)
  local copies, waits for them, and re-layouts  5.97 us (7%)
  other arithmetic  1.91 us (2%)
  between operations  1.1 us (1%)
    ppermute x27, starting transfers between devices, swap(): return lax.ppermute(x, 'ctx', [(i, i ^ off) for i in range(parts)])  38.3 us
    pallas_call x19, Pallas kernels, call(): pl.pallas_call(kernel, out_shape=outs, in_specs=([vmem] * count if spaces...  19.2 us
    ppermute x27, waiting for transfers between devices, swap(): return lax.ppermute(x, 'ctx', [(i, i ^ off) for i in range(parts)])  15.1 us
    unnamed x37, local copies, waits for them, and re-layouts  4.05 us
  transfers between devices with their start and end apart: 30, of which 9 were waited for; matrix products, arithmetic and copies ran while one was open for 4% of the time, Pallas kernels for 20%

profile of v6, /device:TPU:0, one launch (start us, length us, event | category | flops | bytes accessed | tf_op | source)
XLA Modules:
  0.0 81.8 jit_solution(10572507144187737603)
XLA Ops:
  1.8 3.0 %collective-permute-start.1 = (bf16[128,2048]{1,0:T(8,128)(2,1)S(1)}, bf16[128,2048]{1,0:T(8,128)(2,1)S(1)}, u32[]{:S(2)}, u32[]{:S(2)}) collective-permute-start(bf16[128,2048]{1,0:T(8,128)(2,1)S(1)} %constant_dynamic-slice_fusion), channel_id=1, source_target_pairs={{0,4},{2,6},{4,0},{6,2},{8,12},{10,14},{12,8},{14,10},{16,20},{18,... | collective-permute-start | bytes 1572872 | tf_op jit(solution)/shard_map/ppermute | solution.py:317
  4.8 1.5 %collective-permute-start = (bf16[128,2048]{1,0:T(8,128)(2,1)S(1)}, bf16[128,2048]{1,0:T(8,128)(2,1)S(1)}, u32[]{:S(2)}, u32[]{:S(2)}) collective-permute-start(bf16[128,2048]{1,0:T(8,128)(2,1)S(1)} %constant_dynamic-slice_fusion), channel_id=1, source_target_pairs={{0,2},{2,0},{4,6},{6,4},{8,10},{10,8},{12,14},{14,12},{16,18},{18,... | collective-permute-start | bytes 1572872 | tf_op jit(solution)/shard_map/ppermute | solution.py:317
  8.6 2.9 %collective-permute-start.4 = (bf16[128,128]{1,0:T(8,128)(2,1)S(1)}, bf16[128,128]{1,0:T(8,128)(2,1)S(1)}, u32[]{:S(2)}, u32[]{:S(2)}) collective-permute-start(bf16[128,128]{1,0:T(8,128)(2,1)S(1)} %get-tuple-element.49), channel_id=1, source_target_pairs={{0,6},{2,4},{4,2},{6,0},{8,14},{10,12},{12,10},{14,8},{16,22},{18,... | collective-permute-start | bytes 98312 | tf_op jit(solution)/shard_map/ppermute | solution.py:317
  12.9 1.6 %shard_map.102 = (f32[256,384]{1,0:T(8,128)S(1)}, f32[272,384]{1,0:T(8,128)S(1)}, f32[272,384]{1,0:T(8,128)S(1)}, f32[272,384]{1,0:T(8,128)S(1)}) custom-call(s32[4]{0:T(128)S(1)} %pad_add_fusion.refs_0_, f32[256,128]{1,0:T(8,128)S(1)} %copy-done.4, f32[256,128]{1,0:T(8,128)S(1)} %copy-done.12, f32[256,128]{1,0:T(8,128)S(1)} %copy-done.13, ...), custom_call_target="tpu_custom_call" | custom-call | bytes 397328 | tf_op jit(solution)/shard_map/pallas_call | solution.py:42
  14.5 4.8 %collective-permute-done.2.refs_6_.refs_1_ = bf16[128,128]{1,0:T(8,128)(2,1)S(1)} collective-permute-done((bf16[128,128]{1,0:T(8,128)(2,1)S(1)}, bf16[128,128]{1,0:T(8,128)(2,1)S(1)}, u32[]{:S(2)}, u32[]{:S(2)}) %collective-permute-start.2) | collective-permute-done | bytes 32800 | tf_op jit(solution)/shard_map/ppermute | solution.py:317
  19.8 2.8 %collective-permute-start.14 = (bf16[512,128]{1,0:T(8,128)(2,1)S(1)}, bf16[512,128]{1,0:T(8,128)(2,1)S(1)}, u32[]{:S(2)}, u32[]{:S(2)}) collective-permute-start(bf16[512,128]{1,0:T(8,128)(2,1)S(1)} %shard_map.110.refs_0_.refs_1_), channel_id=1, source_target_pairs={{0,16},{2,18},{4,20},{6,22},{8,24},{10,26},{12,28},{14,30},{16,0},... | collective-permute-start | bytes 393224 | tf_op jit(solution)/shard_map/ppermute | solution.py:317
  22.7 2.5 %collective-permute-start.8 = (f16[272,384]{1,0:T(8,128)(2,1)S(1)}, f16[272,384]{1,0:T(8,128)(2,1)S(1)}, u32[]{:S(2)}, u32[]{:S(2)}) collective-permute-start(f16[272,384]{1,0:T(8,128)(2,1)S(1)} %convert_element_type.22), channel_id=1, source_target_pairs={{0,6},{2,4},{4,2},{6,0},{8,14},{10,12},{12,10},{14,8},{16,22},{18,... | collective-permute-start | bytes 626696 | tf_op jit(solution)/shard_map/ppermute | solution.py:317
  26.4 3.2 %collective-permute-done.14.refs_1_.refs_2_ = bf16[512,128]{1,0:T(8,128)(2,1)S(1)} collective-permute-done((bf16[512,128]{1,0:T(8,128)(2,1)S(1)}, bf16[512,128]{1,0:T(8,128)(2,1)S(1)}, u32[]{:S(2)}, u32[]{:S(2)}) %collective-permute-start.14) | collective-permute-done | bytes 131104 | tf_op jit(solution)/shard_map/ppermute | solution.py:317
  31.7 3.6 %collective-permute-done.7 = f16[272,384]{1,0:T(8,128)(2,1)S(1)} collective-permute-done((f16[272,384]{1,0:T(8,128)(2,1)S(1)}, f16[272,384]{1,0:T(8,128)(2,1)S(1)}, u32[]{:S(2)}, u32[]{:S(2)}) %collective-permute-start.7) | collective-permute-done | bytes 208928 | tf_op jit(solution)/shard_map/ppermute | solution.py:317
  35.6 1.5 %collective-permute-start.12 = (bf16[64,2048]{1,0:T(8,128)(2,1)S(1)}, bf16[64,2048]{1,0:T(8,128)(2,1)S(1)}, u32[]{:S(2)}, u32[]{:S(2)}) collective-permute-start(bf16[64,2048]{1,0:T(8,128)(2,1)S(1)} %get-tuple-element.57), channel_id=1, source_target_pairs={{0,4},{2,6},{4,0},{6,2},{8,12},{10,14},{12,8},{14,10},{16,20},{18,... | collective-permute-start | bytes 786440 | tf_op jit(solution)/shard_map/ppermute | solution.py:317
  39.0 1.4 %collective-permute-start.11 = (f32[128,128]{1,0:T(8,128)S(1)}, f32[128,128]{1,0:T(8,128)S(1)}, u32[]{:S(2)}, u32[]{:S(2)}) collective-permute-start(f32[128,128]{1,0:T(8,128)S(1)} %get-tuple-element.53), channel_id=1, source_target_pairs={{0,24},{2,26},{4,28},{6,30},{8,16},{10,18},{12,20},{14,22},{16,8},... | collective-permute-start | bytes 196616 | tf_op jit(solution)/shard_map/ppermute | solution.py:317
  40.4 1.7 %collective-permute-start.10 = (f32[128,128]{1,0:T(8,128)S(1)}, f32[128,128]{1,0:T(8,128)S(1)}, u32[]{:S(2)}, u32[]{:S(2)}) collective-permute-start(f32[128,128]{1,0:T(8,128)S(1)} %get-tuple-element.53), channel_id=1, source_target_pairs={{0,16},{2,18},{4,20},{6,22},{8,24},{10,26},{12,28},{14,30},{16,0},... | collective-permute-start | bytes 196616 | tf_op jit(solution)/shard_map/ppermute | solution.py:317
  42.1 1.3 %collective-permute-start.9 = (f32[128,128]{1,0:T(8,128)S(1)}, f32[128,128]{1,0:T(8,128)S(1)}, u32[]{:S(2)}, u32[]{:S(2)}) collective-permute-start(f32[128,128]{1,0:T(8,128)S(1)} %get-tuple-element.53), channel_id=1, source_target_pairs={{0,8},{2,10},{4,12},{6,14},{8,0},{10,2},{12,4},{14,6},{16,24},{18,... | collective-permute-start | bytes 196616 | tf_op jit(solution)/shard_map/ppermute | solution.py:317
  43.5 1.5 %shard_map.106.refs_3_.refs_7_ = f32[1024,128]{1,0:T(8,128)S(1)} custom-call(f32[1024,384]{1,0:T(8,128)S(1)} %get-tuple-element.51.refs_0_.refs_5_), custom_call_target="tpu_custom_call" | custom-call | flops 402653184 | bytes 1572864 | tf_op jit(solution)/shard_map/pallas_call | solution.py:42
  45.0 1.5 %shard_map.112 = (f32[768,128]{1,0:T(8,128)S(1)}, bf16[2048,128]{1,0:T(8,128)(2,1)S(1)}) custom-call(s32[4]{0:T(128)S(1)} %pad_add_fusion.refs_0_, bf16[512,128]{1,0:T(8,128)(2,1)S(1)} %shard_map.110.refs_0_.refs_1_, bf16[512,128]{1,0:T(8,128)(2,1)S(1)} %collective-permute-done.14.refs_1_.refs_2_, bf16[1024,128]{1,0:T(8,128)(2,1)S(1)} %collective-permute-done.15.refs_3_, ...), custom_call_target="tpu_custom_call" | custom-call | flops 536870912 | bytes 3670032 | tf_op jit(solution)/shard_map/pallas_call | solution.py:42
  52.0 2.0 %shard_map.114 = (f32[1024,128]{1,0:T(8,128)S(1)}, f32[512,128]{1,0:T(8,128)S(1)}, f32[128,128]{1,0:T(8,128)S(1)}) custom-call(s32[4]{0:T(128)S(1)} %pad_add_fusion.refs_0_, f32[768,128]{1,0:T(8,128)S(1)} %copy-done.8, bf16[2048,128]{1,0:T(8,128)(2,1)S(1)} %copy-done.6, bf16[128,2048]{1,0:T(8,128)(2,1)} %shard_map.113.refs_3_, ...), custom_call_target="tpu_custom_call" | custom-call | flops 134217728 | bytes 3538960 | tf_op jit(solution)/shard_map/pallas_call | solution.py:42
  56.2 2.3 %collective-permute-start.23 = (f32[128,128]{1,0:T(8,128)S(1)}, f32[128,128]{1,0:T(8,128)S(1)}, u32[]{:S(2)}, u32[]{:S(2)}) collective-permute-start(f32[128,128]{1,0:T(8,128)S(1)} %get-tuple-element.61.refs_5_), channel_id=1, source_target_pairs={{0,8},{2,10},{4,12},{6,14},{8,0},{10,2},{12,4},{14,6},{16,24},{18,... | collective-permute-start | bytes 196616 | tf_op jit(solution)/shard_map/ppermute | solution.py:317
  58.5 1.9 %shard_map.115 = (f32[512,128]{1,0:T(8,128)S(1)}, bf16[512,128]{1,0:T(8,128)(2,1)S(1)}, bf16[512,128]{1,0:T(8,128)(2,1)S(1)}, bf16[512,128]{1,0:T(8,128)(2,1)S(1)}) custom-call(s32[4]{0:T(128)S(1)} %pad_add_fusion.refs_0_, f32[128,2048]{1,0:T(8,128)S(1)} %get-tuple-element.55.refs_1_, bf16[128,256]{1,0:T(8,128)(2,1)S(1)} %get-tuple-element.56.refs_2_, ...), custom_call_target="tpu_custom_call" | custom-call | flops 134217728 | bytes 2162704 | tf_op jit(solution)/shard_map/pallas_call | solution.py:42
  60.4 1.8 %collective-permute-start.18 = (bf16[512,128]{1,0:T(8,128)(2,1)S(1)}, bf16[512,128]{1,0:T(8,128)(2,1)S(1)}, u32[]{:S(2)}, u32[]{:S(2)}) collective-permute-start(bf16[512,128]{1,0:T(8,128)(2,1)S(1)} %get-tuple-element.64), channel_id=1, source_target_pairs={{0,16},{2,18},{4,20},{6,22},{8,24},{10,26},{12,28},{14,30},{16,0},... | collective-permute-start | bytes 393224 | tf_op jit(solution)/shard_map/ppermute | solution.py:317
  62.2 2.7 %shard_map.118 = (f32[1024,128]{1,0:T(8,128)S(1)}, f32[1024,128]{1,0:T(8,128)S(1)}) custom-call(f32[1024,384]{1,0:T(8,128)S(1)} %get-tuple-element.51.refs_0_.refs_5_, f32[1024,128]{1,0:T(8,128)S(1)} %get-tuple-element.71.refs_1_, f32[512,128]{1,0:T(8,128)S(1)} %get-tuple-element.72.refs_2_, f32[512,128]{1,0:T(8,128)S(1)} %get-tuple-element.62.refs_1_.refs_3_), custom_call_target="tpu_custom_call" | custom-call | flops 805306368 | bytes 2359296 | tf_op jit(solution)/shard_map/pallas_call | solution.py:42
  65.0 2.6 %collective-permute-start.19 = (bf16[512,128]{1,0:T(8,128)(2,1)S(1)}, bf16[512,128]{1,0:T(8,128)(2,1)S(1)}, u32[]{:S(2)}, u32[]{:S(2)}) collective-permute-start(bf16[512,128]{1,0:T(8,128)(2,1)S(1)} %get-tuple-element.65), channel_id=1, source_target_pairs={{0,24},{2,26},{4,28},{6,30},{8,16},{10,18},{12,20},{14,22},{16,8},... | collective-permute-start | bytes 393224 | tf_op jit(solution)/shard_map/ppermute | solution.py:317
  69.8 1.8 %collective-permute-start.28 = (bf16[256,256]{1,0:T(8,128)(2,1)S(1)}, bf16[256,256]{1,0:T(8,128)(2,1)S(1)}, u32[]{:S(2)}, u32[]{:S(2)}) collective-permute-start(bf16[256,256]{1,0:T(8,128)(2,1)S(1)} %get-tuple-element.78), channel_id=1, source_target_pairs={{0,6},{2,4},{4,2},{6,0},{8,14},{10,12},{12,10},{14,8},{16,22},{18,... | collective-permute-start | bytes 393224 | tf_op jit(solution)/shard_map/ppermute | solution.py:317
  74.7 1.8 %collective-permute-start.22 = (f32[128,128]{1,0:T(8,128)S(1)}, f32[128,128]{1,0:T(8,128)S(1)}, u32[]{:S(2)}, u32[]{:S(2)}) collective-permute-start(f32[128,128]{1,0:T(8,128)S(1)} %get-tuple-element.69.refs_11_), channel_id=1, source_target_pairs={{0,6},{2,4},{4,2},{6,0},{8,14},{10,12},{12,10},{14,8},{16,22},{18,... | collective-permute-start | bytes 196616 | tf_op jit(solution)/shard_map/ppermute | solution.py:317
  77.3 1.7 %shard_map.120 = (f32[256,128]{1,0:T(8,128)}, f32[256,128]{1,0:T(8,128)}, f32[2,256]{1,0:T(2,128)S(1)}) custom-call(s32[4]{0:T(128)S(1)} %pad_add_fusion.refs_0_, f32[256,128]{1,0:T(8,128)S(1)} %copy-done.4, s32[2,256]{1,0:T(2,128)S(1)} %bitcast.14, f32[2,256]{1,0:T(2,128)S(1)} %bitcast.16, f32[256,256]{1,0:T(8,128)S(1)} %get-tuple-element.75.refs_4_, ...), custom_call_target="tpu_custom_call" | custom-call | bytes 790544 | tf_op jit(solution)/shard_map/pallas_call | solution.py:42
  (105 shorter events, 27.1 us)
Async XLA Ops:
  1.8 17.6 %collective-permute-start.1 = (bf16[128,2048]{1,0:T(8,128)(2,1)S(1)}, bf16[128,2048]{1,0:T(8,128)(2,1)S(1)}, u32[]{:S(2)}, u32[]{:S(2)}) collective-permute-start(bf16[128,2048]{1,0:T(8,128)(2,1)S(1)} %constant_dynamic-slice_fusion), channel_id=1, source_target_pairs={{0,4},{2,6},{4,0},{6,2},{8,12},{10,14},{12,8},{14,10},{16,20},{18,... | collective-permute-start | bytes 1572872 | tf_op jit(solution)/shard_map/ppermute | solution.py:317
  4.8 14.6 %collective-permute-start = (bf16[128,2048]{1,0:T(8,128)(2,1)S(1)}, bf16[128,2048]{1,0:T(8,128)(2,1)S(1)}, u32[]{:S(2)}, u32[]{:S(2)}) collective-permute-start(bf16[128,2048]{1,0:T(8,128)(2,1)S(1)} %constant_dynamic-slice_fusion), channel_id=1, source_target_pairs={{0,2},{2,0},{4,6},{6,4},{8,10},{10,8},{12,14},{14,12},{16,18},{18,... | collective-permute-start | bytes 1572872 | tf_op jit(solution)/shard_map/ppermute | solution.py:317
  7.9 11.3 %collective-permute-start.2 = (bf16[128,128]{1,0:T(8,128)(2,1)S(1)}, bf16[128,128]{1,0:T(8,128)(2,1)S(1)}, u32[]{:S(2)}, u32[]{:S(2)}) collective-permute-start(bf16[128,128]{1,0:T(8,128)(2,1)S(1)} %get-tuple-element.47), channel_id=1, source_target_pairs={{0,2},{2,0},{4,6},{6,4},{8,10},{10,8},{12,14},{14,12},{16,18},{18,... | collective-permute-start | bytes 98312 | tf_op jit(solution)/shard_map/ppermute | solution.py:317
  8.5 10.7 %collective-permute-start.3 = (bf16[128,128]{1,0:T(8,128)(2,1)S(1)}, bf16[128,128]{1,0:T(8,128)(2,1)S(1)}, u32[]{:S(2)}, u32[]{:S(2)}) collective-permute-start(bf16[128,128]{1,0:T(8,128)(2,1)S(1)} %get-tuple-element.48), channel_id=1, source_target_pairs={{0,4},{2,6},{4,0},{6,2},{8,12},{10,14},{12,8},{14,10},{16,20},{18,... | collective-permute-start | bytes 98312 | tf_op jit(solution)/shard_map/ppermute | solution.py:317
  8.6 10.8 %collective-permute-start.4 = (bf16[128,128]{1,0:T(8,128)(2,1)S(1)}, bf16[128,128]{1,0:T(8,128)(2,1)S(1)}, u32[]{:S(2)}, u32[]{:S(2)}) collective-permute-start(bf16[128,128]{1,0:T(8,128)(2,1)S(1)} %get-tuple-element.49), channel_id=1, source_target_pairs={{0,6},{2,4},{4,2},{6,0},{8,14},{10,12},{12,10},{14,8},{16,22},{18,... | collective-permute-start | bytes 98312 | tf_op jit(solution)/shard_map/ppermute | solution.py:317
  19.5 16.0 %collective-permute-start.5 = (bf16[256,2048]{1,0:T(8,128)(2,1)S(1)}, bf16[256,2048]{1,0:T(8,128)(2,1)S(1)}, u32[]{:S(2)}, u32[]{:S(2)}) collective-permute-start(bf16[256,2048]{1,0:T(8,128)(2,1)S(1)} %shard_map.104.refs_2_.refs_5_), channel_id=1, source_target_pairs={{0,1},{1,0},{2,3},{3,2},{4,5},{5,4},{6,7},{7,6},{8,9},{9,8},{10,11... | collective-permute-start | bytes 3145736 | tf_op jit(solution)/shard_map/ppermute | solution.py:321
  19.8 9.7 %collective-permute-start.14 = (bf16[512,128]{1,0:T(8,128)(2,1)S(1)}, bf16[512,128]{1,0:T(8,128)(2,1)S(1)}, u32[]{:S(2)}, u32[]{:S(2)}) collective-permute-start(bf16[512,128]{1,0:T(8,128)(2,1)S(1)} %shard_map.110.refs_0_.refs_1_), channel_id=1, source_target_pairs={{0,16},{2,18},{4,20},{6,22},{8,24},{10,26},{12,28},{14,30},{16,0},... | collective-permute-start | bytes 393224 | tf_op jit(solution)/shard_map/ppermute | solution.py:317
  22.7 9.0 %collective-permute-start.8 = (f16[272,384]{1,0:T(8,128)(2,1)S(1)}, f16[272,384]{1,0:T(8,128)(2,1)S(1)}, u32[]{:S(2)}, u32[]{:S(2)}) collective-permute-start(f16[272,384]{1,0:T(8,128)(2,1)S(1)} %convert_element_type.22), channel_id=1, source_target_pairs={{0,6},{2,4},{4,2},{6,0},{8,14},{10,12},{12,10},{14,8},{16,22},{18,... | collective-permute-start | bytes 626696 | tf_op jit(solution)/shard_map/ppermute | solution.py:317
  25.2 10.1 %collective-permute-start.7 = (f16[272,384]{1,0:T(8,128)(2,1)S(1)}, f16[272,384]{1,0:T(8,128)(2,1)S(1)}, u32[]{:S(2)}, u32[]{:S(2)}) collective-permute-start(f16[272,384]{1,0:T(8,128)(2,1)S(1)} %convert_element_type.20), channel_id=1, source_target_pairs={{0,4},{2,6},{4,0},{6,2},{8,12},{10,14},{12,8},{14,10},{16,20},{18,... | collective-permute-start | bytes 626696 | tf_op jit(solution)/shard_map/ppermute | solution.py:317
  25.8 9.6 %collective-permute-start.6 = (f16[272,384]{1,0:T(8,128)(2,1)S(1)}, f16[272,384]{1,0:T(8,128)(2,1)S(1)}, u32[]{:S(2)}, u32[]{:S(2)}) collective-permute-start(f16[272,384]{1,0:T(8,128)(2,1)S(1)} %convert_element_type.18), channel_id=1, source_target_pairs={{0,2},{2,0},{4,6},{6,4},{8,10},{10,8},{12,14},{14,12},{16,18},{18,... | collective-permute-start | bytes 626696 | tf_op jit(solution)/shard_map/ppermute | solution.py:317
  29.9 12.2 %collective-permute-start.15 = (bf16[1024,128]{1,0:T(8,128)(2,1)S(1)}, bf16[1024,128]{1,0:T(8,128)(2,1)S(1)}, u32[]{:S(2)}, u32[]{:S(2)}) collective-permute-start(bf16[1024,128]{1,0:T(8,128)(2,1)S(1)} %shard_map.111), channel_id=1, source_target_pairs={{0,8},{2,10},{4,12},{6,14},{8,0},{10,2},{12,4},{14,6},{16,24},{18,... | collective-permute-start | bytes 786440 | tf_op jit(solution)/shard_map/ppermute | solution.py:317
  35.6 12.6 %collective-permute-start.12 = (bf16[64,2048]{1,0:T(8,128)(2,1)S(1)}, bf16[64,2048]{1,0:T(8,128)(2,1)S(1)}, u32[]{:S(2)}, u32[]{:S(2)}) collective-permute-start(bf16[64,2048]{1,0:T(8,128)(2,1)S(1)} %get-tuple-element.57), channel_id=1, source_target_pairs={{0,4},{2,6},{4,0},{6,2},{8,12},{10,14},{12,8},{14,10},{16,20},{18,... | collective-permute-start | bytes 786440 | tf_op jit(solution)/shard_map/ppermute | solution.py:317
  37.1 11.1 %collective-permute-start.13 = (bf16[64,2048]{1,0:T(8,128)(2,1)S(1)}, bf16[64,2048]{1,0:T(8,128)(2,1)S(1)}, u32[]{:S(2)}, u32[]{:S(2)}) collective-permute-start(bf16[64,2048]{1,0:T(8,128)(2,1)S(1)} %get-tuple-element.58), channel_id=1, source_target_pairs={{0,2},{2,0},{4,6},{6,4},{8,10},{10,8},{12,14},{14,12},{16,18},{18,... | collective-permute-start | bytes 786440 | tf_op jit(solution)/shard_map/ppermute | solution.py:317
  39.0 9.1 %collective-permute-start.11 = (f32[128,128]{1,0:T(8,128)S(1)}, f32[128,128]{1,0:T(8,128)S(1)}, u32[]{:S(2)}, u32[]{:S(2)}) collective-permute-start(f32[128,128]{1,0:T(8,128)S(1)} %get-tuple-element.53), channel_id=1, source_target_pairs={{0,24},{2,26},{4,28},{6,30},{8,16},{10,18},{12,20},{14,22},{16,8},... | collective-permute-start | bytes 196616 | tf_op jit(solution)/shard_map/ppermute | solution.py:317
  40.4 7.7 %collective-permute-start.10 = (f32[128,128]{1,0:T(8,128)S(1)}, f32[128,128]{1,0:T(8,128)S(1)}, u32[]{:S(2)}, u32[]{:S(2)}) collective-permute-start(f32[128,128]{1,0:T(8,128)S(1)} %get-tuple-element.53), channel_id=1, source_target_pairs={{0,16},{2,18},{4,20},{6,22},{8,24},{10,26},{12,28},{14,30},{16,0},... | collective-permute-start | bytes 196616 | tf_op jit(solution)/shard_map/ppermute | solution.py:317
  54.0 10.9 %collective-permute-start.25 = (f32[128,128]{1,0:T(8,128)S(1)}, f32[128,128]{1,0:T(8,128)S(1)}, u32[]{:S(2)}, u32[]{:S(2)}) collective-permute-start(f32[128,128]{1,0:T(8,128)S(1)} %get-tuple-element.61.refs_5_), channel_id=1, source_target_pairs={{0,24},{2,26},{4,28},{6,30},{8,16},{10,18},{12,20},{14,22},{16,8},... | collective-permute-start | bytes 196616 | tf_op jit(solution)/shard_map/ppermute | solution.py:317
  55.4 12.3 %collective-permute-start.24 = (f32[128,128]{1,0:T(8,128)S(1)}, f32[128,128]{1,0:T(8,128)S(1)}, u32[]{:S(2)}, u32[]{:S(2)}) collective-permute-start(f32[128,128]{1,0:T(8,128)S(1)} %get-tuple-element.61.refs_5_), channel_id=1, source_target_pairs={{0,16},{2,18},{4,20},{6,22},{8,24},{10,26},{12,28},{14,30},{16,0},... | collective-permute-start | bytes 196616 | tf_op jit(solution)/shard_map/ppermute | solution.py:317
  56.2 11.4 %collective-permute-start.23 = (f32[128,128]{1,0:T(8,128)S(1)}, f32[128,128]{1,0:T(8,128)S(1)}, u32[]{:S(2)}, u32[]{:S(2)}) collective-permute-start(f32[128,128]{1,0:T(8,128)S(1)} %get-tuple-element.61.refs_5_), channel_id=1, source_target_pairs={{0,8},{2,10},{4,12},{6,14},{8,0},{10,2},{12,4},{14,6},{16,24},{18,... | collective-permute-start | bytes 196616 | tf_op jit(solution)/shard_map/ppermute | solution.py:317
  60.4 9.4 %collective-permute-start.17 = (bf16[512,128]{1,0:T(8,128)(2,1)S(1)}, bf16[512,128]{1,0:T(8,128)(2,1)S(1)}, u32[]{:S(2)}, u32[]{:S(2)}) collective-permute-start(bf16[512,128]{1,0:T(8,128)(2,1)S(1)} %get-tuple-element.63), channel_id=1, source_target_pairs={{0,8},{2,10},{4,12},{6,14},{8,0},{10,2},{12,4},{14,6},{16,24},{18,... | collective-permute-start | bytes 393224 | tf_op jit(solution)/shard_map/ppermute | solution.py:317
  60.4 11.9 %collective-permute-start.18 = (bf16[512,128]{1,0:T(8,128)(2,1)S(1)}, bf16[512,128]{1,0:T(8,128)(2,1)S(1)}, u32[]{:S(2)}, u32[]{:S(2)}) collective-permute-start(bf16[512,128]{1,0:T(8,128)(2,1)S(1)} %get-tuple-element.64), channel_id=1, source_target_pairs={{0,16},{2,18},{4,20},{6,22},{8,24},{10,26},{12,28},{14,30},{16,0},... | collective-permute-start | bytes 393224 | tf_op jit(solution)/shard_map/ppermute | solution.py:317
  65.0 7.3 %collective-permute-start.19 = (bf16[512,128]{1,0:T(8,128)(2,1)S(1)}, bf16[512,128]{1,0:T(8,128)(2,1)S(1)}, u32[]{:S(2)}, u32[]{:S(2)}) collective-permute-start(bf16[512,128]{1,0:T(8,128)(2,1)S(1)} %get-tuple-element.65), channel_id=1, source_target_pairs={{0,24},{2,26},{4,28},{6,30},{8,16},{10,18},{12,20},{14,22},{16,8},... | collective-permute-start | bytes 393224 | tf_op jit(solution)/shard_map/ppermute | solution.py:317
  68.0 6.7 %collective-permute-start.26 = (bf16[256,256]{1,0:T(8,128)(2,1)S(1)}, bf16[256,256]{1,0:T(8,128)(2,1)S(1)}, u32[]{:S(2)}, u32[]{:S(2)}) collective-permute-start(bf16[256,256]{1,0:T(8,128)(2,1)S(1)} %get-tuple-element.76), channel_id=1, source_target_pairs={{0,2},{2,0},{4,6},{6,4},{8,10},{10,8},{12,14},{14,12},{16,18},{18,... | collective-permute-start | bytes 393224 | tf_op jit(solution)/shard_map/ppermute | solution.py:317
  69.2 7.3 %collective-permute-start.27 = (bf16[256,256]{1,0:T(8,128)(2,1)S(1)}, bf16[256,256]{1,0:T(8,128)(2,1)S(1)}, u32[]{:S(2)}, u32[]{:S(2)}) collective-permute-start(bf16[256,256]{1,0:T(8,128)(2,1)S(1)} %get-tuple-element.77), channel_id=1, source_target_pairs={{0,4},{2,6},{4,0},{6,2},{8,12},{10,14},{12,8},{14,10},{16,20},{18,... | collective-permute-start | bytes 393224 | tf_op jit(solution)/shard_map/ppermute | solution.py:317
  69.8 7.5 %collective-permute-start.28 = (bf16[256,256]{1,0:T(8,128)(2,1)S(1)}, bf16[256,256]{1,0:T(8,128)(2,1)S(1)}, u32[]{:S(2)}, u32[]{:S(2)}) collective-permute-start(bf16[256,256]{1,0:T(8,128)(2,1)S(1)} %get-tuple-element.78), channel_id=1, source_target_pairs={{0,6},{2,4},{4,2},{6,0},{8,14},{10,12},{12,10},{14,8},{16,22},{18,... | collective-permute-start | bytes 393224 | tf_op jit(solution)/shard_map/ppermute | solution.py:317
  (24 other events, 121.8 us)
